TPU v7x, 32 devices: a whole 2x2x4 slice. The times are simulated.
32 devices in a mesh: dp: 8 (over z, y), rep: 4 (over x, core).
Axes of the slice: x: 2, y: 2, z: 4, core: 2. Of those that a mesh axis runs over, the one named last changes fastest.
Arguments:
- q_tokens: bfloat16 [128, 64, 512], P(('dp', 'rep')), may hold values from -6 to 6
- p_tokens: bfloat16 [128, 256, 512], P(('dp', 'rep')), may hold values from -6 to 6
- q_cotangent: bfloat16 [128, 64, 512], P(('dp', 'rep')), may hold values from -0.29882812 to 0.29882812
- p_cotangent: bfloat16 [128, 256, 512], P(('dp', 'rep')), may hold values from -0.29882812 to 0.29882812
- positives: int32 [128, 4], P(('dp', 'rep')), may hold values from 0 to 127, all different within a row
- counts: int32 [128], P(('dp', 'rep')), may hold values from 1 to 4
- w_query: bfloat16 [2, 512, 512], replicated, may hold values from -0.25 to 0.25
- b_query: float32 [2, 512], replicated, may hold values from -1.2 to 1.2
- w_key: bfloat16 [2, 512, 512], replicated, may hold values from -0.25 to 0.25
- w_value: bfloat16 [2, 512, 512], replicated, may hold values from -0.25 to 0.25
- b_value: float32 [2, 512], replicated, may hold values from -1.2 to 1.2
- w_out: bfloat16 [2, 512, 512], replicated, may hold values from -1 to 1
- b_out: float32 [2, 512], replicated, may hold values from -1.2 to 1.2
- gain_one: float32 [2, 512], replicated, may hold values from 0.5 to 1.5
- shift_one: float32 [2, 512], replicated, may hold values from -1.2 to 1.2
- w_up: bfloat16 [2, 512, 2048], replicated, may hold values from -0.25 to 0.25
- b_up: float32 [2, 2048], replicated, may hold values from -1.2 to 1.2
- w_down: bfloat16 [2, 2048, 512], replicated, may hold values from -0.1875 to 0.1875
- b_down: float32 [2, 512], replicated, may hold values from -1.2 to 1.2
- gain_two: float32 [2, 512], replicated, may hold values from 0.5 to 1.5
- shift_two: float32 [2, 512], replicated, may hold values from -1.2 to 1.2
Outputs:
- q_out: bfloat16 [128, 64, 512], P(('dp', 'rep'))
- p_out: bfloat16 [128, 256, 512], P(('dp', 'rep'))
- loss_terms: float32 [128], P(('dp', 'rep'))
- q_grad: float32 [128, 64, 512], P(('dp', 'rep'))
- p_grad: float32 [128, 256, 512], P(('dp', 'rep'))
- grad_w_query: float32 [2, 512, 512], replicated
- grad_b_query: float32 [2, 512], replicated
- grad_w_key: float32 [2, 512, 512], replicated
- grad_w_value: float32 [2, 512, 512], replicated
- grad_b_value: float32 [2, 512], replicated
- grad_w_out: float32 [2, 512, 512], replicated
- grad_b_out: float32 [2, 512], replicated
- grad_gain_one: float32 [2, 512], replicated
- grad_shift_one: float32 [2, 512], replicated
- grad_w_up: float32 [2, 512, 2048], replicated
- grad_b_up: float32 [2, 2048], replicated
- grad_w_down: float32 [2, 2048, 512], replicated
- grad_b_down: float32 [2, 512], replicated
- grad_gain_two: float32 [2, 512], replicated
- grad_shift_two: float32 [2, 512], replicated
Inputs may be any that keep to these rules, and one draw needn't show every extreme that they name: `positives`: the used slots of a question name different passages.
All inputs are finite; a program needn't handle non-finite values.
Results may differ from a plain program's by a relative error of at most 0.014.
Values may be sent and summed in bfloat16 or wider, within the bound.
No kernel may reach another device: no remote copies, remote signals or barrier semaphores. Data moves between devices by JAX's collectives and lax.ppermute only.
A program may use at most 192 MiB of HBM per device.

v0:
```python
import math

import jax
import jax.numpy as jnp
from jax import lax
from jax.sharding import PartitionSpec as P

NH = 8


EPS = 1e-06
HIGH = lax.Precision.HIGHEST
F32 = jnp.float32
B16 = jnp.bfloat16


def layer_norm(v, gain, shift):
    centre = v - jnp.mean(v, -1, keepdims=True)
    spread = jnp.mean(centre * centre, -1, keepdims=True)
    return centre * lax.rsqrt(spread + EPS) * gain + shift


def exact_gelu(v):
    return jax.nn.gelu(v, approximate=False)


def encoder_forward(tokens, weights):
    (
        w_query,
        b_query,
        w_key,
        w_value,
        b_value,
        w_out,
        b_out,
        gain_one,
        shift_one,
        w_up,
        b_up,
        w_down,
        b_down,
        gain_two,
        shift_two,
    ) = weights
    count, length, width = tokens.shape
    heads = NH
    hsize = width // heads
    rows = tokens.reshape(count * length, width)
    query = (jnp.dot(rows, w_query, preferred_element_type=F32) + b_query).astype(B16)
    key = jnp.dot(rows, w_key, preferred_element_type=F32).astype(B16)
    value = (jnp.dot(rows, w_value, preferred_element_type=F32) + b_value).astype(B16)
    q_heads = query.reshape(count, length, heads, hsize)
    k_heads = key.reshape(count, length, heads, hsize)
    v_heads = value.reshape(count, length, heads, hsize)
    scores = jnp.einsum("blhd,bmhd->bhlm", q_heads, k_heads, preferred_element_type=F32) * (
        1.0 / math.sqrt(hsize)
    )
    top = jnp.max(scores, -1, keepdims=True)
    expo = jnp.exp(scores - top)
    probs = expo / jnp.sum(expo, -1, keepdims=True)
    probs_low = probs.astype(B16)
    attended = jnp.einsum("bhlm,bmhd->blhd", probs_low, v_heads, preferred_element_type=F32).astype(
        B16
    )
    attended = attended.reshape(count * length, width)
    first = rows.astype(F32) + jnp.dot(attended, w_out, preferred_element_type=F32) + b_out
    normed = layer_norm(first, gain_one, shift_one)
    normed_low = normed.astype(B16)
    inner = jnp.dot(normed_low, w_up, preferred_element_type=F32) + b_up
    activated = exact_gelu(inner).astype(B16)
    second = normed + jnp.dot(activated, w_down, preferred_element_type=F32) + b_down
    output = layer_norm(second, gain_two, shift_two)
    kept = (
        rows,
        q_heads,
        k_heads,
        v_heads,
        probs,
        probs_low,
        attended,
        first,
        normed_low,
        inner,
        activated,
        second,
    )
    return (output, kept)


def encoder_backward(weights, kept, d_output):
    (
        w_query,
        b_query,
        w_key,
        w_value,
        b_value,
        w_out,
        b_out,
        gain_one,
        shift_one,
        w_up,
        b_up,
        w_down,
        b_down,
        gain_two,
        shift_two,
    ) = weights
    (
        rows,
        q_heads,
        k_heads,
        v_heads,
        probs,
        probs_low,
        attended,
        first,
        normed_low,
        inner,
        activated,
        second,
    ) = kept
    count, length, heads, hsize = q_heads.shape
    width = heads * hsize
    scale = 1.0 / math.sqrt(hsize)
    _, norm_two_back = jax.vjp(layer_norm, second, gain_two, shift_two)
    d_second, g_gain_two, g_shift_two = norm_two_back(d_output)
    d_down = d_second.astype(B16)
    g_w_down = jnp.einsum("rf,ro->fo", activated, d_down, preferred_element_type=F32)
    g_b_down = jnp.sum(d_down.astype(F32), 0)
    d_activated = jnp.einsum("ro,fo->rf", d_down, w_down, preferred_element_type=F32)
    _, gelu_back = jax.vjp(exact_gelu, inner)
    d_inner = gelu_back(d_activated)[0].astype(B16)
    g_w_up = jnp.einsum("ri,rf->if", normed_low, d_inner, preferred_element_type=F32)
    g_b_up = jnp.sum(d_inner.astype(F32), 0)
    d_normed = d_second + jnp.einsum("rf,if->ri", d_inner, w_up, preferred_element_type=F32)
    _, norm_one_back = jax.vjp(layer_norm, first, gain_one, shift_one)
    d_first, g_gain_one, g_shift_one = norm_one_back(d_normed)
    d_branch = d_first.astype(B16)
    g_w_out = jnp.einsum("ri,ro->io", attended, d_branch, preferred_element_type=F32)
    g_b_out = jnp.sum(d_branch.astype(F32), 0)
    d_attended = jnp.einsum("ro,io->ri", d_branch, w_out, preferred_element_type=F32).astype(B16)
    d_attended = d_attended.reshape(count, length, heads, hsize)
    d_probs = jnp.einsum("blhd,bmhd->bhlm", d_attended, v_heads, preferred_element_type=F32)
    d_value = jnp.einsum(
        "bhlm,blhd->bmhd", probs_low, d_attended, preferred_element_type=F32
    ).astype(B16)
    d_scores = (probs * (d_probs - jnp.sum(probs * d_probs, -1, keepdims=True))).astype(B16)
    d_query = (
        jnp.einsum("bhlm,bmhd->blhd", d_scores, k_heads, preferred_element_type=F32) * scale
    ).astype(B16)
    d_key = (
        jnp.einsum("bhlm,blhd->bmhd", d_scores, q_heads, preferred_element_type=F32) * scale
    ).astype(B16)
    d_query = d_query.reshape(count * length, width)
    d_key = d_key.reshape(count * length, width)
    d_value = d_value.reshape(count * length, width)
    g_w_query = jnp.einsum("ri,ro->io", rows, d_query, preferred_element_type=F32)
    g_b_query = jnp.sum(d_query.astype(F32), 0)
    g_w_key = jnp.einsum("ri,ro->io", rows, d_key, preferred_element_type=F32)
    g_w_value = jnp.einsum("ri,ro->io", rows, d_value, preferred_element_type=F32)
    g_b_value = jnp.sum(d_value.astype(F32), 0)
    d_rows = d_first + jnp.einsum("ro,io->ri", d_query, w_query, preferred_element_type=F32)
    d_rows = d_rows + jnp.einsum("ro,io->ri", d_key, w_key, preferred_element_type=F32)
    d_rows = d_rows + jnp.einsum("ro,io->ri", d_value, w_value, preferred_element_type=F32)
    grads = (
        g_w_query,
        g_b_query,
        g_w_key,
        g_w_value,
        g_b_value,
        g_w_out,
        g_b_out,
        g_gain_one,
        g_shift_one,
        g_w_up,
        g_b_up,
        g_w_down,
        g_b_down,
        g_gain_two,
        g_shift_two,
    )
    return (d_rows.reshape(count, length, width), grads)


def build_mask(positives, counts, passages):
    live = jnp.arange(positives.shape[1])[None, :] < counts[:, None]
    hits = (positives[:, :, None] == jnp.arange(passages)[None, None, :]) & live[:, :, None]
    return jnp.sum(hits.astype(F32), 1)


def contrast(sim, mask):
    top = jnp.max(sim, -1, keepdims=True)
    expo = jnp.exp(sim - top)
    total = jnp.sum(expo, -1)
    pos_total = jnp.sum(mask * expo, -1)
    loss_terms = jnp.log(total) - jnp.log(pos_total)
    coeff = expo / total[:, None] - mask * expo / pos_total[:, None]
    return (loss_terms, coeff)


def shards(
    q_tokens,
    p_tokens,
    q_cotangent,
    p_cotangent,
    positives,
    counts,
    w_query,
    b_query,
    w_key,
    w_value,
    b_value,
    w_out,
    b_out,
    gain_one,
    shift_one,
    w_up,
    b_up,
    w_down,
    b_down,
    gain_two,
    shift_two,
):
    stacked = (
        w_query,
        b_query,
        w_key,
        w_value,
        b_value,
        w_out,
        b_out,
        gain_one,
        shift_one,
        w_up,
        b_up,
        w_down,
        b_down,
        gain_two,
        shift_two,
    )
    q_weights = tuple((w[0] for w in stacked))
    p_weights = tuple((w[1] for w in stacked))
    q_count, q_length, width = q_tokens.shape
    p_count, p_length, _ = p_tokens.shape
    q_output, q_kept = encoder_forward(q_tokens, q_weights)
    p_output, p_kept = encoder_forward(p_tokens, p_weights)
    q_output = q_output.reshape(q_count, q_length, width)
    p_output = p_output.reshape(p_count, p_length, width)
    cls_q = q_output[:, 0].astype(B16)
    cls_p = p_output[:, 0].astype(B16)
    scale = 2.0 / math.sqrt(width)
    every_cls = lax.all_gather(cls_p, ("dp", "rep"), axis=0, tiled=True)
    passages = every_cls.shape[0]
    sim = jnp.einsum("qi,pi->qp", cls_q, every_cls, preferred_element_type=F32) * scale
    mask = build_mask(positives, counts, passages)
    loss_terms, coeff = contrast(sim, mask)
    d_cls_q = jnp.dot(coeff, every_cls.astype(F32), precision=HIGH) * scale
    partial_p = jnp.einsum("qp,qi->pi", coeff, cls_q.astype(F32), precision=HIGH) * scale
    d_cls_p = lax.psum_scatter(partial_p, ("dp", "rep"), scatter_dimension=0, tiled=True)
    q_dout = q_cotangent.astype(F32).at[:, 0].add(d_cls_q).reshape(q_count * q_length, width)
    p_dout = p_cotangent.astype(F32).at[:, 0].add(d_cls_p).reshape(p_count * p_length, width)
    q_grad, q_terms = encoder_backward(q_weights, q_kept, q_dout)
    p_grad, p_terms = encoder_backward(p_weights, p_kept, p_dout)
    joined = [jnp.stack([q_terms[i], p_terms[i]]) for i in range(15)]
    summed = lax.psum(
        (
            joined[0],
            joined[1],
            joined[2],
            joined[3],
            joined[4],
            joined[5],
            joined[6],
            joined[7],
            joined[8],
            joined[9],
            joined[10],
            joined[11],
            joined[12],
            joined[13],
            joined[14],
        ),
        ("dp", "rep"),
    )
    return (
        q_output.astype(B16),
        p_output.astype(B16),
        loss_terms,
        q_grad,
        p_grad,
        summed[0],
        summed[1],
        summed[2],
        summed[3],
        summed[4],
        summed[5],
        summed[6],
        summed[7],
        summed[8],
        summed[9],
        summed[10],
        summed[11],
        summed[12],
        summed[13],
        summed[14],
    )


def solution(mesh):
    placed = (
        P(("dp", "rep"), None, None),
        P(("dp", "rep"), None, None),
        P(("dp", "rep"), None, None),
        P(("dp", "rep"), None, None),
        P(("dp", "rep"), None),
        P(("dp", "rep")),
        P(),
        P(),
        P(),
        P(),
        P(),
        P(),
        P(),
        P(),
        P(),
        P(),
        P(),
        P(),
        P(),
        P(),
        P(),
    )
    return jax.shard_map(
        shards,
        mesh=mesh,
        in_specs=placed,
        out_specs=(
            P(("dp", "rep"), None, None),
            P(("dp", "rep"), None, None),
            P(("dp", "rep")),
            P(("dp", "rep"), None, None),
            P(("dp", "rep"), None, None),
            P(),
            P(),
            P(),
            P(),
            P(),
            P(),
            P(),
            P(),
            P(),
            P(),
            P(),
            P(),
            P(),
            P(),
            P(),
        ),
        check_vma=False,
    )
```

profile of v0, /device:TPU:0, one launch (start us, length us, event | category | flops | bytes accessed | tf_op | source)
XLA Modules:
  0.0 763.0 jit_solution(15628112435374657471)
XLA Ops:
  19.2 8.1 %multiply_convert_fusion.4 = (bf16[256,2048]{1,0:T(8,128)(2,1)S(1)}, f32[256,2048]{1,0:T(8,128)}, f32[256,2048]{1,0:T(8,128)}) fusion(f32[2048]{0:T(1024)S(1)} %bitcast.379, bf16[2,512,2048]{2,1,0:T(8,128)(2,1)} %param.40, f32[256,512]{1,0:T(8,128)S(1)} %get-tuple-element.192, f32[512]{0:T(512)S(1)} %bitcast.350, f32[512]{0:T(512)S(1)} %bitcast.345, ...), kind=kOutput, calls=%fused_computation.83 | convolution fusion | flops 572129280 | bytes 7878656 | tf_op jit(solution)/shard_map/dot_general | solution.py:69
  32.3 2.8 reshape.388
  35.1 1.9 copy.169
  37.0 3.0 add_convert_fusion.3
  40.1 2.8 reshape.389
  42.9 2.0 copy.167
  44.8 2.8 reshape.390
  47.6 2.3 copy.168
  50.0 7.9 %fusion.192 = (f32[4,8,256]{2,1,0:T(8,128)S(1)}, f32[4,8,256,256]{2,3,1,0:T(8,128)}) fusion(bf16[4,256,8,64]{1,3,2,0:T(8,128)(2,1)} %copy.167, bf16[4,256,8,64]{1,3,2,0:T(8,128)(2,1)} %copy.168), kind=kOutput, calls=%fused_computation.295 | convolution fusion | flops 274727168 | bytes 10518528 | tf_op jit(solution)/shard_map/sub | solution.py:59
  57.9 4.2 fusion.63
  66.6 22.3 %multiply_convert_fusion.1 = (bf16[1024,2048]{1,0:T(8,128)(2,1)S(1)}, f32[1024,2048]{1,0:T(8,128)}, f32[1024,2048]{1,0:T(8,128)}) fusion(f32[2048]{0:T(1024)S(1)} %bitcast.375, bf16[2,512,2048]{2,1,0:T(8,128)(2,1)S(1)} %copy-done.81, f32[1024,512]{1,0:T(8,128)S(1)} %get-tuple-element.199, f32[512]{0:T(512)S(1)} %bitcast.364, f32[512]{0:T(512)S(1)} %bitcast.353, ...), kind=kOutput, calls=%fused_computation.10 | convolution fusion | flops 2288517120 | bytes 25186304 | tf_op jit(solution)/shard_map/dot_general | solution.py:69
  88.9 2.6 fusion.194
  93.4 43.9 %all-gather = bf16[128,1,512]{2,1,0:T(2,128)(2,1)S(1)} all-gather(bf16[4,1,512]{2,1,0:T(2,128)(2,1)S(1)} %slice.177), channel_id=2, replica_groups=mesh['dp'=8,'rep'=4] {'dp','rep'}, dimensions={0}, use_global_device_ids=true | all-gather | bytes 135168 | tf_op jit(solution)/shard_map/all_gather | solution.py:252
  145.9 3.7 convert_reduce_fusion.2
  153.4 2.1 reshape.365
  155.4 2.1 multiply_reduce_fusion.7
  160.9 2.9 convert_reduce_fusion.6
  163.8 2.4 convolution_bitcast_fusion.4
  166.2 2.8 convolution_bitcast_fusion.3
  169.0 2.7 convolution_bitcast_fusion.1
  174.2 2.3 copy.182
  177.9 2.3 copy.184
  180.2 2.1 reshape.368
  182.2 3.4 copy_convert_fusion
  188.2 2.2 convolution_bitcast_fusion.5
  190.5 71.0 %all-reduce.6.cloned.1.call-done = f32[128,512]{1,0:T(8,128)} async-done(((f32[128,512]{1,0:T(8,128)}), f32[128,512]{1,0:T(8,128)}) %all-reduce.6.cloned.1.call-update) | async-done | bytes 262160
  262.8 2.3 copy.186
  268.6 8.7 %convert_reduce_fusion = (f32[2048]{0:T(1024)S(1)}, bf16[1024,2048]{1,0:T(8,128)(2,1)S(1)}) fusion(f32[1024,2048]{1,0:T(8,128)} %get-tuple-element.168, bf16[1024,512]{1,0:T(8,128)(2,1)S(1)} %get-tuple-element.154, bf16[2,2048,512]{2,1,0:T(8,128)(2,1)S(1)} %copy-done.80, f32[1024,2048]{1,0:T(8,128)} %get-tuple-element.200, f32[2048]{0:T(1024)S(1)} %bitcast.376), kind=kOutput, calls=%fused_computation.6 | convolution fusion | flops 2183133184 | bytes 24133632 | tf_op jit(solution)/shard_map/ro,fo->rf/dot_general | solution.py:130
  277.4 3.0 multiply_reduce_fusion.2
  285.5 3.9 reshape.391
  289.4 3.0 copy.188
  292.4 5.6 multiply_reduce_fusion
  298.0 4.9 multiply_convert_fusion
  308.3 2.6 convolution_bitcast_fusion.2
  311.0 2.5 convolution_bitcast_fusion
  326.5 4.2 pad_maximum_fusion
  330.7 4.4 pad_maximum_fusion.1
  335.1 2.5 pad_maximum_fusion.2
  343.0 42.6 %all-reduce.1 = (f32[2,512]{1,0:T(2,128)}, f32[2,512]{1,0:T(2,128)}, f32[2,512]{1,0:T(2,128)}, f32[2,512]{1,0:T(2,128)}, f32[2,512]{1,0:T(2,128)}, /*index=5*/f3...) all-reduce(f32[2,512]{1,0:T(2,128)S(1)} %get-tuple-element.225, ...), channel_id=1, replica_groups=mesh['dp'=8,'rep'=4] {'dp','rep'}, use_global_device_ids=true, to_apply=%region_30.0 | all-reduce | flops 12288 | bytes 98304 | tf_op jit(solution)/shard_map/psum | solution.py:265
  385.6 2.3 fusion.94
  387.9 2.3 fusion.97
  390.3 2.4 add_add_fusion.2
  392.8 342.1 %all-reduce.8.cloned.1.call-done = (f32[2,512,512]{1,2,0:T(8,128)}, f32[2,512,512]{1,2,0:T(8,128)}, f32[2,512,512]{1,2,0:T(8,128)}, f32[2,512,512]{2,1,0:T(8,128...) async-done(((f32[2,512,512]{1,2,0:T(8,128)}, f32[2,512,512]{1,2,0:T(8,128)}, f32[2,512,512]{1,2,0:T(8,128)}, f32[2,512,512]{2,1,0:T(8,128)}, f32[2,512,2048]{2,1,0:T(8,128)}, ...) | async-done | bytes 25165840 | tf_op jit(solution)/shard_map/psum | solution.py:265
  734.8 3.0 copy.199
  737.8 1.8 copy.200
  739.6 3.0 copy.201
  744.0 8.6 %copy.292 = f32[2,512,2048]{2,1,0:T(8,128)} copy(f32[2,512,2048]{2,1,0:T(8,128)} %get-tuple-element.247) | data formatting | bytes 16777216
  752.6 3.4 copy.293
  (306 shorter events, 80.1 us)
Async XLA Ops:
  7.2 5.8 copy-start.19
  7.2 5.8 copy-start.36
  7.2 254.2 %all-reduce.6.cloned.1.call-start = ((), (), s32[]{:S(2)}) async-start(), calls=%async_computation | async-start | bytes 524288
  12.1 3.9 copy-start.60
  17.4 9.9 %copy-start.29 = (bf16[256,512]{1,0:T(8,128)(2,1)}, bf16[256,512]{1,0:T(8,128)(2,1)S(1)}, u32[]{:S(2)}) copy-start(bf16[256,512]{1,0:T(8,128)(2,1)S(1)} %reshape.355) | copy-start | bytes 786436
  19.2 8.1 %copy-start.77 = (bf16[2,2048,512]{2,1,0:T(8,128)(2,1)S(1)}, bf16[2,2048,512]{2,1,0:T(8,128)(2,1)}, u32[]{:S(2)}) copy-start(bf16[2,2048,512]{2,1,0:T(8,128)(2,1)} %param.42) | copy-start | bytes 12582916
  49.9 7.9 %copy-start.41 = (bf16[4,256,8,64]{1,3,2,0:T(8,128)(2,1)S(1)}, bf16[4,256,8,64]{1,3,2,0:T(8,128)(2,1)}, u32[]{:S(2)}) copy-start(bf16[4,256,8,64]{1,3,2,0:T(8,128)(2,1)} %copy.169) | copy-start | bytes 3145732
  63.6 2.9 copy-start.81
  64.5 24.4 %copy-start = (f32[1024,512]{1,0:T(8,128)}, f32[1024,512]{1,0:T(8,128)S(1)}, u32[]{:S(2)}) copy-start(f32[1024,512]{1,0:T(8,128)S(1)} %get-tuple-element.199) | copy-start | bytes 6291460
  66.6 22.3 %copy-start.78 = (bf16[2,2048,512]{2,1,0:T(8,128)(2,1)S(1)}, bf16[2,2048,512]{2,1,0:T(8,128)(2,1)}, u32[]{:S(2)}) copy-start(bf16[2,2048,512]{2,1,0:T(8,128)(2,1)} %param.42) | copy-start | bytes 12582916
  88.9 2.6 copy-start.88
  92.0 45.5 %copy-start.87 = (s32[4]{0:T(128)S(1)}, s32[4]{0:T(128)}, u32[]{:S(2)}) copy-start(s32[4]{0:T(128)} %param.30) | copy-start | bytes 52
  92.0 46.3 %copy-start.74 = (s32[4,4]{1,0:T(4,128)S(1)}, s32[4,4]{1,0:T(4,128)}, u32[]{:S(2)}) copy-start(s32[4,4]{1,0:T(4,128)} %param.29) | copy-start | bytes 196
  138.6 5.7 copy-start.70
  140.2 594.6 %all-reduce.8.cloned.1.call-start = ((), (), s32[]{:S(2)}) async-start(), calls=%async_computation.1 | async-start | bytes 50331648 | tf_op jit(solution)/shard_map/psum | solution.py:265
  144.5 5.1 copy-start.45
  145.9 3.7 copy-start.82
  166.2 2.8 copy-start.23
  166.2 2.8 copy-start.46
  169.0 2.7 copy-start.61
  174.2 11.4 %copy-start.24 = (bf16[256,512]{1,0:T(8,128)(2,1)}, bf16[256,512]{1,0:T(8,128)(2,1)S(1)}, u32[]{:S(2)}) copy-start(bf16[256,512]{1,0:T(8,128)(2,1)S(1)} %reshape.366) | copy-start | bytes 786436
  177.9 9.1 %copy-start.26 = (bf16[256,512]{1,0:T(8,128)(2,1)}, bf16[256,512]{1,0:T(8,128)(2,1)S(1)}, u32[]{:S(2)}) copy-start(bf16[256,512]{1,0:T(8,128)(2,1)S(1)} %reshape.367) | copy-start | bytes 786436
  267.2 10.1 %copy-start.49 = (bf16[1024,512]{1,0:T(8,128)(2,1)}, bf16[1024,512]{1,0:T(8,128)(2,1)S(1)}, u32[]{:S(2)}) copy-start(bf16[1024,512]{1,0:T(8,128)(2,1)S(1)} %get-tuple-element.154) | copy-start | bytes 3145732
  268.6 8.8 %copy-start.1 = (f32[1024,512]{1,0:T(8,128)S(1)}, f32[1024,512]{1,0:T(8,128)}, u32[]{:S(2)}) copy-start(f32[1024,512]{1,0:T(8,128)} %copy-done) | copy-start | bytes 6291460
  268.6 8.8 %copy-start.83 = (bf16[2,512,2048]{2,1,0:T(8,128)(2,1)S(1)}, bf16[2,512,2048]{2,1,0:T(8,128)(2,1)}, u32[]{:S(2)}) copy-start(bf16[2,512,2048]{2,1,0:T(8,128)(2,1)} %param.40) | copy-start | bytes 12582916
  277.3 3.0 copy-start.7
  281.2 2.5 copy-start.65
  292.4 12.9 %slice-start = ((s8[8388608]{0:T(1024)(128)(4,1)}), s8[4194304]{0:T(1024)(128)(4,1)S(1)}, s32[]{:S(2)}) async-start(s8[8388608]{0:T(1024)(128)(4,1)} %bitcast.316), calls=%async_computation.2 | async-start | bytes 8388608
  298.0 4.9 copy-start.15
  298.0 7.3 slice-start.1
  305.5 2.8 copy-start.8
  308.3 2.6 copy-start.50
  308.3 2.6 copy-start.89
  314.5 4.4 copy-start.11
  316.6 3.9 copy-start.13
  323.5 2.9 copy-start.5
  326.5 4.2 copy-start.6
  330.6 4.4 copy-start.20
  330.6 4.4 copy-start.21
  330.6 4.4 copy-start.55
  330.6 4.4 copy-start.56
  338.6 2.6 copy-start.28
  339.7 2.7 copy-start.2
  385.6 4.6 copy-start.40
  734.8 3.0 copy-start.33
  739.6 3.0 copy-start.32
  742.7 9.9 %slice-start.2 = ((s8[8388608]{0:T(1024)(128)(4,1)}), s8[4194304]{0:T(1024)(128)(4,1)S(1)}, s32[]{:S(2)}) async-start(s8[8388608]{0:T(1024)(128)(4,1)} %bitcast.318), calls=%async_computation.4 | async-start | bytes 8388608
  744.0 8.6 %slice-start.3 = ((s8[8388608]{0:T(1024)(128)(4,1)}), s8[4194304]{0:T(1024)(128)(4,1)S(1)}, s32[]{:S(2)}) async-start(s8[8388608]{0:T(1024)(128)(4,1)} %bitcast.318), calls=%async_computation.5 | async-start | bytes 8388608
  (48 other events, 75.0 us)
Sparse Core Ops, SparseCore 0:
  140.3 121.0 all-reduce.5
  337.8 396.9 all-reduce.7
where the time goes:
time: 773 us; the launch traced here: 763 us
  waiting for transfers between devices  413 us (53%)
  matrix products  130 us (17%)
  blocking collectives  86.5 us (11%)
  local copies, waits for them, and re-layouts  84.5 us (11%)
  other arithmetic  32.8 us (4%)
  between operations  15.5 us (2%)
    psum x1, waiting for transfers between devices, shards(): lax.psum((joined[0], joined[1], joined[2], joined[3], joined[4], joined[5...  342 us
    unnamed x3, waiting for transfers between devices  71 us
    all_gather x1, blocking collectives, shards(): every_cls = lax.all_gather(cls_p, ('dp', 'rep'), axis=0, tiled=True)  43.9 us
    psum x1, blocking collectives, shards(): lax.psum((joined[0], joined[1], joined[2], joined[3], joined[4], joined[5...  42.6 us
    unnamed x198, local copies, waits for them, and re-layouts  38.6 us
    dot_general x2, matrix products, encoder_forward(): inner = jnp.dot(normed_low, w_up, preferred_element_type=F32) + b_up  30.4 us
  transfers between devices with their start and end apart: 2, of which 2 were waited for; matrix products, arithmetic and copies ran while one was open for 8% of the time, Pallas kernels for 0%

commit v1 on v0

v1 whole, which is shorter than its diff:
```python
import functools

import jax
import jax.numpy as jnp
import numpy as np
from jax import lax
from jax.experimental import pallas as pl
from jax.experimental.pallas import tpu as pltpu
from jax.sharding import PartitionSpec as P

HEADS = 8
HS = 64
EPS = 1e-06
F32 = jnp.float32
B16 = jnp.bfloat16
I32 = jnp.int32
HIGH = lax.Precision.HIGHEST
AXES = ("dp", "rep")
SCALE = 0.125
MIB = 1 << 20
ANY = pl.BlockSpec(memory_space=pl.ANY)
SMEM = pl.BlockSpec(memory_space=pltpu.SMEM)
VMEM = pl.BlockSpec(memory_space=pltpu.VMEM)
SMALL = ("b_query", "b_value", "b_out", "gain_one", "shift_one", "b_down", "gain_two", "shift_two")
NSMALL = 12


def dot(a, b):
    return lax.dot_general(a, b, (((1,), (0,)), ((), ())), preferred_element_type=F32)


def dot_nt(a, b):
    return lax.dot_general(a, b, (((1,), (1,)), ((), ())), preferred_element_type=F32)


def dot_tn(a, b):
    return lax.dot_general(a, b, (((0,), (0,)), ((), ())), preferred_element_type=F32)


def dot_high(a, b):
    return lax.dot_general(
        a, b, (((1,), (0,)), ((), ())), precision=HIGH, preferred_element_type=F32
    )


def centred(v):
    c = v - jnp.mean(v, -1, keepdims=True)
    r = lax.rsqrt(jnp.mean(c * c, -1, keepdims=True) + EPS)
    return c * r, r


def norm_back(v, gain, d_out):
    hat, r = centred(v)
    g_gain = jnp.sum(d_out * hat, 0, keepdims=True)
    g_shift = jnp.sum(d_out, 0, keepdims=True)
    d_hat = d_out * gain
    mean_a = jnp.mean(d_hat, -1, keepdims=True)
    mean_b = jnp.mean(d_hat * hat, -1, keepdims=True)
    return r * (d_hat - mean_a - hat * mean_b), g_gain, g_shift, hat


def gelu_pair(x):
    e = jnp.exp(-0.5 * (x * x))
    t = 1.0 / (1.0 + 0.23164188825 * jnp.abs(x))
    poly = t * (
        0.127414796
        + t * (-0.142248368 + t * (0.7107068705 + t * (-0.7265760135 + t * 0.5307027145)))
    )
    tail = poly * e
    phi = jnp.where(x < 0, tail, 1.0 - tail)
    return x * phi, phi + x * (e * 0.3989422804014327)


def stacked(x, group):
    lane = lax.broadcasted_iota(I32, x.shape, 1) // HS
    zero = jnp.zeros_like(x)
    return jnp.concatenate([jnp.where(lane == g, x, zero) for g in range(group)], 0)


def diagonal(o, group):
    rows = o.shape[0] // group
    lane = lax.broadcasted_iota(I32, (rows, o.shape[1]), 1) // HS
    out = o[:rows]
    for g in range(1, group):
        out = jnp.where(lane == g, o[g * rows : (g + 1) * rows], out)
    return out


def softmax(s):
    e = jnp.exp(s - jnp.max(s, -1, keepdims=True))
    return e * (1.0 / jnp.sum(e, -1, keepdims=True))


def attend(q, k, v, group, keep_probs):
    wide = HS * group
    parts = []
    for t in range(HEADS // group):
        at = slice(t * wide, (t + 1) * wide)
        probs = softmax(dot_nt(stacked(q[:, at], group), k[:, at])).astype(B16)
        keep_probs(t, probs)
        parts.append(diagonal(dot(probs, v[:, at]), group))
    return jnp.concatenate(parts, 1).astype(B16)


def attend_back(q, k, v, d_att, group, probs_of):
    wide = HS * group
    dq, dk, dv = [], [], []
    for t in range(HEADS // group):
        at = slice(t * wide, (t + 1) * wide)
        probs = probs_of(t)
        d_stack = stacked(d_att[:, at], group)
        d_probs = dot_nt(d_stack, v[:, at])
        dv.append(dot_tn(probs, d_stack))
        p32 = probs.astype(F32)
        inside = jnp.sum(p32 * d_probs, -1, keepdims=True)
        d_scores = (p32 * (d_probs - inside)).astype(B16)
        dq.append(diagonal(dot(d_scores, k[:, at]), group) * SCALE)
        dk.append(dot_tn(d_scores, stacked(q[:, at], group)))
    return tuple(jnp.concatenate(x, 1).astype(B16) for x in (dq, dk, dv))


def feed(first, w_up, b_up, w_down, b_down, gain, shift, keep):
    hat, _ = centred(first)
    normed = hat * gain + shift
    low = normed.astype(B16)
    second = normed + b_down
    for j in range(w_up.shape[1] // 512):
        at = slice(j * 512, (j + 1) * 512)
        act, slope = gelu_pair(dot(low, w_up[:, at]) + b_up[:, at])
        act = act.astype(B16)
        keep(at, act, slope)
        second = second + dot(act, w_down[at, :])
    return second


def row(ref, e):
    return ref[e : e + 1, :]


def front_kernel(
    positives,
    counts,
    p_x,
    q_x,
    bq,
    bv,
    bo,
    g1,
    s1,
    bu,
    bd,
    g2,
    s2,
    wq,
    wk,
    wv,
    wo,
    wu,
    wd,
    pq,
    pk,
    pv,
    qq,
    qk,
    qv,
    q_probs,
    q_att,
    q_first,
    q_second,
    q_act,
    q_slope,
    q_out,
    payload,
    wqkv_s,
    wo_s,
    wu_s,
    wd_s,
    cls_att,
    cls_x,
    pay_s,
    sems,
):
    b = pl.program_id(0)
    nb = pl.num_programs(0)
    ql = q_x.shape[0] // nb
    copies = [
        pltpu.make_async_copy(src, dst, sems.at[i])
        for i, (src, dst) in enumerate(
            (
                (wq, wqkv_s.at[0]),
                (wk, wqkv_s.at[1]),
                (wv, wqkv_s.at[2]),
                (wo, wo_s),
                (wu, wu_s),
                (wd, wd_s),
            )
        )
    ]

    @pl.when(b == 0)
    def _():
        for c in copies:
            c.start()
        cls_att[...] = jnp.zeros_like(cls_att)
        cls_x[...] = jnp.zeros_like(cls_x)
        for c in copies[:3]:
            c.wait()
        x = q_x[...]
        qq[...] = (dot(x, wqkv_s[0, 0]) + row(bq, 0)).astype(B16) * SCALE
        qk[...] = dot(x, wqkv_s[1, 0]).astype(B16)
        qv[...] = (dot(x, wqkv_s[2, 0]) + row(bv, 0)).astype(B16)

    x = p_x[...]
    q = (dot(x, wqkv_s[0, 1]) + row(bq, 1)).astype(B16) * SCALE
    k = dot(x, wqkv_s[1, 1]).astype(B16)
    v = (dot(x, wqkv_s[2, 1]) + row(bv, 1)).astype(B16)
    pq[...], pk[...], pv[...] = q, k, v
    width = x.shape[1]
    own = (
        lax.broadcasted_iota(I32, (HEADS, width), 1) // HS
        == lax.broadcasted_iota(I32, (HEADS, width), 0)
    )
    q_rows = jnp.where(own, jnp.broadcast_to(q[0:1].astype(F32), (HEADS, width)), 0.0).astype(B16)
    probs = softmax(dot_nt(q_rows, k)).astype(B16)
    mixed = jnp.sum(jnp.where(own, dot(probs, v), 0.0), 0, keepdims=True)
    cls_att[pl.ds(b, 1), :] = mixed
    cls_x[pl.ds(b, 1), :] = x[0:1].astype(F32)

    at = pl.ds(pl.multiple_of(b * ql, ql), ql)

    def keep_probs(t, value):
        q_probs[b, t] = value

    q_att[at, :] = attend(qq[at, :], qk[at, :], qv[at, :], 4, keep_probs)

    @pl.when(b == nb - 1)
    def _():
        for c in copies[3:]:
            c.wait()
        first = cls_x[...] + dot(cls_att[...].astype(B16), wo_s[1]) + row(bo, 1)
        second = feed(
            first, wu_s.at[1], row(bu, 1), wd_s.at[1], row(bd, 1), row(g1, 1), row(s1, 1),
            lambda at, act, slope: None,
        )
        cls_p = centred(second)[0] * row(g2, 1) + row(s2, 1)
        first = q_x[...].astype(F32) + dot(q_att[...], wo_s[0]) + row(bo, 0)
        q_first[...] = first

        def keep(at, act, slope):
            q_act[:, at] = act
            q_slope[:, at] = slope.astype(B16)

        second = feed(
            first, wu_s.at[0], row(bu, 0), wd_s.at[0], row(bd, 0), row(g1, 0), row(s1, 0), keep
        )
        q_second[...] = second
        out = centred(second)[0] * row(g2, 0) + row(s2, 0)
        q_out[...] = out.astype(B16)
        pay_s[...] = jnp.zeros_like(pay_s)
        lanes = lax.broadcasted_iota(I32, (1, width), 1)
        for i in range(4):
            pay_s[i : i + 1, :] = cls_p[i : i + 1]
            pay_s[4 + i : 5 + i, :] = out[i * ql : i * ql + 1]
            mask = jnp.zeros((1, width), F32)
            for j in range(positives.shape[1]):
                mask = jnp.where((lanes == positives[i, j]) & (j < counts[i]), 1.0, mask)
            pay_s[8 + i : 9 + i, :] = mask
        payload[...] = pay_s[...].astype(B16)


def passage_attention_kernel(q, k, v, x, bo, wo, probs, att, first, wo_s, sem):
    copy = pltpu.make_async_copy(wo.at[1], wo_s, sem)

    @pl.when(pl.program_id(0) == 0)
    def _():
        copy.start()

    def keep_probs(t, value):
        probs[t] = value

    a = attend(q[...], k[...], v[...], 2, keep_probs)
    att[...] = a

    @pl.when(pl.program_id(0) == 0)
    def _():
        copy.wait()

    first[...] = x[...].astype(F32) + dot(a, wo_s[...]) + row(bo, 1)


def passage_feed_kernel(first, g1, s1, bu, bd, g2, s2, wu, wd, act, slope, second, out, wu_s, wd_s, sems):
    copies = [
        pltpu.make_async_copy(wu.at[1], wu_s, sems.at[0]),
        pltpu.make_async_copy(wd.at[1], wd_s, sems.at[1]),
    ]

    @pl.when(pl.program_id(0) == 0)
    def _():
        for c in copies:
            c.start()
        for c in copies:
            c.wait()

    def keep(at, a, s):
        act[:, at] = a
        slope[:, at] = s.astype(B16)

    result = feed(first[...], wu_s, row(bu, 1), wd_s, row(bd, 1), row(g1, 1), row(s1, 1), keep)
    second[...] = result
    out[...] = (centred(result)[0] * row(g2, 1) + row(s2, 1)).astype(B16)


def send_unit(wide, grads, table, keep, send, offset, sem_keep, sem_send):
    half, _, width = keep.shape
    blocks = 2 * half
    rows = grads.shape[0] * grads.shape[1] // (width * blocks)
    across = grads.shape[1] // width

    def start(out, base, sem):
        def body(r, carry):
            c = table[base + r]
            src = grads.at[
                pl.ds(pl.multiple_of(c // across * rows, rows), rows),
                pl.ds(pl.multiple_of(c % across * width, width), width),
            ] if wide else grads.at[pl.ds(pl.multiple_of(c * rows, rows), rows), :]
            pltpu.make_async_copy(src, out.at[r, pl.ds(offset, rows), :], sem).start()
            return carry

        lax.fori_loop(0, half, body, 0)

    start(send, half, sem_send)
    start(keep, 0, sem_keep)


def wait_units(keep, send, sem_keep, sem_send):
    pltpu.make_async_copy(send, send, sem_send).wait()
    pltpu.make_async_copy(keep, keep, sem_keep).wait()


def feed_back(d_out, second, first, slope, w_down, w_up, g2, g1, s1):
    d_second, gg2, gs2, _ = norm_back(second, g2, d_out)
    d_down = d_second.astype(B16)
    gb_down = jnp.sum(d_down.astype(F32), 0, keepdims=True)
    d_normed = d_second
    d_inner, gb_up = [], []
    for j in range(w_up.shape[1] // 512):
        at = slice(j * 512, (j + 1) * 512)
        d = (dot_nt(d_down, w_down[at, :]) * slope[:, at].astype(F32)).astype(B16)
        gb_up.append(jnp.sum(d.astype(F32), 0, keepdims=True))
        d_normed = d_normed + dot_nt(d, w_up[:, at])
        d_inner.append(d)
    d_first, gg1, gs1, hat = norm_back(first, g1, d_normed)
    low = (hat * g1 + s1).astype(B16)
    return d_down, d_inner, d_first, low, (gg1, gs1, gb_down, gg2, gs2, gb_up)


def contrast(rowsel, gathered, base, scale):
    total_rows = rowsel.shape[0]
    z = gathered[...]
    place = lax.broadcasted_iota(I32, (total_rows, z.shape[0]), 1)
    sel = rowsel[...]

    def rows_at(k):
        return dot(jnp.where(place == sel + k, 1.0, 0.0).astype(B16), z)

    all_p, all_q, mask = rows_at(0), rows_at(4), rows_at(8)[:, :total_rows]
    sim = dot_nt(all_q.astype(B16), all_p.astype(B16)) * scale
    expo = jnp.exp(sim - jnp.max(sim, -1, keepdims=True))
    total = jnp.sum(expo, -1, keepdims=True)
    hit = mask * expo
    pos_total = jnp.sum(hit, -1, keepdims=True)
    terms = jnp.log(total) - jnp.log(pos_total)
    coeff = expo / total - hit / pos_total
    mine = jnp.where(
        lax.broadcasted_iota(I32, (8, total_rows), 1)
        == base + lax.broadcasted_iota(I32, (8, total_rows), 0),
        1.0,
        0.0,
    )
    d_q = dot_high(dot_high(mine, coeff), all_p) * scale
    d_p = dot_high(dot_high(mine, coeff.T), all_q) * scale
    return dot_high(mine, jnp.broadcast_to(terms, (total_rows, 128))), d_q, d_p


def question_back_kernel(
    table,
    rowsel,
    gathered,
    x,
    cot,
    q,
    k,
    v,
    probs,
    att,
    first,
    second,
    act,
    slope,
    g1,
    s1,
    g2,
    wq,
    wk,
    wv,
    wo,
    wu,
    wd,
    terms,
    d_cls_p,
    x_grad,
    small,
    keep,
    send,
    wqkv_s,
    wo_s,
    wu_s,
    wd_s,
    g_down,
    g_up,
    g_att,
    sems,
    out_sems,
):
    copies = [
        pltpu.make_async_copy(src.at[0], dst, sems.at[i])
        for i, (src, dst) in enumerate(
            (
                (wd, wd_s),
                (wu, wu_s),
                (wo, wo_s),
                (wq, wqkv_s.at[0]),
                (wk, wqkv_s.at[1]),
                (wv, wqkv_s.at[2]),
            )
        )
    ]
    for c in copies:
        c.start()
    n = table.shape[0] - 1
    rows = 2048 // n
    count = 4
    length = x.shape[0] // count
    width = x.shape[1]
    scale = 2.0 / float(np.sqrt(width))
    loss, d_q, d_p = contrast(rowsel, gathered, table[n] * count, scale)
    terms[...] = loss
    d_cls_p[...] = d_p
    place = lax.broadcasted_iota(I32, x.shape, 0)
    d_out = cot[...].astype(F32)
    for i in range(count):
        d_out = d_out + jnp.where(place == i * length, d_q[i : i + 1], 0.0)
    for c in copies[:2]:
        c.wait()
    d_down, d_inner, d_first, low, sums = feed_back(
        d_out, second[...], first[...], slope, wd_s, wu_s, row(g2, 0), row(g1, 0), row(s1, 0)
    )
    gg1, gs1, gb_down, gg2, gs2, gb_up = sums
    g_down[...] = dot_tn(act[...], d_down).astype(B16)
    send_unit(False, g_down, table, keep, send, 0, out_sems.at[0], out_sems.at[1])
    for j, d in enumerate(d_inner):
        g_up[:, j * 512 : (j + 1) * 512] = dot_tn(low, d).astype(B16)
    send_unit(True, g_up, table, keep, send, rows, out_sems.at[0], out_sems.at[1])
    for c in copies[2:]:
        c.wait()
    d_branch = d_first.astype(B16)
    d_att = dot_nt(d_branch, wo_s[...]).astype(B16)
    dq, dk, dv = [], [], []
    for i in range(count):
        at = slice(i * length, (i + 1) * length)
        one = attend_back(
            q[at, :], k[at, :], v[at, :], d_att[at], 4, lambda t, i=i: probs[i, t]
        )
        for parts, value in zip((dq, dk, dv), one):
            parts.append(value)
    dq, dk, dv = (jnp.concatenate(p, 0) for p in (dq, dk, dv))
    rows_x = x[...]
    for i, d in enumerate((dq, dk, dv)):
        g_att[i * width : (i + 1) * width, :] = dot_tn(rows_x, d).astype(B16)
    g_att[3 * width :, :] = dot_tn(att[...], d_branch).astype(B16)
    send_unit(False, g_att, table, keep, send, 2 * rows, out_sems.at[0], out_sems.at[1])
    x_grad[...] = (
        d_first + dot_nt(dq, wqkv_s[0]) + dot_nt(dk, wqkv_s[1]) + dot_nt(dv, wqkv_s[2])
    )
    small[...] = jnp.zeros_like(small)
    values = (
        jnp.sum(dq.astype(F32), 0, keepdims=True),
        jnp.sum(dv.astype(F32), 0, keepdims=True),
        jnp.sum(d_branch.astype(F32), 0, keepdims=True),
        gg1, gs1, gb_down, gg2, gs2, *gb_up,
    )
    for i, value in enumerate(values):
        small[i : i + 1, :] = value
    wait_units(keep, send, out_sems.at[0], out_sems.at[1])


def passage_feed_back_kernel(
    table,
    d_cls,
    cot,
    first,
    second,
    slope,
    g1,
    s1,
    g2,
    act,
    wu,
    wd,
    d_first,
    small,
    keep,
    send,
    wu_s,
    wd_s,
    act_s,
    d_down_s,
    d_inner_s,
    low_s,
    g_down,
    g_up,
    sems,
    out_sems,
):
    b = pl.program_id(0)
    nb = pl.num_programs(0)
    copies = [
        pltpu.make_async_copy(src, dst, sems.at[i])
        for i, (src, dst) in enumerate(((wd.at[1], wd_s), (wu.at[1], wu_s), (act, act_s)))
    ]

    @pl.when(b == 0)
    def _():
        for c in copies:
            c.start()
        small[...] = jnp.zeros_like(small)
        for c in copies[:2]:
            c.wait()

    length = cot.shape[0]
    place = lax.broadcasted_iota(I32, cot.shape, 0)
    d_out = cot[...].astype(F32) + jnp.where(place == 0, d_cls[pl.ds(b, 1), :], 0.0)
    d_down, d_inner, d_one, low, sums = feed_back(
        d_out, second[...], first[...], slope, wd_s, wu_s, row(g2, 1), row(g1, 1), row(s1, 1)
    )
    at = pl.ds(pl.multiple_of(b * length, length), length)
    d_down_s[at, :] = d_down
    low_s[at, :] = low
    for j, d in enumerate(d_inner):
        d_inner_s[at, j * 512 : (j + 1) * 512] = d
    d_first[...] = d_one
    gg1, gs1, gb_down, gg2, gs2, gb_up = sums
    for i, value in enumerate((gg1, gs1, gb_down, gg2, gs2, *gb_up)):
        small[3 + i : 4 + i, :] += value

    @pl.when(b == nb - 1)
    def _():
        copies[2].wait()
        for j in range(4):
            at = slice(j * 512, (j + 1) * 512)
            g_down[at, :] = dot_tn(act_s[:, at], d_down_s[...]).astype(B16)
        send_unit(False, g_down, table, keep, send, 0, out_sems.at[0], out_sems.at[1])
        for j in range(4):
            at = slice(j * 512, (j + 1) * 512)
            g_up[:, at] = dot_tn(low_s[...], d_inner_s[:, at]).astype(B16)
        rows = 2048 // (table.shape[0] - 1)
        send_unit(True, g_up, table, keep, send, rows, out_sems.at[0], out_sems.at[1])
        wait_units(keep, send, out_sems.at[0], out_sems.at[1])


def passage_attention_back_kernel(
    table,
    d_first,
    q,
    k,
    v,
    probs,
    x,
    small_q,
    small_p,
    att,
    wq,
    wk,
    wv,
    wo,
    x_grad,
    keep,
    send,
    wqkv_s,
    wo_s,
    att_s,
    x_s,
    branch_s,
    d_s,
    small_s,
    sent_s,
    g_att,
    sems,
    out_sems,
):
    b = pl.program_id(0)
    nb = pl.num_programs(0)
    copies = [
        pltpu.make_async_copy(src, dst, sems.at[i])
        for i, (src, dst) in enumerate(
            (
                (wo.at[1], wo_s),
                (wq.at[1], wqkv_s.at[0]),
                (wk.at[1], wqkv_s.at[1]),
                (wv.at[1], wqkv_s.at[2]),
                (att, att_s),
            )
        )
    ]

    @pl.when(b == 0)
    def _():
        for c in copies:
            c.start()
        small_s[...] = small_p[...]
        copies[0].wait()

    length, width = d_first.shape
    d_branch = d_first[...].astype(B16)
    d_att = dot_nt(d_branch, wo_s[...]).astype(B16)
    dq, dk, dv = attend_back(q[...], k[...], v[...], d_att, 2, lambda t: probs[t])
    at = pl.ds(pl.multiple_of(b * length, length), length)
    branch_s[at, :] = d_branch
    x_s[at, :] = x[...]
    for i, d in enumerate((dq, dk, dv)):
        d_s[i, at, :] = d
    for i, d in enumerate((dq, dv, d_branch)):
        small_s[i : i + 1, :] += jnp.sum(d.astype(F32), 0, keepdims=True)

    @pl.when(b == 0)
    def _():
        for c in copies[1:4]:
            c.wait()

    x_grad[...] = (
        d_first[...] + dot_nt(dq, wqkv_s[0]) + dot_nt(dk, wqkv_s[1]) + dot_nt(dv, wqkv_s[2])
    )

    @pl.when(b == nb - 1)
    def _():
        copies[4].wait()
        for i in range(3):
            g_att[i * width : (i + 1) * width, :] = dot_tn(x_s[...], d_s[i]).astype(B16)
        g_att[3 * width :, :] = dot_tn(att_s[...], branch_s[...]).astype(B16)
        send_unit(False, g_att, table, keep, send, 0, out_sems.at[0], out_sems.at[1])
        sent_s[...] = jnp.zeros_like(sent_s)
        top = lax.broadcasted_iota(I32, (16, width), 0) == 0
        for e, ref in enumerate((small_q, small_s)):
            for i in range(NSMALL):
                sent_s[e * NSMALL + i] = jnp.where(top, ref[i : i + 1, :], 0.0).astype(B16)
        n = table.shape[0] - 1
        half = n // 2
        rows = 2048 // n

        def start(out, base, sem):
            def body(r, carry):
                pltpu.make_async_copy(
                    sent_s.at[table[base + r]], out.at[r, pl.ds(rows, 16), :], sem
                ).start()
                return carry

            lax.fori_loop(0, half, body, 0)

        start(send, half, out_sems.at[1])
        start(keep, 0, out_sems.at[0])
        wait_units(keep, send, out_sems.at[0], out_sems.at[1])


def place_kernel(e, kinds, starts, n_alias, with_small, *refs):
    table = refs[0]
    pieces = refs[1 : 1 + len(starts)]
    outs = refs[1 + len(starts) + n_alias :]
    n_out = sum(4 if kind == "att" else 1 for kind in kinds)
    n_small = 9 if with_small else 0
    targets, smalls = outs[:n_out], outs[n_out : n_out + n_small]
    scratch = outs[n_out + n_small :]
    stages, sems = scratch[: len(kinds)], scratch[len(kinds)]
    small_s = scratch[len(kinds) + 1] if with_small else None
    n = table.shape[0] - 1
    rows = 2048 // n
    for piece, start in zip(pieces, starts):

        def body(r, carry, piece=piece, start=start):
            c = table[start + r]
            k = 0
            for u, kind in enumerate(kinds):
                stage = stages[u].at[start + r]
                stage[...] = piece[r, u * rows : (u + 1) * rows, :].astype(F32)
                if kind == "down":
                    pltpu.make_async_copy(
                        stage,
                        targets[k].at[e, pl.ds(pl.multiple_of(c * rows, rows), rows), :],
                        sems.at[k],
                    ).start()
                    k += 1
                elif kind == "up":
                    pltpu.make_async_copy(
                        stage,
                        targets[k].at[
                            e,
                            pl.ds(pl.multiple_of(c // 4 * rows, rows), rows),
                            pl.ds(pl.multiple_of(c % 4 * 512, 512), 512),
                        ],
                        sems.at[k],
                    ).start()
                    k += 1
                else:
                    quarter = n // 4
                    for m in range(4):

                        @pl.when(c // quarter == m)
                        def _(m=m, k=k, stage=stage):
                            at = pl.ds(pl.multiple_of(c % quarter * rows, rows), rows)
                            pltpu.make_async_copy(
                                stage, targets[k + m].at[e, at, :], sems.at[k + m]
                            ).start()

                    k += 4
            if with_small:
                block = piece[r, len(kinds) * rows : len(kinds) * rows + 16, :].astype(F32)
                small_s[c] = block[0:8]
            return carry

        lax.fori_loop(0, piece.shape[0], body, 0)
    if with_small:
        for f in range(2):
            for i in range(8):
                smalls[i][f : f + 1, :] = small_s[f * NSMALL + i, 0:1, :]
            for j in range(4):
                smalls[8][f : f + 1, j * 512 : (j + 1) * 512] = small_s[f * NSMALL + 8 + j, 0:1, :]
    for k, target in enumerate(targets):
        pltpu.make_async_copy(target.at[e], target.at[e], sems.at[k]).wait()


def rounds_of(mesh_shape):
    dp, rep = mesh_shape["dp"], mesh_shape["rep"]
    rep_bits = [1 << i for i in range(rep.bit_length() - 1)]
    dp_bits = [rep << i for i in range(dp.bit_length() - 1)]
    even = rep_bits[:1] + rep_bits[1:] + dp_bits
    odd = rep_bits[:1] + dp_bits[:1] + rep_bits[1:] + dp_bits[1:]
    return even, odd


def order_table(rounds, n):
    depth = len(rounds[0])
    table = np.zeros((n, n), np.int32)
    for d in range(n):
        for r in range(n):
            c = d ^ (rounds[0][0] if r >> (depth - 1) & 1 else 0)
            for k in range(1, depth):
                if r >> (depth - 1 - k) & 1:
                    c ^= rounds[c & 1][k]
            table[d, r] = c
    return table


def exchange(x, rounds, k, n):
    perm = [(d, d ^ rounds[d & 1][k]) for d in range(n)]
    return lax.ppermute(x, AXES, perm)


def add(a, b):
    return (a.astype(F32) + b.astype(F32)).astype(B16)


def reduce_blocks(keep, send, rounds, n):
    depth = len(rounds[0])
    for k in range(depth):
        got = exchange(send, rounds, k, n)
        half = keep.shape[0] // 2
        if half:
            send = add(keep[half:], got[half:])
            keep = add(keep[:half], got[:half])
        else:
            keep = add(keep, got)
    return keep


def gather_blocks(block, rounds, n):
    depth = len(rounds[0])
    pieces = [block]
    for k in range(depth - 1, -1, -1):
        if k > 0 and len(pieces) > 1:
            pieces = [jnp.concatenate(pieces, 0)]
        pieces = pieces + [exchange(p, rounds, k, n) for p in pieces]
    return pieces


def gather_rows(x, n):
    got = x[None]
    bits = [1 << i for i in range(n.bit_length() - 1)]
    while bits:
        now, bits = bits[:2], bits[2:]
        masks = [0, now[0]] + ([now[1], now[0] | now[1]] if len(now) > 1 else [])
        got = jnp.concatenate(
            [got]
            + [lax.ppermute(got, AXES, [(d, d ^ m) for d in range(n)]) for m in masks[1:]],
            0,
        )
    return got


def params(limit):
    return pltpu.CompilerParams(vmem_limit_bytes=limit * MIB)


def cost(flops, nbytes):
    return pl.CostEstimate(flops=int(flops), bytes_accessed=int(nbytes), transcendentals=0)


def shape(dims, dtype=F32):
    return jax.ShapeDtypeStruct(dims, dtype)


def sem(count):
    return pltpu.SemaphoreType.DMA((count,))


def shards(
    mesh_shape,
    q_tokens,
    p_tokens,
    q_cotangent,
    p_cotangent,
    positives,
    counts,
    wq,
    bq,
    wk,
    wv,
    bv,
    wo,
    bo,
    g1,
    s1,
    wu,
    bu,
    wd,
    bd,
    g2,
    s2,
):
    n = mesh_shape["dp"] * mesh_shape["rep"]
    rounds = rounds_of(mesh_shape)
    me = lax.axis_index("dp") * mesh_shape["rep"] + lax.axis_index("rep")
    table = lax.dynamic_index_in_dim(jnp.asarray(order_table(rounds, n)), me, 0, False)
    table = jnp.concatenate([table, me[None].astype(I32)])
    qn, ql, h = q_tokens.shape
    pn, plen, _ = p_tokens.shape
    ff = wu.shape[2]
    qr, pr = qn * ql, pn * plen
    assert qn == 4 and pn == 4 and h == 512 and ff == 2048 and 24 <= n and 4 * n <= h
    q_x, p_x = q_tokens.reshape(qr, h), p_tokens.reshape(pr, h)
    q_cot, p_cot = q_cotangent.reshape(qr, h), p_cotangent.reshape(pr, h)
    every = jnp.arange(4 * n, dtype=I32)
    rowsel = ((every // 4) ^ me) * 16 + every % 4

    def seq(width=h):
        return pl.BlockSpec((plen, width), lambda b: (b, 0))

    def whole(*dims):
        return pl.BlockSpec(dims, lambda b: (0,) * len(dims))

    one = whole(2, h)
    front = pl.pallas_call(
        front_kernel,
        name="front",
        grid=(pn,),
        in_specs=[SMEM, SMEM, seq(), whole(qr, h), one, one, one, one, one, whole(2, ff), one, one, one]
        + [ANY] * 6,
        out_specs=[seq()] * 3
        + [whole(qr, h)] * 3
        + [whole(qn, 2, 4 * ql, ql), whole(qr, h), whole(qr, h), whole(qr, h)]
        + [whole(qr, ff), whole(qr, ff), whole(qr, h), whole(16, h)],
        out_shape=[shape((pr, h), B16)] * 3
        + [shape((qr, h), B16)] * 3
        + [shape((qn, 2, 4 * ql, ql), B16), shape((qr, h), B16), shape((qr, h)), shape((qr, h))]
        + [shape((qr, ff), B16), shape((qr, ff), B16), shape((qr, h), B16), shape((16, h), B16)],
        scratch_shapes=[
            pltpu.VMEM((3, 2, h, h), B16),
            pltpu.VMEM((2, h, h), B16),
            pltpu.VMEM((2, h, ff), B16),
            pltpu.VMEM((2, ff, h), B16),
            pltpu.VMEM((8, h), F32),
            pltpu.VMEM((8, h), F32),
            pltpu.VMEM((16, h), F32),
            sem(6),
        ],
        compiler_params=params(40),
        cost_estimate=cost(5e9, 25e6),
    )(positives, counts, p_x, q_x, bq, bv, bo, g1, s1, bu, bd, g2, s2, wq, wk, wv, wo, wu, wd)
    (pq, pk, pv, qq, qk, qv, q_probs, q_att, q_first, q_second, q_act, q_slope, q_out, payload) = front

    gathered = gather_rows(payload, n).reshape(n * 16, h)

    groups = HEADS // 2
    probs_spec = pl.BlockSpec((None, groups, 2 * plen, plen), lambda b: (b, 0, 0, 0))
    p_probs, p_att, p_first = pl.pallas_call(
        passage_attention_kernel,
        name="passage_attention",
        grid=(pn,),
        in_specs=[seq()] * 4 + [one, ANY],
        out_specs=[probs_spec, seq(), seq()],
        out_shape=[
            shape((pn, groups, 2 * plen, plen), B16),
            shape((pr, h), B16),
            shape((pr, h)),
        ],
        scratch_shapes=[pltpu.VMEM((h, h), B16), pltpu.SemaphoreType.DMA],
        compiler_params=params(32),
        cost_estimate=cost(4e9, 12e6),
    )(pq, pk, pv, p_x, bo, wo)
    p_act, p_slope, p_second, p_out = pl.pallas_call(
        passage_feed_kernel,
        name="passage_feed",
        grid=(pn,),
        in_specs=[seq(), one, one, whole(2, ff), one, one, one, ANY, ANY],
        out_specs=[seq(ff), seq(ff), seq(), seq()],
        out_shape=[
            shape((pr, ff), B16),
            shape((pr, ff), B16),
            shape((pr, h)),
            shape((pr, h), B16),
        ],
        scratch_shapes=[pltpu.VMEM((h, ff), B16), pltpu.VMEM((ff, h), B16), sem(2)],
        compiler_params=params(32),
        cost_estimate=cost(9e9, 18e6),
    )(p_first, g1, s1, bu, bd, g2, s2, wu, wd)

    rows = 2048 // n
    half = n // 2
    terms, d_cls_p, q_grad, small_q, q_keep, q_send = pl.pallas_call(
        question_back_kernel,
        name="question_back",
        in_specs=[SMEM] + [VMEM] * 16 + [ANY] * 6,
        out_specs=[VMEM] * 4 + [ANY] * 2,
        out_shape=[
            shape((8, 128)),
            shape((8, h)),
            shape((qr, h)),
            shape((16, h)),
            shape((half, 3 * rows, h), B16),
            shape((half, 3 * rows, h), B16),
        ],
        scratch_shapes=[
            pltpu.VMEM((3, h, h), B16),
            pltpu.VMEM((h, h), B16),
            pltpu.VMEM((h, ff), B16),
            pltpu.VMEM((ff, h), B16),
            pltpu.VMEM((ff, h), B16),
            pltpu.VMEM((h, ff), B16),
            pltpu.VMEM((4 * h, h), B16),
            sem(6),
            sem(2),
        ],
        compiler_params=params(40),
        cost_estimate=cost(5e9, 20e6),
    )(
        table, rowsel[:, None], gathered, q_x, q_cot, qq, qk, qv, q_probs, q_att, q_first, q_second,
        q_act, q_slope, g1, s1, g2, wq, wk, wv, wo, wu, wd,
    )
    q_block = reduce_blocks(q_keep, q_send, rounds, n)
    q_pieces = gather_blocks(q_block, rounds, n)

    d_first, small_p, f_keep, f_send = pl.pallas_call(
        passage_feed_back_kernel,
        name="passage_feed_back",
        grid=(pn,),
        in_specs=[SMEM, whole(8, h), seq(), seq(), seq(), seq(ff), one, one, one] + [ANY] * 3,
        out_specs=[seq(), whole(16, h), ANY, ANY],
        out_shape=[
            shape((pr, h)),
            shape((16, h)),
            shape((half, 2 * rows, h), B16),
            shape((half, 2 * rows, h), B16),
        ],
        scratch_shapes=[
            pltpu.VMEM((h, ff), B16),
            pltpu.VMEM((ff, h), B16),
            pltpu.VMEM((pr, ff), B16),
            pltpu.VMEM((pr, h), B16),
            pltpu.VMEM((pr, ff), B16),
            pltpu.VMEM((pr, h), B16),
            pltpu.VMEM((ff, h), B16),
            pltpu.VMEM((h, ff), B16),
            sem(3),
            sem(2),
        ],
        compiler_params=params(44),
        cost_estimate=cost(18e9, 22e6),
    )(table, d_cls_p, p_cot, p_first, p_second, p_slope, g1, s1, g2, p_act, wu, wd)
    f_block = reduce_blocks(f_keep, f_send, rounds, n)
    f_pieces = gather_blocks(f_block, rounds, n)

    p_grad, a_keep, a_send = pl.pallas_call(
        passage_attention_back_kernel,
        name="passage_attention_back",
        grid=(pn,),
        in_specs=[SMEM, seq(), seq(), seq(), seq(), probs_spec, seq(), whole(16, h), whole(16, h)]
        + [ANY] * 5,
        out_specs=[seq(), ANY, ANY],
        out_shape=[
            shape((pr, h)),
            shape((half, rows + 16, h), B16),
            shape((half, rows + 16, h), B16),
        ],
        scratch_shapes=[
            pltpu.VMEM((3, h, h), B16),
            pltpu.VMEM((h, h), B16),
            pltpu.VMEM((pr, h), B16),
            pltpu.VMEM((pr, h), B16),
            pltpu.VMEM((pr, h), B16),
            pltpu.VMEM((3, pr, h), B16),
            pltpu.VMEM((16, h), F32),
            pltpu.VMEM((n, 16, h), B16),
            pltpu.VMEM((4 * h, h), B16),
            sem(5),
            sem(2),
        ],
        compiler_params=params(44),
        cost_estimate=cost(10e9, 20e6),
    )(table, d_first, pq, pk, pv, p_probs, p_x, small_q, small_p, p_att, wq, wk, wv, wo)
    a_block = reduce_blocks(a_keep, a_send, rounds, n)
    a_pieces = gather_blocks(a_block, rounds, n)

    def place(e, kinds, pieces, before, with_small):
        starts, at = [], 0
        for piece in pieces:
            starts.append(at)
            at += piece.shape[0]
        dims = []
        for kind in kinds:
            dims += {"down": [(2, ff, h)], "up": [(2, h, ff)], "att": [(2, h, h)] * 4}[kind]
        outs = [shape(d) for d in dims]
        smalls = [shape((2, h))] * 8 + [shape((2, ff))] if with_small else []
        first = 1 + len(pieces)
        return pl.pallas_call(
            functools.partial(place_kernel, e, kinds, tuple(starts), len(before), with_small),
            name="place",
            in_specs=[SMEM] + [VMEM] * len(pieces) + [ANY] * len(before),
            out_specs=[ANY] * len(outs) + [VMEM] * len(smalls),
            out_shape=outs + smalls,
            input_output_aliases={first + i: i for i in range(len(before))},
            scratch_shapes=[pltpu.VMEM((n, rows, h), F32) for _ in kinds]
            + [sem(len(outs))]
            + ([pltpu.VMEM((n, 8, h), F32)] if with_small else []),
            compiler_params=params(40),
            cost_estimate=cost(1e6, len(kinds) * 6 * MIB),
        )(table, *pieces, *before)

    down, up, gq, gk, gv, go = place(0, ("down", "up", "att"), q_pieces, [], False)
    down, up = place(1, ("down", "up"), f_pieces, [down, up], False)
    gq, gk, gv, go, *smalls = place(1, ("att",), a_pieces, [gq, gk, gv, go], True)
    sbq, sbv, sbo, sg1, ss1, sbd, sg2, ss2, sbu = smalls
    return (
        q_out.reshape(qn, ql, h),
        p_out.reshape(pn, plen, h),
        terms[:qn, 0],
        q_grad.reshape(qn, ql, h),
        p_grad.reshape(pn, plen, h),
        gq, sbq, gk, gv, sbv, go, sbo, sg1, ss1, up, sbu, down, sbd, sg2, ss2,
    )


def solution(mesh):
    split = P(AXES)
    return jax.shard_map(
        functools.partial(shards, dict(mesh.shape)),
        mesh=mesh,
        in_specs=(split,) * 6 + (P(),) * 15,
        out_specs=(split,) * 5 + (P(),) * 15,
        check_vma=False,
    )
```

time: 773 us -> 304 us (0.39); the launches traced: 763 us -> 303 us
  waiting for transfers between devices: 413 us -> 112 us
  matrix products: 130 us -> 0 us
  Pallas kernels: 0 us -> 100 us
  blocking collectives: 86.5 us -> 0 us
  local copies, waits for them, and re-layouts: 84.5 us -> 49.5 us
  starting transfers between devices: 0.25 us -> 31.3 us
  other arithmetic: 32.8 us -> 7.95 us
  between operations: 15.5 us -> 1.68 us
    psum x1 -> x0, waiting for transfers between devices: 342 us -> none  [shards(): lax.psum((joined[0], joined[1], joined[2], joined[3], joined[4], joined[5...]
    dot_general x49 -> x0, matrix products: 121 us -> none  [the longest x2 30.4 us: encoder_forward(): inner = jnp.dot(normed_low, w_up, preferred_element_type=F32) + b_up]
    ppermute x0 -> x40, waiting for transfers between devices: none -> 112 us  [the longest x33 97.7 us: exchange(): return lax.ppermute(x, AXES, perm)]
    pallas_call x0 -> x9, Pallas kernels: none -> 100 us  [the longest x1 21.5 us: shards(): pl.pallas_call(passage_feed_back_kernel, name='passage_feed_back', grid=(...]
    unnamed x3 -> x0, waiting for transfers between devices: 71 us -> none
    all_gather x1 -> x0, blocking collectives: 43.9 us -> none  [shards(): every_cls = lax.all_gather(cls_p, ('dp', 'rep'), axis=0, tiled=True)]
    psum x1 -> x0, blocking collectives: 42.6 us -> none  [shards(): lax.psum((joined[0], joined[1], joined[2], joined[3], joined[4], joined[5...]
    ppermute x0 -> x40, starting transfers between devices: none -> 31.3 us  [the longest x33 22.1 us: exchange(): return lax.ppermute(x, AXES, perm)]
  transfers between devices with their start and end apart: 2 -> 40, of which waited for: 2 -> 19; matrix products, arithmetic and copies ran while one was open for 8% -> 3% of each run, Pallas kernels for 0% -> 23%
where the time goes in v1:
time: 304 us; the launch traced here: 303 us
  waiting for transfers between devices  112 us (37%)
  Pallas kernels  100 us (33%)
  local copies, waits for them, and re-layouts  49.5 us (16%)
  starting transfers between devices  31.3 us (10%)
  other arithmetic  7.95 us (3%)
    ppermute x33, waiting for transfers between devices, exchange(): return lax.ppermute(x, AXES, perm)  97.7 us
    unnamed x156, local copies, waits for them, and re-layouts  47.5 us
    ppermute x33, starting transfers between devices, exchange(): return lax.ppermute(x, AXES, perm)  22.1 us
    pallas_call x1, Pallas kernels, shards(): pl.pallas_call(passage_feed_back_kernel, name='passage_feed_back', grid=(...  21.5 us
    pallas_call x1, Pallas kernels, shards(): pl.pallas_call(passage_attention_back_kernel, name='passage_attention_bac...  17.1 us
    pallas_call x1, Pallas kernels, shards(): pl.pallas_call(question_back_kernel, name='question_back', in_specs=[SMEM...  15.4 us
    ppermute x7, waiting for transfers between devices, gather_rows(): lax.ppermute(got, AXES, [(d, d ^ m) for d in range(n)])  14.5 us
    pallas_call x1, Pallas kernels, shards(): pl.pallas_call(passage_feed_kernel, name='passage_feed', grid=(pn,), in_s...  14.2 us
  transfers between devices with their start and end apart: 40, of which 19 were waited for; matrix products, arithmetic and copies ran while one was open for 3% of the time, Pallas kernels for 23%

profile of v1, /device:TPU:0, one launch (start us, length us, event | category | flops | bytes accessed | tf_op | source)
XLA Modules:
  0.0 303.0 jit_solution(34028417276375969)
XLA Ops:
  1.9 1.2 copy-done.6
  3.1 1.2 copy-done.9
  4.3 1.2 copy-done.12
  5.6 1.2 copy-done.15
  15.3 12.9 %front.1 = (bf16[1024,512]{1,0:T(8,128)(2,1)S(1)}, bf16[1024,512]{1,0:T(8,128)(2,1)S(1)}, bf16[1024,512]{1,0:T(8,128)(2,1)S(1)}, bf16[256,512]{1,0:T(8,128)(2,1)...) custom-call(s32[4,4]{1,0:T(4,128)S(1)} %copy-done.38, ...), custom_call_target="tpu_custom_call" | custom-call | flops 5000000000 | bytes 25000000 | tf_op jit(solution)/shard_map/front/pallas_call | solution.py:870
  37.6 2.4 collective-permute-start.2
  41.4 2.3 collective-permute-done.1
  43.7 2.6 collective-permute-start.5
  49.1 1.9 collective-permute-done.3
  52.9 2.6 collective-permute-start.6
  56.3 10.2 %collective-permute-done.6 = bf16[16,16,512]{2,1,0:T(8,128)(2,1)S(1)} collective-permute-done((bf16[16,16,512]{2,1,0:T(8,128)(2,1)}, bf16[16,16,512]{2,1,0:T(8,128)(2,1)S(1)}, u32[]{:S(2)}, u32[]{:S(2)}) %collective-permute-start.6) | collective-permute-done | bytes 262176 | tf_op jit(solution)/shard_map/ppermute | solution.py:802
  67.8 1.2 copy-done.16
  69.0 1.2 copy-done.41
  70.2 1.2 copy-done.43
  77.5 15.4 %question_back.1 = (f32[8,128]{1,0:T(8,128)S(1)}, f32[8,512]{1,0:T(8,128)S(1)}, f32[256,512]{1,0:T(8,128)}, f32[16,512]{1,0:T(8,128)S(1)}, bf16[16,192,512]{2,1,...) custom-call(s32[33]{0:T(128)S(1)} %pad_add_fusion.table.refs_0_, s32[128,1]{1,0:T(8,128)S(1)} %fusion.8.rowsel, ...), custom_call_target="tpu_custom_call" | custom-call | flops 5000000000 | bytes 20000000 | tf_op jit(solution)/shard_map/question_back/pallas_call | solution.py:937
  94.2 1.2 copy-done.60
  96.7 7.1 %passage_attention.1 = (bf16[4,4,512,256]{3,2,1,0:T(8,128)(2,1)S(1)}, bf16[1024,512]{1,0:T(8,128)(2,1)S(1)}, f32[1024,512]{1,0:T(8,128)S(1)}) custom-call(bf16[1024,512]{1,0:T(8,128)(2,1)S(1)} %copy-done.57, bf16[1024,512]{1,0:T(8,128)(2,1)S(1)} %copy-done.60, bf16[1024,512]{1,0:T(8,128)(2,1)S(1)} %copy-done.63, bf16[1024,512]{1,0:T(8,128)(2,1)S(1)} %bitcast.22, ...), custom_call_target="tpu_custom_call" | custom-call | flops 4000000000 | bytes 12000000 | tf_op jit(solution)/shard_map/passage_attention/pallas_call | solution.py:903
  104.9 14.2 %passage_feed.1 = (bf16[1024,2048]{1,0:T(8,128)(2,1)S(1)}, bf16[1024,2048]{1,0:T(8,128)(2,1)S(1)}, f32[1024,512]{1,0:T(8,128)S(1)}, bf16[1024,512]{1,0:T(8,128)(2,1)}) custom-call(f32[1024,512]{1,0:T(8,128)S(1)} %get-tuple-element.79.first, f32[2,512]{1,0:T(2,128)S(1)} %copy-done.33, f32[2,512]{1,0:T(2,128)S(1)} %copy-done.35, f32[2,2048]{1,0:T(2,128)S(1)} %copy-done.23, ...), custom_call_target="tpu_custom_call" | custom-call | flops 8999999488 | bytes 18000000 | tf_op jit(solution)/shard_map/passage_feed/pallas_call | solution.py:918
  119.1 2.0 copy-done.71
  121.1 1.3 copy-done.73
  122.4 4.5 %add_convert_fusion.1 = (bf16[8,192,512]{2,1,0:T(8,128)(2,1)S(1)}, bf16[8,192,512]{2,1,0:T(8,128)(2,1)S(1)}) fusion(bf16[16,192,512]{2,1,0:T(8,128)(2,1)} %collective-permute-done.18, bf16[16,192,512]{2,1,0:T(8,128)(2,1)S(1)} %get-tuple-element.105), kind=kLoop, calls=%fused_computation.1 | loop fusion | flops 6291456 | bytes 9437184 | tf_op jit(solution)/shard_map/convert_element_type | solution.py:768
  127.7 21.5 %passage_feed_back.1 = (f32[1024,512]{1,0:T(8,128)S(1)}, f32[16,512]{1,0:T(8,128)S(1)}, bf16[16,128,512]{2,1,0:T(8,128)(2,1)S(1)}, bf16[16,128,512]{2,1,0:T(8,128)(2,1)S(1)}) custom-call(s32[33]{0:T(128)S(1)} %pad_add_fusion.table.refs_0_, f32[8,512]{1,0:T(8,128)S(1)} %get-tuple-element.93.d_cls, bf16[1024,512]{1,0:T(8,128)(2,1)S(1)} %bitcast.20, ...), custom_call_target="tpu_custom_call" | custom-call | flops 17999998976 | bytes 22000000 | tf_op jit(solution)/shard_map/passage_feed_back/pallas_call | solution.py:970
  151.4 2.1 collective-permute-done.29
  154.2 1.3 collective-permute-start.30
  155.6 12.7 %collective-permute-done.20 = bf16[4,192,512]{2,1,0:T(8,128)(2,1)S(1)} collective-permute-done((bf16[4,192,512]{2,1,0:T(8,128)(2,1)S(1)}, bf16[4,192,512]{2,1,0:T(8,128)(2,1)S(1)}, u32[]{:S(2)}, u32[]{:S(2)}) %collective-permute-start.20) | collective-permute-done | bytes 786464 | tf_op jit(solution)/shard_map/ppermute | solution.py:764
  169.4 17.1 %passage_attention_back.1 = (f32[1024,512]{1,0:T(8,128)}, bf16[16,80,512]{2,1,0:T(8,128)(2,1)}, bf16[16,80,512]{2,1,0:T(8,128)(2,1)}) custom-call(s32[33]{0:T(128)S(1)} %pad_add_fusion.table.refs_0_, f32[1024,512]{1,0:T(8,128)} %copy-done.72, bf16[1024,512]{1,0:T(8,128)(2,1)S(1)} %copy-done.58, bf16[1024,512]{1,0:T(8,128)(2,1)S(1)} %copy-done.61, ...), custom_call_target="tpu_custom_call" | custom-call | flops 10000000000 | bytes 20000000 | tf_op jit(solution)/shard_map/passage_attention_back/pallas_call | solution.py:1000
  187.0 3.3 %collective-permute-start.22 = (bf16[1,192,512]{2,1,0:T(8,128)(2,1)S(1)}, bf16[1,192,512]{2,1,0:T(8,128)(2,1)S(1)}, u32[]{:S(2)}, u32[]{:S(2)}) collective-permute-start(bf16[1,192,512]{2,1,0:T(8,128)(2,1)S(1)} %add_convert_fusion.17), channel_id=1, source_target_pairs={{0,16},{1,17},{2,18},{3,19},{4,20},{5,21},{6,22},{7,23},{8,24},{9,... | collective-permute-start | bytes 589832 | tf_op jit(solution)/shard_map/ppermute | solution.py:764
  190.4 9.6 %collective-permute-done.22 = bf16[1,192,512]{2,1,0:T(8,128)(2,1)S(1)} collective-permute-done((bf16[1,192,512]{2,1,0:T(8,128)(2,1)S(1)}, bf16[1,192,512]{2,1,0:T(8,128)(2,1)S(1)}, u32[]{:S(2)}, u32[]{:S(2)}) %collective-permute-start.22) | collective-permute-done | bytes 196640 | tf_op jit(solution)/shard_map/ppermute | solution.py:764
  200.3 3.0 collective-permute-start.32
  203.2 8.9 %collective-permute-done.23 = bf16[1,192,512]{2,1,0:T(8,128)(2,1)S(1)} collective-permute-done((bf16[1,192,512]{2,1,0:T(8,128)(2,1)S(1)}, bf16[1,192,512]{2,1,0:T(8,128)(2,1)S(1)}, u32[]{:S(2)}, u32[]{:S(2)}) %collective-permute-start.23) | collective-permute-done | bytes 196640 | tf_op jit(solution)/shard_map/ppermute | solution.py:764
  212.7 1.6 collective-permute-start.8
  214.3 1.9 collective-permute-start.33
  216.2 9.8 %collective-permute-done.24 = bf16[2,192,512]{2,1,0:T(8,128)(2,1)S(1)} collective-permute-done((bf16[2,192,512]{2,1,0:T(8,128)(2,1)S(1)}, bf16[2,192,512]{2,1,0:T(8,128)(2,1)S(1)}, u32[]{:S(2)}, u32[]{:S(2)}) %collective-permute-start.24) | collective-permute-done | bytes 393248 | tf_op jit(solution)/shard_map/ppermute | solution.py:764
  228.6 6.1 %collective-permute-done.34 = bf16[1,128,512]{2,1,0:T(8,128)(2,1)S(1)} collective-permute-done((bf16[1,128,512]{2,1,0:T(8,128)(2,1)S(1)}, bf16[1,128,512]{2,1,0:T(8,128)(2,1)S(1)}, u32[]{:S(2)}, u32[]{:S(2)}) %collective-permute-start.34) | collective-permute-done | bytes 131104 | tf_op jit(solution)/shard_map/ppermute | solution.py:764
  234.8 3.4 %collective-permute-done.25 = bf16[4,192,512]{2,1,0:T(8,128)(2,1)S(1)} collective-permute-done((bf16[4,192,512]{2,1,0:T(8,128)(2,1)S(1)}, bf16[4,192,512]{2,1,0:T(8,128)(2,1)S(1)}, u32[]{:S(2)}, u32[]{:S(2)}) %collective-permute-start.25) | collective-permute-done | bytes 786464 | tf_op jit(solution)/shard_map/ppermute | solution.py:764
  238.3 1.5 collective-permute-start.26
  239.9 4.2 %collective-permute-done.9 = bf16[4,80,512]{2,1,0:T(8,128)(2,1)S(1)} collective-permute-done((bf16[4,80,512]{2,1,0:T(8,128)(2,1)S(1)}, bf16[4,80,512]{2,1,0:T(8,128)(2,1)S(1)}, u32[]{:S(2)}, u32[]{:S(2)}) %collective-permute-start.9) | collective-permute-done | bytes 327712 | tf_op jit(solution)/shard_map/ppermute | solution.py:764
  244.3 6.0 %collective-permute-done.10 = bf16[2,80,512]{2,1,0:T(8,128)(2,1)S(1)} collective-permute-done((bf16[2,80,512]{2,1,0:T(8,128)(2,1)S(1)}, bf16[2,80,512]{2,1,0:T(8,128)(2,1)S(1)}, u32[]{:S(2)}, u32[]{:S(2)}) %collective-permute-start.10) | collective-permute-done | bytes 163872 | tf_op jit(solution)/shard_map/ppermute | solution.py:764
  250.5 6.3 %collective-permute-done.11 = bf16[1,80,512]{2,1,0:T(8,128)(2,1)S(1)} collective-permute-done((bf16[1,80,512]{2,1,0:T(8,128)(2,1)S(1)}, bf16[1,80,512]{2,1,0:T(8,128)(2,1)S(1)}, u32[]{:S(2)}, u32[]{:S(2)}) %collective-permute-start.11) | collective-permute-done | bytes 81952 | tf_op jit(solution)/shard_map/ppermute | solution.py:764
  257.0 2.2 collective-permute-done.36
  259.3 1.6 collective-permute-start.37
  260.9 1.7 collective-permute-done.12
  263.0 5.0 %collective-permute-done.13 = bf16[2,80,512]{2,1,0:T(8,128)(2,1)S(1)} collective-permute-done((bf16[2,80,512]{2,1,0:T(8,128)(2,1)S(1)}, bf16[2,80,512]{2,1,0:T(8,128)(2,1)S(1)}, u32[]{:S(2)}, u32[]{:S(2)}) %collective-permute-start.13) | collective-permute-done | bytes 163872 | tf_op jit(solution)/shard_map/ppermute | solution.py:764
  268.2 10.5 %collective-permute-done.14 = bf16[4,80,512]{2,1,0:T(8,128)(2,1)S(1)} collective-permute-done((bf16[4,80,512]{2,1,0:T(8,128)(2,1)S(1)}, bf16[4,80,512]{2,1,0:T(8,128)(2,1)S(1)}, u32[]{:S(2)}, u32[]{:S(2)}) %collective-permute-start.14) | collective-permute-done | bytes 327712 | tf_op jit(solution)/shard_map/ppermute | solution.py:764
  280.4 9.1 %collective-permute-done.15.refs_2_ = bf16[8,80,512]{2,1,0:T(8,128)(2,1)S(1)} collective-permute-done((bf16[8,80,512]{2,1,0:T(8,128)(2,1)S(1)}, bf16[8,80,512]{2,1,0:T(8,128)(2,1)S(1)}, u32[]{:S(2)}, u32[]{:S(2)}) %collective-permute-start.15) | collective-permute-done | bytes 655392 | tf_op jit(solution)/shard_map/ppermute | solution.py:764
  290.6 5.1 %place.3 = (f32[2,2048,512]{2,1,0:T(8,128)}, f32[2,512,2048]{2,1,0:T(8,128)}, f32[2,512,512]{2,1,0:T(8,128)}, f32[2,512,512]{2,1,0:T(8,128)}, f32[2,512,512]{2,1,0:T(8,128)}, /*index=5*/f32[2,512,512]{2,1,0:T(8,128)}) custom-call(s32[33]{0:T(128)S(1)} %pad_add_fusion.table.refs_0_, bf16[8,192,512]{2,1,0:T(8,128)(2,1)S(1)} %pad_maximum_fusion.refs_1_, ...), custom_call_target="tpu_custom_call" | custom-call | flops 1000000 | bytes 18874368 | tf_op jit(solution)/shard_map/place/pallas_call | solution.py:1042
  295.7 3.8 %place.5 = (f32[2,2048,512]{2,1,0:T(8,128)}, f32[2,512,2048]{2,1,0:T(8,128)}) custom-call(s32[33]{0:T(128)S(1)} %pad_add_fusion.table.refs_0_, bf16[8,128,512]{2,1,0:T(8,128)(2,1)S(1)} %pad_maximum_fusion.1.refs_1_, bf16[8,128,512]{2,1,0:T(8,128)(2,1)S(1)} %collective-permute-done.37.refs_2_, ...), custom_call_target="tpu_custom_call", output_to_operand_aliasing={{0}: (5, {}), {1}: (6, {})} | custom-call | flops 1000000 | bytes 12582912 | tf_op jit(solution)/shard_map/place/pallas_call | solution.py:1042
  299.6 3.2 %place.4 = (f32[2,512,512]{2,1,0:T(8,128)}, f32[2,512,512]{2,1,0:T(8,128)}, f32[2,512,512]{2,1,0:T(8,128)}, f32[2,512,512]{2,1,0:T(8,128)}, f32[2,512]{1,0:T(2,1...) custom-call(s32[33]{0:T(128)S(1)} %pad_add_fusion.table.refs_0_, ...), custom_call_target="tpu_custom_call", output_to_operand_aliasing={{0}: (5, {}), {1}: (6, {}), {2}: (7, {}), {3}: (8, {})} | custom-call | flops 1000000 | bytes 6291456 | tf_op jit(solution)/shard_map/place/pallas_call | solution.py:1042
  (228 shorter events, 49.6 us)
Async XLA Ops:
  15.3 51.2 %copy-start.7 = (bf16[2,512,512]{2,1,0:T(8,128)(2,1)S(1)}, bf16[2,512,512]{2,1,0:T(8,128)(2,1)}, u32[]{:S(2)}) copy-start(bf16[2,512,512]{2,1,0:T(8,128)(2,1)} %wq.5) | copy-start | bytes 3145732
  15.3 51.2 %copy-start.10 = (bf16[2,512,512]{2,1,0:T(8,128)(2,1)S(1)}, bf16[2,512,512]{2,1,0:T(8,128)(2,1)}, u32[]{:S(2)}) copy-start(bf16[2,512,512]{2,1,0:T(8,128)(2,1)} %wk.5) | copy-start | bytes 3145732
  15.3 51.2 %copy-start.20 = (bf16[4,64,512]{2,1,0:T(8,128)(2,1)S(1)}, bf16[4,64,512]{2,1,0:T(8,128)(2,1)}, u32[]{:S(2)}) copy-start(bf16[4,64,512]{2,1,0:T(8,128)(2,1)} %param.22) | copy-start | bytes 786436
  15.3 51.2 %copy-start.21 = (bf16[4,64,512]{2,1,0:T(8,128)(2,1)S(1)}, bf16[4,64,512]{2,1,0:T(8,128)(2,1)}, u32[]{:S(2)}) copy-start(bf16[4,64,512]{2,1,0:T(8,128)(2,1)} %param.24) | copy-start | bytes 786436
  15.3 51.2 %copy-start.33 = (f32[2,512]{1,0:T(2,128)S(1)}, f32[2,512]{1,0:T(2,128)}, u32[]{:S(2)}) copy-start(f32[2,512]{1,0:T(2,128)} %g1.7) | copy-start | bytes 12292
  15.3 51.2 %copy-start.35 = (f32[2,512]{1,0:T(2,128)S(1)}, f32[2,512]{1,0:T(2,128)}, u32[]{:S(2)}) copy-start(f32[2,512]{1,0:T(2,128)} %s1_.7) | copy-start | bytes 12292
  15.3 51.2 %copy-start.37 = (f32[2,512]{1,0:T(2,128)S(1)}, f32[2,512]{1,0:T(2,128)}, u32[]{:S(2)}) copy-start(f32[2,512]{1,0:T(2,128)} %g2.7) | copy-start | bytes 12292
  37.6 3.8 %collective-permute-start.2 = (bf16[1,16,512]{2,1,0:T(8,128)(2,1)S(1)}, bf16[1,16,512]{2,1,0:T(8,128)(2,1)S(1)}, u32[]{:S(2)}, u32[]{:S(2)}) collective-permute-start(bf16[1,16,512]{2,1,0:T(8,128)(2,1)S(1)} %bitcast.15), channel_id=1, source_target_pairs={{0,3},{1,2},{2,1},{3,0},{4,7},{5,6},{6,5},{7,4},{8,11},{9,10},{10,... | collective-permute-start | bytes 49160 | tf_op jit(solution)/shard_map/ppermute | solution.py:802
  40.0 3.7 %collective-permute-start.1 = (bf16[1,16,512]{2,1,0:T(8,128)(2,1)S(1)}, bf16[1,16,512]{2,1,0:T(8,128)(2,1)S(1)}, u32[]{:S(2)}, u32[]{:S(2)}) collective-permute-start(bf16[1,16,512]{2,1,0:T(8,128)(2,1)S(1)} %bitcast.16), channel_id=1, source_target_pairs={{0,2},{1,3},{2,0},{3,1},{4,6},{5,7},{6,4},{7,5},{8,10},{9,11},{10,... | collective-permute-start | bytes 49160 | tf_op jit(solution)/shard_map/ppermute | solution.py:802
  40.5 3.1 %collective-permute-start = (bf16[1,16,512]{2,1,0:T(8,128)(2,1)S(1)}, bf16[1,16,512]{2,1,0:T(8,128)(2,1)S(1)}, u32[]{:S(2)}, u32[]{:S(2)}) collective-permute-start(bf16[1,16,512]{2,1,0:T(8,128)(2,1)S(1)} %bitcast.17), channel_id=1, source_target_pairs={{0,1},{1,0},{2,3},{3,2},{4,5},{5,4},{6,7},{7,6},{8,9},{9,8},{10,11... | collective-permute-start | bytes 49160 | tf_op jit(solution)/shard_map/ppermute | solution.py:802
  43.7 8.6 %collective-permute-start.5 = (bf16[4,16,512]{2,1,0:T(8,128)(2,1)S(1)}, bf16[4,16,512]{2,1,0:T(8,128)(2,1)S(1)}, u32[]{:S(2)}, u32[]{:S(2)}) collective-permute-start(bf16[4,16,512]{2,1,0:T(8,128)(2,1)S(1)} %pad_maximum_fusion.9), channel_id=1, source_target_pairs={{0,12},{1,13},{2,14},{3,15},{4,8},{5,9},{6,10},{7,11},{8,4},{9,5},... | collective-permute-start | bytes 196616 | tf_op jit(solution)/shard_map/ppermute | solution.py:802
  46.3 5.4 %collective-permute-start.4 = (bf16[4,16,512]{2,1,0:T(8,128)(2,1)S(1)}, bf16[4,16,512]{2,1,0:T(8,128)(2,1)S(1)}, u32[]{:S(2)}, u32[]{:S(2)}) collective-permute-start(bf16[4,16,512]{2,1,0:T(8,128)(2,1)S(1)} %pad_maximum_fusion.9), channel_id=1, source_target_pairs={{0,8},{1,9},{2,10},{3,11},{4,12},{5,13},{6,14},{7,15},{8,0},{9,1},... | collective-permute-start | bytes 196616 | tf_op jit(solution)/shard_map/ppermute | solution.py:802
  46.8 4.3 %collective-permute-start.3 = (bf16[4,16,512]{2,1,0:T(8,128)(2,1)S(1)}, bf16[4,16,512]{2,1,0:T(8,128)(2,1)S(1)}, u32[]{:S(2)}, u32[]{:S(2)}) collective-permute-start(bf16[4,16,512]{2,1,0:T(8,128)(2,1)S(1)} %pad_maximum_fusion.9), channel_id=1, source_target_pairs={{0,4},{1,5},{2,6},{3,7},{4,0},{5,1},{6,2},{7,3},{8,12},{9,13},{10,... | collective-permute-start | bytes 196616 | tf_op jit(solution)/shard_map/ppermute | solution.py:802
  52.9 13.5 %collective-permute-start.6 = (bf16[16,16,512]{2,1,0:T(8,128)(2,1)}, bf16[16,16,512]{2,1,0:T(8,128)(2,1)S(1)}, u32[]{:S(2)}, u32[]{:S(2)}) collective-permute-start(bf16[16,16,512]{2,1,0:T(8,128)(2,1)} %get-tuple-element.148), channel_id=1, source_target_pairs={{0,16},{1,17},{2,18},{3,19},{4,20},{5,21},{6,22},{7,23},{8,24},{9,... | collective-permute-start | bytes 786440 | tf_op jit(solution)/shard_map/ppermute | solution.py:802
  92.9 29.5 %collective-permute-start.18 = (bf16[16,192,512]{2,1,0:T(8,128)(2,1)}, bf16[16,192,512]{2,1,0:T(8,128)(2,1)}, u32[]{:S(2)}, u32[]{:S(2)}) collective-permute-start(bf16[16,192,512]{2,1,0:T(8,128)(2,1)} %get-tuple-element.106), channel_id=1, source_target_pairs={{0,1},{1,0},{2,3},{3,2},{4,5},{5,4},{6,7},{7,6},{8,9},{9,8},{10,11... | collective-permute-start | bytes 9437192 | tf_op jit(solution)/shard_map/ppermute | solution.py:764
  126.9 22.4 %collective-permute-start.19 = (bf16[8,192,512]{2,1,0:T(8,128)(2,1)S(1)}, bf16[8,192,512]{2,1,0:T(8,128)(2,1)S(1)}, u32[]{:S(2)}, u32[]{:S(2)}) collective-permute-start(bf16[8,192,512]{2,1,0:T(8,128)(2,1)S(1)} %get-tuple-element.131), channel_id=1, source_target_pairs={{0,2},{1,5},{2,0},{3,7},{4,6},{5,1},{6,4},{7,3},{8,10},{9,13},{10,... | collective-permute-start | bytes 4718600 | tf_op jit(solution)/shard_map/ppermute | solution.py:764
  149.3 4.2 %collective-permute-start.29 = (bf16[16,128,512]{2,1,0:T(8,128)(2,1)S(1)}, bf16[16,128,512]{2,1,0:T(8,128)(2,1)S(1)}, u32[]{:S(2)}, u32[]{:S(2)}) collective-permute-start(bf16[16,128,512]{2,1,0:T(8,128)(2,1)S(1)} %get-tuple-element.121), channel_id=1, source_target_pairs={{0,1},{1,0},{2,3},{3,2},{4,5},{5,4},{6,7},{7,6},{8,9},{9,8},{10,11... | collective-permute-start | bytes 6291464 | tf_op jit(solution)/shard_map/ppermute | solution.py:764
  150.7 17.6 %collective-permute-start.20 = (bf16[4,192,512]{2,1,0:T(8,128)(2,1)S(1)}, bf16[4,192,512]{2,1,0:T(8,128)(2,1)S(1)}, u32[]{:S(2)}, u32[]{:S(2)}) collective-permute-start(bf16[4,192,512]{2,1,0:T(8,128)(2,1)S(1)} %get-tuple-element.135), channel_id=1, source_target_pairs={{0,4},{1,3},{2,6},{3,1},{4,0},{5,7},{6,2},{7,5},{8,12},{9,11},{10,... | collective-permute-start | bytes 2359304 | tf_op jit(solution)/shard_map/ppermute | solution.py:764
  154.2 32.3 %collective-permute-start.30 = (bf16[8,128,512]{2,1,0:T(8,128)(2,1)S(1)}, bf16[8,128,512]{2,1,0:T(8,128)(2,1)S(1)}, u32[]{:S(2)}, u32[]{:S(2)}) collective-permute-start(bf16[8,128,512]{2,1,0:T(8,128)(2,1)S(1)} %get-tuple-element.133), channel_id=1, source_target_pairs={{0,2},{1,5},{2,0},{3,7},{4,6},{5,1},{6,4},{7,3},{8,10},{9,13},{10,... | collective-permute-start | bytes 3145736 | tf_op jit(solution)/shard_map/ppermute | solution.py:764
  168.5 18.5 %collective-permute-start.21 = (bf16[2,192,512]{2,1,0:T(8,128)(2,1)S(1)}, bf16[2,192,512]{2,1,0:T(8,128)(2,1)S(1)}, u32[]{:S(2)}, u32[]{:S(2)}) collective-permute-start(bf16[2,192,512]{2,1,0:T(8,128)(2,1)S(1)} %get-tuple-element.141), channel_id=1, source_target_pairs={{0,8},{1,9},{2,10},{3,11},{4,12},{5,13},{6,14},{7,15},{8,0},{9,1},... | collective-permute-start | bytes 1179656 | tf_op jit(solution)/shard_map/ppermute | solution.py:764
  186.5 25.7 %collective-permute-start.7 = (bf16[16,80,512]{2,1,0:T(8,128)(2,1)}, bf16[16,80,512]{2,1,0:T(8,128)(2,1)S(1)}, u32[]{:S(2)}, u32[]{:S(2)}) collective-permute-start(bf16[16,80,512]{2,1,0:T(8,128)(2,1)} %get-tuple-element.104), channel_id=1, source_target_pairs={{0,1},{1,0},{2,3},{3,2},{4,5},{5,4},{6,7},{7,6},{8,9},{9,8},{10,11... | collective-permute-start | bytes 3932168 | tf_op jit(solution)/shard_map/ppermute | solution.py:764
  186.9 25.3 %copy-start.74 = (bf16[16,80,512]{2,1,0:T(8,128)(2,1)S(1)}, bf16[16,80,512]{2,1,0:T(8,128)(2,1)}, u32[]{:S(2)}) copy-start(bf16[16,80,512]{2,1,0:T(8,128)(2,1)} %get-tuple-element.103) | copy-start | bytes 3932164
  186.9 13.2 %collective-permute-start.31 = (bf16[4,128,512]{2,1,0:T(8,128)(2,1)S(1)}, bf16[4,128,512]{2,1,0:T(8,128)(2,1)S(1)}, u32[]{:S(2)}, u32[]{:S(2)}) collective-permute-start(bf16[4,128,512]{2,1,0:T(8,128)(2,1)S(1)} %get-tuple-element.139), channel_id=1, source_target_pairs={{0,4},{1,3},{2,6},{3,1},{4,0},{5,7},{6,2},{7,5},{8,12},{9,11},{10,... | collective-permute-start | bytes 1572872 | tf_op jit(solution)/shard_map/ppermute | solution.py:764
  187.0 12.9 %collective-permute-start.22 = (bf16[1,192,512]{2,1,0:T(8,128)(2,1)S(1)}, bf16[1,192,512]{2,1,0:T(8,128)(2,1)S(1)}, u32[]{:S(2)}, u32[]{:S(2)}) collective-permute-start(bf16[1,192,512]{2,1,0:T(8,128)(2,1)S(1)} %add_convert_fusion.17), channel_id=1, source_target_pairs={{0,16},{1,17},{2,18},{3,19},{4,20},{5,21},{6,22},{7,23},{8,24},{9,... | collective-permute-start | bytes 589832 | tf_op jit(solution)/shard_map/ppermute | solution.py:764
  200.0 12.1 %collective-permute-start.23 = (bf16[1,192,512]{2,1,0:T(8,128)(2,1)S(1)}, bf16[1,192,512]{2,1,0:T(8,128)(2,1)S(1)}, u32[]{:S(2)}, u32[]{:S(2)}) collective-permute-start(bf16[1,192,512]{2,1,0:T(8,128)(2,1)S(1)} %add_convert_fusion.16), channel_id=1, source_target_pairs={{0,16},{1,17},{2,18},{3,19},{4,20},{5,21},{6,22},{7,23},{8,24},{9,... | collective-permute-start | bytes 589832 | tf_op jit(solution)/shard_map/ppermute | solution.py:764
  200.3 14.0 %collective-permute-start.32 = (bf16[2,128,512]{2,1,0:T(8,128)(2,1)S(1)}, bf16[2,128,512]{2,1,0:T(8,128)(2,1)S(1)}, u32[]{:S(2)}, u32[]{:S(2)}) collective-permute-start(bf16[2,128,512]{2,1,0:T(8,128)(2,1)S(1)} %get-tuple-element.145), channel_id=1, source_target_pairs={{0,8},{1,9},{2,10},{3,11},{4,12},{5,13},{6,14},{7,15},{8,0},{9,1},... | collective-permute-start | bytes 786440 | tf_op jit(solution)/shard_map/ppermute | solution.py:764
  212.1 13.9 %collective-permute-start.24 = (bf16[2,192,512]{2,1,0:T(8,128)(2,1)S(1)}, bf16[2,192,512]{2,1,0:T(8,128)(2,1)S(1)}, u32[]{:S(2)}, u32[]{:S(2)}) collective-permute-start(bf16[2,192,512]{2,1,0:T(8,128)(2,1)S(1)} %pad_maximum_fusion.5), channel_id=1, source_target_pairs={{0,8},{1,9},{2,10},{3,11},{4,12},{5,13},{6,14},{7,15},{8,0},{9,1},... | collective-permute-start | bytes 1179656 | tf_op jit(solution)/shard_map/ppermute | solution.py:764
  212.7 14.6 %collective-permute-start.8 = (bf16[8,80,512]{2,1,0:T(8,128)(2,1)S(1)}, bf16[8,80,512]{2,1,0:T(8,128)(2,1)S(1)}, u32[]{:S(2)}, u32[]{:S(2)}) collective-permute-start(bf16[8,80,512]{2,1,0:T(8,128)(2,1)S(1)} %get-tuple-element.137), channel_id=1, source_target_pairs={{0,2},{1,5},{2,0},{3,7},{4,6},{5,1},{6,4},{7,3},{8,10},{9,13},{10,... | collective-permute-start | bytes 1966088 | tf_op jit(solution)/shard_map/ppermute | solution.py:764
  214.3 11.9 %collective-permute-start.33 = (bf16[1,128,512]{2,1,0:T(8,128)(2,1)S(1)}, bf16[1,128,512]{2,1,0:T(8,128)(2,1)S(1)}, u32[]{:S(2)}, u32[]{:S(2)}) collective-permute-start(bf16[1,128,512]{2,1,0:T(8,128)(2,1)S(1)} %add_convert_fusion.22), channel_id=1, source_target_pairs={{0,16},{1,17},{2,18},{3,19},{4,20},{5,21},{6,22},{7,23},{8,24},{9,... | collective-permute-start | bytes 393224 | tf_op jit(solution)/shard_map/ppermute | solution.py:764
  226.1 12.1 %collective-permute-start.25 = (bf16[4,192,512]{2,1,0:T(8,128)(2,1)S(1)}, bf16[4,192,512]{2,1,0:T(8,128)(2,1)S(1)}, u32[]{:S(2)}, u32[]{:S(2)}) collective-permute-start(bf16[4,192,512]{2,1,0:T(8,128)(2,1)S(1)} %pad_maximum_fusion.2), channel_id=1, source_target_pairs={{0,4},{1,3},{2,6},{3,1},{4,0},{5,7},{6,2},{7,5},{8,12},{9,11},{10,... | collective-permute-start | bytes 2359304 | tf_op jit(solution)/shard_map/ppermute | solution.py:764
  226.3 8.4 %collective-permute-start.34 = (bf16[1,128,512]{2,1,0:T(8,128)(2,1)S(1)}, bf16[1,128,512]{2,1,0:T(8,128)(2,1)S(1)}, u32[]{:S(2)}, u32[]{:S(2)}) collective-permute-start(bf16[1,128,512]{2,1,0:T(8,128)(2,1)S(1)} %add_convert_fusion.21), channel_id=1, source_target_pairs={{0,16},{1,17},{2,18},{3,19},{4,20},{5,21},{6,22},{7,23},{8,24},{9,... | collective-permute-start | bytes 393224 | tf_op jit(solution)/shard_map/ppermute | solution.py:764
  227.5 16.5 %collective-permute-start.9 = (bf16[4,80,512]{2,1,0:T(8,128)(2,1)S(1)}, bf16[4,80,512]{2,1,0:T(8,128)(2,1)S(1)}, u32[]{:S(2)}, u32[]{:S(2)}) collective-permute-start(bf16[4,80,512]{2,1,0:T(8,128)(2,1)S(1)} %get-tuple-element.143), channel_id=1, source_target_pairs={{0,4},{1,3},{2,6},{3,1},{4,0},{5,7},{6,2},{7,5},{8,12},{9,11},{10,... | collective-permute-start | bytes 983048 | tf_op jit(solution)/shard_map/ppermute | solution.py:764
  234.7 9.5 %collective-permute-start.35 = (bf16[2,128,512]{2,1,0:T(8,128)(2,1)S(1)}, bf16[2,128,512]{2,1,0:T(8,128)(2,1)S(1)}, u32[]{:S(2)}, u32[]{:S(2)}) collective-permute-start(bf16[2,128,512]{2,1,0:T(8,128)(2,1)S(1)} %pad_maximum_fusion.7), channel_id=1, source_target_pairs={{0,8},{1,9},{2,10},{3,11},{4,12},{5,13},{6,14},{7,15},{8,0},{9,1},... | collective-permute-start | bytes 786440 | tf_op jit(solution)/shard_map/ppermute | solution.py:764
  238.3 29.8 %collective-permute-start.26 = (bf16[8,192,512]{2,1,0:T(8,128)(2,1)S(1)}, bf16[8,192,512]{2,1,0:T(8,128)(2,1)S(1)}, u32[]{:S(2)}, u32[]{:S(2)}) collective-permute-start(bf16[8,192,512]{2,1,0:T(8,128)(2,1)S(1)} %pad_maximum_fusion.refs_1_), channel_id=1, source_target_pairs={{0,2},{1,5},{2,0},{3,7},{4,6},{5,1},{6,4},{7,3},{8,10},{9,13},{10,... | collective-permute-start | bytes 4718600 | tf_op jit(solution)/shard_map/ppermute | solution.py:764
  244.1 6.3 %collective-permute-start.10 = (bf16[2,80,512]{2,1,0:T(8,128)(2,1)S(1)}, bf16[2,80,512]{2,1,0:T(8,128)(2,1)S(1)}, u32[]{:S(2)}, u32[]{:S(2)}) collective-permute-start(bf16[2,80,512]{2,1,0:T(8,128)(2,1)S(1)} %get-tuple-element.147), channel_id=1, source_target_pairs={{0,8},{1,9},{2,10},{3,11},{4,12},{5,13},{6,14},{7,15},{8,0},{9,1},... | collective-permute-start | bytes 491528 | tf_op jit(solution)/shard_map/ppermute | solution.py:764
  244.3 14.9 %collective-permute-start.36 = (bf16[4,128,512]{2,1,0:T(8,128)(2,1)S(1)}, bf16[4,128,512]{2,1,0:T(8,128)(2,1)S(1)}, u32[]{:S(2)}, u32[]{:S(2)}) collective-permute-start(bf16[4,128,512]{2,1,0:T(8,128)(2,1)S(1)} %pad_maximum_fusion.4), channel_id=1, source_target_pairs={{0,4},{1,3},{2,6},{3,1},{4,0},{5,7},{6,2},{7,5},{8,12},{9,11},{10,... | collective-permute-start | bytes 1572872 | tf_op jit(solution)/shard_map/ppermute | solution.py:764
  250.4 6.4 %collective-permute-start.11 = (bf16[1,80,512]{2,1,0:T(8,128)(2,1)S(1)}, bf16[1,80,512]{2,1,0:T(8,128)(2,1)S(1)}, u32[]{:S(2)}, u32[]{:S(2)}) collective-permute-start(bf16[1,80,512]{2,1,0:T(8,128)(2,1)S(1)} %add_convert_fusion.25), channel_id=1, source_target_pairs={{0,16},{1,17},{2,18},{3,19},{4,20},{5,21},{6,22},{7,23},{8,24},{9,... | collective-permute-start | bytes 245768 | tf_op jit(solution)/shard_map/ppermute | solution.py:764
  256.9 5.7 %collective-permute-start.12 = (bf16[1,80,512]{2,1,0:T(8,128)(2,1)S(1)}, bf16[1,80,512]{2,1,0:T(8,128)(2,1)S(1)}, u32[]{:S(2)}, u32[]{:S(2)}) collective-permute-start(bf16[1,80,512]{2,1,0:T(8,128)(2,1)S(1)} %add_convert_fusion.24), channel_id=1, source_target_pairs={{0,16},{1,17},{2,18},{3,19},{4,20},{5,21},{6,22},{7,23},{8,24},{9,... | collective-permute-start | bytes 245768 | tf_op jit(solution)/shard_map/ppermute | solution.py:764
  256.9 32.5 %collective-permute-start.27 = (bf16[8,192,512]{2,1,0:T(8,128)(2,1)S(1)}, bf16[8,192,512]{2,1,0:T(8,128)(2,1)S(1)}, u32[]{:S(2)}, u32[]{:S(2)}) collective-permute-start(bf16[8,192,512]{2,1,0:T(8,128)(2,1)S(1)} %pad_maximum_fusion.refs_1_), channel_id=1, source_target_pairs={{0,1},{1,0},{2,3},{3,2},{4,5},{5,4},{6,7},{7,6},{8,9},{9,8},{10,11... | collective-permute-start | bytes 4718600 | tf_op jit(solution)/shard_map/ppermute | solution.py:764
  259.3 20.6 %collective-permute-start.37 = (bf16[8,128,512]{2,1,0:T(8,128)(2,1)S(1)}, bf16[8,128,512]{2,1,0:T(8,128)(2,1)S(1)}, u32[]{:S(2)}, u32[]{:S(2)}) collective-permute-start(bf16[8,128,512]{2,1,0:T(8,128)(2,1)S(1)} %pad_maximum_fusion.1.refs_1_), channel_id=1, source_target_pairs={{0,2},{1,5},{2,0},{3,7},{4,6},{5,1},{6,4},{7,3},{8,10},{9,13},{10,... | collective-permute-start | bytes 3145736 | tf_op jit(solution)/shard_map/ppermute | solution.py:764
  262.6 5.4 %collective-permute-start.13 = (bf16[2,80,512]{2,1,0:T(8,128)(2,1)S(1)}, bf16[2,80,512]{2,1,0:T(8,128)(2,1)S(1)}, u32[]{:S(2)}, u32[]{:S(2)}) collective-permute-start(bf16[2,80,512]{2,1,0:T(8,128)(2,1)S(1)} %pad_maximum_fusion.8), channel_id=1, source_target_pairs={{0,8},{1,9},{2,10},{3,11},{4,12},{5,13},{6,14},{7,15},{8,0},{9,1},... | collective-permute-start | bytes 491528 | tf_op jit(solution)/shard_map/ppermute | solution.py:764
  268.0 10.7 %collective-permute-start.14 = (bf16[4,80,512]{2,1,0:T(8,128)(2,1)S(1)}, bf16[4,80,512]{2,1,0:T(8,128)(2,1)S(1)}, u32[]{:S(2)}, u32[]{:S(2)}) collective-permute-start(bf16[4,80,512]{2,1,0:T(8,128)(2,1)S(1)} %pad_maximum_fusion.6), channel_id=1, source_target_pairs={{0,4},{1,3},{2,6},{3,1},{4,0},{5,7},{6,2},{7,5},{8,12},{9,11},{10,... | collective-permute-start | bytes 983048 | tf_op jit(solution)/shard_map/ppermute | solution.py:764
  268.1 22.5 %collective-permute-start.28 = (bf16[8,192,512]{2,1,0:T(8,128)(2,1)S(1)}, bf16[8,192,512]{2,1,0:T(8,128)(2,1)S(1)}, u32[]{:S(2)}, u32[]{:S(2)}) collective-permute-start(bf16[8,192,512]{2,1,0:T(8,128)(2,1)S(1)} %collective-permute-done.26.refs_2_), channel_id=1, source_target_pairs={{0,1},{1,0},{2,3},{3,2},{4,5},{5,4},{6,7},{7,6},{8,9},{9,8},{10,11... | collective-permute-start | bytes 4718600 | tf_op jit(solution)/shard_map/ppermute | solution.py:764
  278.8 10.7 %collective-permute-start.15 = (bf16[8,80,512]{2,1,0:T(8,128)(2,1)S(1)}, bf16[8,80,512]{2,1,0:T(8,128)(2,1)S(1)}, u32[]{:S(2)}, u32[]{:S(2)}) collective-permute-start(bf16[8,80,512]{2,1,0:T(8,128)(2,1)S(1)} %pad_maximum_fusion.3.refs_1_), channel_id=1, source_target_pairs={{0,2},{1,5},{2,0},{3,7},{4,6},{5,1},{6,4},{7,3},{8,10},{9,13},{10,... | collective-permute-start | bytes 1966088 | tf_op jit(solution)/shard_map/ppermute | solution.py:764
  279.8 15.9 %collective-permute-start.38 = (bf16[8,128,512]{2,1,0:T(8,128)(2,1)S(1)}, bf16[8,128,512]{2,1,0:T(8,128)(2,1)S(1)}, u32[]{:S(2)}, u32[]{:S(2)}) collective-permute-start(bf16[8,128,512]{2,1,0:T(8,128)(2,1)S(1)} %pad_maximum_fusion.1.refs_1_), channel_id=1, source_target_pairs={{0,1},{1,0},{2,3},{3,2},{4,5},{5,4},{6,7},{7,6},{8,9},{9,8},{10,11... | collective-permute-start | bytes 3145736 | tf_op jit(solution)/shard_map/ppermute | solution.py:764
  279.9 15.9 %collective-permute-start.39 = (bf16[8,128,512]{2,1,0:T(8,128)(2,1)S(1)}, bf16[8,128,512]{2,1,0:T(8,128)(2,1)S(1)}, u32[]{:S(2)}, u32[]{:S(2)}) collective-permute-start(bf16[8,128,512]{2,1,0:T(8,128)(2,1)S(1)} %collective-permute-done.37.refs_2_), channel_id=1, source_target_pairs={{0,1},{1,0},{2,3},{3,2},{4,5},{5,4},{6,7},{7,6},{8,9},{9,8},{10,11... | collective-permute-start | bytes 3145736 | tf_op jit(solution)/shard_map/ppermute | solution.py:764
  289.5 10.1 %collective-permute-start.16 = (bf16[8,80,512]{2,1,0:T(8,128)(2,1)S(1)}, bf16[8,80,512]{2,1,0:T(8,128)(2,1)S(1)}, u32[]{:S(2)}, u32[]{:S(2)}) collective-permute-start(bf16[8,80,512]{2,1,0:T(8,128)(2,1)S(1)} %pad_maximum_fusion.3.refs_1_), channel_id=1, source_target_pairs={{0,1},{1,0},{2,3},{3,2},{4,5},{5,4},{6,7},{7,6},{8,9},{9,8},{10,11... | collective-permute-start | bytes 1966088 | tf_op jit(solution)/shard_map/ppermute | solution.py:764
  289.5 10.1 %collective-permute-start.17 = (bf16[8,80,512]{2,1,0:T(8,128)(2,1)S(1)}, bf16[8,80,512]{2,1,0:T(8,128)(2,1)S(1)}, u32[]{:S(2)}, u32[]{:S(2)}) collective-permute-start(bf16[8,80,512]{2,1,0:T(8,128)(2,1)S(1)} %collective-permute-done.15.refs_2_), channel_id=1, source_target_pairs={{0,1},{1,0},{2,3},{3,2},{4,5},{5,4},{6,7},{7,6},{8,9},{9,8},{10,11... | collective-permute-start | bytes 1966088 | tf_op jit(solution)/shard_map/ppermute | solution.py:764
  (67 other events, 320.7 us)

commit v2 on v1

v2 whole, which is shorter than its diff:
```python
import functools

import jax
import jax.numpy as jnp
import numpy as np
from jax import lax
from jax.experimental import pallas as pl
from jax.experimental.pallas import tpu as pltpu
from jax.sharding import PartitionSpec as P

HEADS = 8
HS = 64
EPS = 1e-06
F32 = jnp.float32
B16 = jnp.bfloat16
I32 = jnp.int32
HIGH = lax.Precision.HIGHEST
AXES = ("dp", "rep")
SCALE = 0.125
MIB = 1 << 20
FAR = -3e38
ANY = pl.BlockSpec(memory_space=pl.ANY)
SMEM = pl.BlockSpec(memory_space=pltpu.SMEM)
VMEM = pl.BlockSpec(memory_space=pltpu.VMEM)
SMALL = ("b_query", "b_value", "b_out", "gain_one", "shift_one", "b_down", "gain_two", "shift_two")
NSMALL = 12


def dot(a, b):
    return lax.dot_general(a, b, (((1,), (0,)), ((), ())), preferred_element_type=F32)


def dot_nt(a, b):
    return lax.dot_general(a, b, (((1,), (1,)), ((), ())), preferred_element_type=F32)


def dot_tn(a, b):
    return lax.dot_general(a, b, (((0,), (0,)), ((), ())), preferred_element_type=F32)


def dot_high(a, b):
    return lax.dot_general(
        a, b, (((1,), (0,)), ((), ())), precision=HIGH, preferred_element_type=F32
    )


def centred(v):
    c = v - jnp.mean(v, -1, keepdims=True)
    r = lax.rsqrt(jnp.mean(c * c, -1, keepdims=True) + EPS)
    return c * r, r


def norm_back(hat, r, gain, d_out):
    g_gain = jnp.sum(d_out * hat, 0, keepdims=True)
    g_shift = jnp.sum(d_out, 0, keepdims=True)
    d_hat = d_out * gain
    mean_a = jnp.mean(d_hat, -1, keepdims=True)
    mean_b = jnp.mean(d_hat * hat, -1, keepdims=True)
    return r * (d_hat - mean_a - hat * mean_b), g_gain, g_shift


def gelu_pair(x):
    phi = 0.5 + 0.5 * lax.erf(x * 0.7071067811865476)
    return x * phi, phi + x * (jnp.exp(x * x * -0.5) * 0.3989422804014327)


def stacked(x, group):
    lane = lax.broadcasted_iota(I32, x.shape, 1) // HS
    zero = jnp.zeros_like(x)
    return jnp.concatenate([jnp.where(lane == g, x, zero) for g in range(group)], 0)


def diagonal(o, group):
    rows = o.shape[0] // group
    lane = lax.broadcasted_iota(I32, (rows, o.shape[1]), 1) // HS
    out = o[:rows]
    for g in range(1, group):
        out = jnp.where(lane == g, o[g * rows : (g + 1) * rows], out)
    return out


def softmax(s):
    e = jnp.exp(s - jnp.max(s, -1, keepdims=True))
    return e * (1.0 / jnp.sum(e, -1, keepdims=True))


def attend(q, k, v, group, keep_probs, length=None):
    wide = HS * group
    parts = []
    for t in range(HEADS // group):
        at = slice(t * wide, (t + 1) * wide)
        scores = dot_nt(stacked(q[:, at], group), k[:, at])
        if length:
            rows = lax.broadcasted_iota(I32, scores.shape, 0) % q.shape[0]
            apart = rows // length != lax.broadcasted_iota(I32, scores.shape, 1) // length
            scores = jnp.where(apart, FAR, scores)
        probs = softmax(scores).astype(B16)
        keep_probs(t, probs)
        parts.append(diagonal(dot(probs, v[:, at]), group))
    return jnp.concatenate(parts, 1).astype(B16)


def attend_back(q, k, v, d_att, group, probs_of):
    wide = HS * group
    dq, dk, dv = [], [], []
    for t in range(HEADS // group):
        at = slice(t * wide, (t + 1) * wide)
        probs = probs_of(t)
        d_stack = stacked(d_att[:, at], group)
        d_probs = dot_nt(d_stack, v[:, at])
        dv.append(dot_tn(probs, d_stack))
        p32 = probs.astype(F32)
        inside = jnp.sum(p32 * d_probs, -1, keepdims=True)
        d_scores = (p32 * (d_probs - inside)).astype(B16)
        dq.append(diagonal(dot(d_scores, k[:, at]), group) * SCALE)
        dk.append(dot_tn(d_scores, stacked(q[:, at], group)))
    return tuple(jnp.concatenate(x, 1).astype(B16) for x in (dq, dk, dv))


def feed(first, w_up, b_up, w_down, b_down, gain, shift, keep, tile=512):
    hat, r = centred(first)
    normed = hat * gain + shift
    low = normed.astype(B16)
    second = normed + b_down
    for j in range(w_up.shape[1] // tile):
        at = slice(j * tile, (j + 1) * tile)
        act, slope = gelu_pair(dot(low, w_up[:, at]) + b_up[:, at])
        act = act.astype(B16)
        keep(at, act, slope)
        second = second + dot(act, w_down[at, :])
    return second, hat, r, low


def feed_both(first, w_up, b_up, w_down, b_down, g1, s1, g2, s2, d_out, slopes, keep_act, keep_inner):
    def keep(at, act, slope):
        keep_act(at, act)
        slopes[:, at] = slope

    ff = w_up.shape[1]
    second, hat, r, low = feed(first, w_up, b_up, w_down, b_down, g1, s1, keep, ff)
    hat2, r2 = centred(second)
    out = (hat2 * g2 + s2).astype(B16)
    d_second, gg2, gs2 = norm_back(hat2, r2, g2, d_out)
    d_down = d_second.astype(B16)
    gb_down = jnp.sum(d_down.astype(F32), 0, keepdims=True)
    d = (dot_nt(d_down, w_down[...]) * slopes[...]).astype(B16)
    keep_inner(slice(0, ff), d)
    gb_up = jnp.sum(d.astype(F32), 0, keepdims=True)
    gb_up = [gb_up[:, j * 512 : (j + 1) * 512] for j in range(ff // 512)]
    d_normed = d_second + dot_nt(d, w_up[...])
    d_first, gg1, gs1 = norm_back(hat, r, g1, d_normed)
    return out, d_down, d_first, low, (gg1, gs1, gb_down, gg2, gs2, *gb_up)


def cls_rows(q, k, v, count):
    total, width = q.shape
    length = total // count
    rows = count * HEADS
    own = (
        lax.broadcasted_iota(I32, (rows, width), 1) // HS
        == lax.broadcasted_iota(I32, (rows, width), 0) % HEADS
    )
    first = [
        jnp.broadcast_to(q[i * length : i * length + 1, :].astype(F32), (HEADS, width))
        for i in range(count)
    ]
    q_rows = jnp.where(own, jnp.concatenate(first, 0), 0.0).astype(B16)
    scores = dot_nt(q_rows, k[...])
    apart = (
        lax.broadcasted_iota(I32, scores.shape, 0) // HEADS
        != lax.broadcasted_iota(I32, scores.shape, 1) // length
    )
    probs = softmax(jnp.where(apart, FAR, scores)).astype(B16)
    mixed = jnp.where(own, dot(probs, v[...]), 0.0)
    return jnp.concatenate(
        [
            jnp.sum(mixed[i * HEADS : (i + 1) * HEADS], 0, keepdims=True)
            for i in range(count)
        ],
        0,
    )


def row(ref, e):
    return ref[e : e + 1, :]


def front_kernel(
    positives, counts, bq, bv, bo, g1, s1, bu, bd, g2, s2, p_x, q_x, wq, wk, wv, wo, wu, wd,
    pq, pk, pv, qq, qk, qv, payload,
    p_s, q_s, wqkv_s, wo_s, wu_s, wd_s, p_out, q_out, pay_s, sems, out_sems,
):
    width = q_x.shape[1]
    count = 4

    def load(i, src, dst):
        return pltpu.make_async_copy(src, dst, sems.at[i])

    w_in = (wq, wk, wv)
    first_in = [load(0, p_x, p_s)]
    first_in += [load(1 + i, w.at[1], wqkv_s.at[1, i]) for i, w in enumerate(w_in)]
    q_in = [load(4, q_x, q_s)]
    q_in += [load(5 + i, w.at[0], wqkv_s.at[0, i]) for i, w in enumerate(w_in)]
    later = [load(8, wo, wo_s), load(9, wu, wu_s), load(10, wd, wd_s)]
    for c in first_in + q_in + later:
        c.start()

    def project(x, e, held, targets):
        copies = []
        for i, (bias, target) in enumerate(zip((bq, None, bv), targets)):
            y = dot(x[...], wqkv_s[e, i])
            y = (y if bias is None else y + row(bias, e)).astype(B16)
            held[i] = y * SCALE if i == 0 else y
            copies.append(pltpu.make_async_copy(held.at[i], target, out_sems.at[3 * e + i]))
            copies[-1].start()
        return copies

    for c in first_in:
        c.wait()
    out = project(p_s, 1, p_out, (pq, pk, pv))
    for c in q_in:
        c.wait()
    out += project(q_s, 0, q_out, (qq, qk, qv))

    pay_s[...] = jnp.zeros_like(pay_s)
    lanes = lax.broadcasted_iota(I32, (1, width), 1)
    for i in range(count):
        mask = jnp.zeros((1, width), F32)
        for j in range(positives.shape[1]):
            mask = jnp.where((lanes == positives[i, j]) & (j < counts[i]), 1.0, mask)
        pay_s[8 + i : 9 + i, :] = mask
    att = [cls_rows(held.at[0], held.at[1], held.at[2], count) for held in (p_out, q_out)]
    for c in later:
        c.wait()
    for e, start, mixed, x in ((1, 0, att[0], p_s), (0, 4, att[1], q_s)):
        length = x.shape[0] // count
        own = [x[i * length : i * length + 1, :].astype(F32) for i in range(count)]
        zero = [jnp.zeros((4, width), F32)]
        mixed = jnp.concatenate([mixed] + zero, 0).astype(B16)
        first = jnp.concatenate(own + zero, 0) + dot(mixed, wo_s[e]) + row(bo, e)
        second, _, _, _ = feed(
            first, wu_s.at[e], row(bu, e), wd_s.at[e], row(bd, e), row(g1, e), row(s1, e),
            lambda at, act, slope: None, 2048,
        )
        done = centred(second)[0] * row(g2, e) + row(s2, e)
        pay_s[start : start + 4, :] = done[:4]
    payload[...] = pay_s[...].astype(B16)
    for c in out:
        c.wait()


def passage_attention_kernel(q, k, v, x, bo, wo, probs, att, first, wo_s, sem):
    copy = pltpu.make_async_copy(wo.at[1], wo_s, sem)

    @pl.when(pl.program_id(0) == 0)
    def _():
        copy.start()

    def keep_probs(t, value):
        probs[t] = value

    a = attend(q[...], k[...], v[...], 4, keep_probs)
    att[...] = a

    @pl.when(pl.program_id(0) == 0)
    def _():
        copy.wait()

    first[...] = x[...].astype(F32) + dot(a, wo_s[...]) + row(bo, 1)


def question_attention_kernel(length, q, k, v, x, bo, wo, probs, att, first):
    def keep_probs(t, value):
        probs[t] = value

    a = attend(q[...], k[...], v[...], 4, keep_probs, length)
    att[...] = a
    first[...] = x[...].astype(F32) + dot(a, wo[...]) + row(bo, 0)


def send_unit(wide, grads, table, keep, send, offset, sem_keep, sem_send):
    half, _, width = keep.shape
    blocks = 2 * half
    rows = grads.shape[0] * grads.shape[1] // (width * blocks)
    across = grads.shape[1] // width

    def start(out, base, sem):
        def body(r, carry):
            c = table[base + r]
            src = grads.at[
                pl.ds(pl.multiple_of(c // across * rows, rows), rows),
                pl.ds(pl.multiple_of(c % across * width, width), width),
            ] if wide else grads.at[pl.ds(pl.multiple_of(c * rows, rows), rows), :]
            pltpu.make_async_copy(src, out.at[r, pl.ds(offset, rows), :], sem).start()
            return carry

        lax.fori_loop(0, half, body, 0)

    start(send, half, sem_send)
    start(keep, 0, sem_keep)


def wait_units(keep, send, sem_keep, sem_send):
    pltpu.make_async_copy(send, send, sem_send).wait()
    pltpu.make_async_copy(keep, keep, sem_keep).wait()


def contrast(gathered, me, scale):
    z = jnp.concatenate([g[...] for g in gathered], 0)
    n = z.shape[0] // 16
    total_rows = 4 * n
    base = me * 4
    place = lax.broadcasted_iota(I32, (total_rows, z.shape[0]), 1)
    index = lax.broadcasted_iota(I32, (total_rows, z.shape[0]), 0)
    apart = (index // 4) ^ me
    block = jnp.zeros_like(apart)
    depth = n.bit_length() - 1
    for i in range(depth):
        block = block + (((apart >> i) & 1) << (depth - 1 - i))
    sel = block * 16 + index % 4

    def rows_at(k):
        return dot(jnp.where(place == sel + k, 1.0, 0.0).astype(B16), z)

    all_p, all_q, mask = rows_at(0), rows_at(4), rows_at(8)[:, :total_rows]
    sim = dot_nt(all_q.astype(B16), all_p.astype(B16)) * scale
    expo = jnp.exp(sim - jnp.max(sim, -1, keepdims=True))
    total = jnp.sum(expo, -1, keepdims=True)
    hit = mask * expo
    pos_total = jnp.sum(hit, -1, keepdims=True)
    terms = jnp.log(total) - jnp.log(pos_total)
    coeff = expo / total - hit / pos_total
    mine = jnp.where(
        lax.broadcasted_iota(I32, (8, total_rows), 1)
        == base + lax.broadcasted_iota(I32, (8, total_rows), 0),
        1.0,
        0.0,
    )
    d_q = dot_high(dot_high(mine, coeff), all_p) * scale
    d_p = dot_high(dot_high(mine, coeff.T), all_q) * scale
    return dot_high(mine, jnp.broadcast_to(terms, (total_rows, 128))), d_q, d_p


def question_back_kernel(
    table, gathered_a, gathered_b, x, cot, q, k, v, probs, att, first,
    g1, s1, bu, bd, g2, s2, wq, wk, wv, wo, wu, wd,
    terms, d_cls_p, x_grad, small, out, keep, send,
    wqkv_s, wo_s, wu_s, wd_s, act_s, slope_s, inner_s, g_down, g_up, g_att, sems, out_sems,
):
    copies = [
        pltpu.make_async_copy(src.at[0], dst, sems.at[i])
        for i, (src, dst) in enumerate(
            (
                (wu, wu_s),
                (wd, wd_s),
                (wo, wo_s),
                (wq, wqkv_s.at[0]),
                (wk, wqkv_s.at[1]),
                (wv, wqkv_s.at[2]),
            )
        )
    ]
    for c in copies:
        c.start()
    n = keep.shape[0] * 2
    rows = 2048 // n
    count = 4
    length = x.shape[0] // count
    width = x.shape[1]
    loss, d_q, d_p = contrast(
        (gathered_a, gathered_b), table[n], 2.0 / float(np.sqrt(width))
    )
    terms[...] = loss
    d_cls_p[...] = d_p
    place = lax.broadcasted_iota(I32, x.shape, 0)
    d_out = cot[...].astype(F32)
    for i in range(count):
        d_out = d_out + jnp.where(place == i * length, d_q[i : i + 1], 0.0)
    for c in copies[:2]:
        c.wait()

    def keep_act(at, value):
        act_s[:, at] = value

    def keep_inner(at, value):
        inner_s[:, at] = value

    out[...], d_down, d_first, low, sums = feed_both(
        first[...], wu_s, row(bu, 0), wd_s, row(bd, 0), row(g1, 0), row(s1, 0), row(g2, 0),
        row(s2, 0), d_out, slope_s, keep_act, keep_inner,
    )
    sems_out = (out_sems.at[0], out_sems.at[1])
    g_down[...] = dot_tn(act_s[...], d_down).astype(B16)
    send_unit(False, g_down, table, keep, send, 0, *sems_out)
    g_up[...] = dot_tn(low, inner_s[...]).astype(B16)
    send_unit(True, g_up, table, keep, send, rows, *sems_out)
    for c in copies[2:]:
        c.wait()
    d_branch = d_first.astype(B16)
    d_att = dot_nt(d_branch, wo_s[...]).astype(B16)
    dq, dk, dv = attend_back(q[...], k[...], v[...], d_att, 4, lambda t: probs[t])
    rows_x = x[...]
    for i, d in enumerate((dq, dk, dv)):
        g_att[i * width : (i + 1) * width, :] = dot_tn(rows_x, d).astype(B16)
    g_att[3 * width :, :] = dot_tn(att[...], d_branch).astype(B16)
    send_unit(False, g_att, table, keep, send, 2 * rows, *sems_out)
    x_grad[...] = (
        d_first + dot_nt(dq, wqkv_s[0]) + dot_nt(dk, wqkv_s[1]) + dot_nt(dv, wqkv_s[2])
    )
    small[...] = jnp.zeros_like(small)
    values = [jnp.sum(d.astype(F32), 0, keepdims=True) for d in (dq, dv, d_branch)]
    for i, value in enumerate((*values, *sums)):
        small[i : i + 1, :] = value
    wait_units(keep, send, *sems_out)


def passage_feed_kernel(
    steps, table, d_cls, cot, first, g1, s1, bu, bd, g2, s2, wu, wd,
    out, d_first, small, keep, send,
    wu_s, wd_s, slope_s, act_s, inner_s, down_s, low_s, g_down, g_up, sems, out_sems,
):
    b = pl.program_id(0)
    sems_out = (out_sems.at[0], out_sems.at[1])
    rows = 2048 // (2 * keep.shape[0])
    total_rows = act_s.shape[0]
    per = 4 // steps

    @pl.when(b < steps)
    def _():
        copies = [
            pltpu.make_async_copy(src, dst, sems.at[i])
            for i, (src, dst) in enumerate(((wu.at[1], wu_s), (wd.at[1], wd_s)))
        ]

        @pl.when(b == 0)
        def _():
            for c in copies:
                c.start()
            small[...] = jnp.zeros_like(small)
            for c in copies:
                c.wait()

        place = lax.broadcasted_iota(I32, cot.shape, 0)
        d_out = cot[...].astype(F32)
        for i in range(per):
            mine = d_cls[pl.ds(b * per + i, 1), :]
            d_out = d_out + jnp.where(place == i * (cot.shape[0] // per), mine, 0.0)
        mine = pl.ds(pl.multiple_of(b * cot.shape[0], cot.shape[0]), cot.shape[0])

        def keep_act(at, value):
            act_s[mine, at] = value

        def keep_inner(at, value):
            inner_s[mine, at] = value

        out[...], down_s[mine, :], d_first[...], low_s[mine, :], sums = feed_both(
            first[...], wu_s, row(bu, 1), wd_s, row(bd, 1), row(g1, 1), row(s1, 1), row(g2, 1),
            row(s2, 1), d_out, slope_s, keep_act, keep_inner,
        )
        for i, value in enumerate(sums):
            small[3 + i : 4 + i, :] += value

    @pl.when(b == steps)
    def _():
        g_down[...] = dot_tn(act_s[...], down_s[...]).astype(B16)
        send_unit(False, g_down, table, keep, send, 0, *sems_out)

    @pl.when(b == steps + 1)
    def _():
        g_up[...] = dot_tn(low_s[...], inner_s[...]).astype(B16)
        send_unit(True, g_up, table, keep, send, rows, *sems_out)
        wait_units(keep, send, *sems_out)


def passage_attention_back_kernel(
    table, small_q, small_p, d_first, q, k, v, probs, x, att, wq, wk, wv, wo,
    x_grad, keep, send,
    wqkv_s, wo_s, x_s, att_s, d_s, small, sent_s, g_att, sems, out_sems,
):
    b = pl.program_id(0)
    nb = pl.num_programs(0)
    length, width = d_first.shape
    n = 2 * keep.shape[0]
    rows = 2048 // n
    copies = [
        pltpu.make_async_copy(src, dst, sems.at[i])
        for i, (src, dst) in enumerate(
            (
                (wo.at[1], wo_s),
                (wq.at[1], wqkv_s.at[0]),
                (wk.at[1], wqkv_s.at[1]),
                (wv.at[1], wqkv_s.at[2]),
                (x, x_s),
                (att, att_s),
            )
        )
    ]

    @pl.when(b == 0)
    def _():
        for c in copies:
            c.start()
        small[...] = small_p[...]
        for c in copies[:4]:
            c.wait()

    d_branch = d_first[...].astype(B16)
    d_att = dot_nt(d_branch, wo_s[...]).astype(B16)
    dq, dk, dv = attend_back(q[...], k[...], v[...], d_att, 4, lambda t: probs[t])
    mine = pl.ds(pl.multiple_of(b * length, length), length)
    for i, d in enumerate((dq, dk, dv, d_branch)):
        d_s[i, mine, :] = d
    for i, d in enumerate((dq, dv, d_branch)):
        small[i : i + 1, :] += jnp.sum(d.astype(F32), 0, keepdims=True)
    x_grad[...] = (
        d_first[...] + dot_nt(dq, wqkv_s[0]) + dot_nt(dk, wqkv_s[1]) + dot_nt(dv, wqkv_s[2])
    )

    @pl.when(b == nb - 1)
    def _():
        sent_s[...] = jnp.zeros_like(sent_s)
        top = lax.broadcasted_iota(I32, (16, width), 0) == 0
        for e, ref in enumerate((small_q, small)):
            for i in range(NSMALL):
                sent_s[e * NSMALL + i] = jnp.where(top, ref[i : i + 1, :], 0.0).astype(B16)
        for base, out, sem in ((n // 2, send, out_sems.at[1]), (0, keep, out_sems.at[0])):

            def body(r, carry, base=base, out=out, sem=sem):
                pltpu.make_async_copy(
                    sent_s.at[table[base + r]], out.at[r, pl.ds(rows, 16), :], sem
                ).start()
                return carry

            lax.fori_loop(0, n // 2, body, 0)
        for c in copies[4:]:
            c.wait()
        for i in range(3):
            g_att[i * width : (i + 1) * width, :] = dot_tn(x_s[...], d_s[i]).astype(B16)
        g_att[3 * width :, :] = dot_tn(att_s[...], d_s[3]).astype(B16)
        send_unit(False, g_att, table, keep, send, 0, out_sems.at[0], out_sems.at[1])
        wait_units(keep, send, out_sems.at[0], out_sems.at[1])


def place_kernel(e, kinds, starts, n_alias, with_small, *refs):
    table = refs[0]
    pieces = refs[1 : 1 + len(starts)]
    outs = refs[1 + len(starts) + n_alias :]
    n_out = sum(4 if kind == "att" else 1 for kind in kinds)
    n_small = 9 if with_small else 0
    targets, smalls = outs[:n_out], outs[n_out : n_out + n_small]
    scratch = outs[n_out + n_small :]
    stages, sems = scratch[: len(kinds)], scratch[len(kinds)]
    small_s = scratch[len(kinds) + 1] if with_small else None
    n = starts[-1] + pieces[-1].shape[0]
    rows = 2048 // n
    for piece, start in zip(pieces, starts):

        def body(r, carry, piece=piece, start=start):
            c = table[start + r]
            k = 0
            for u, kind in enumerate(kinds):
                stage = stages[u].at[start + r]
                stage[...] = piece[r, u * rows : (u + 1) * rows, :].astype(F32)
                if kind == "down":
                    pltpu.make_async_copy(
                        stage,
                        targets[k].at[e, pl.ds(pl.multiple_of(c * rows, rows), rows), :],
                        sems.at[k],
                    ).start()
                    k += 1
                elif kind == "up":
                    pltpu.make_async_copy(
                        stage,
                        targets[k].at[
                            e,
                            pl.ds(pl.multiple_of(c // 4 * rows, rows), rows),
                            pl.ds(pl.multiple_of(c % 4 * 512, 512), 512),
                        ],
                        sems.at[k],
                    ).start()
                    k += 1
                else:
                    quarter = n // 4
                    for m in range(4):

                        @pl.when(c // quarter == m)
                        def _(m=m, k=k, stage=stage):
                            at = pl.ds(pl.multiple_of(c % quarter * rows, rows), rows)
                            pltpu.make_async_copy(
                                stage, targets[k + m].at[e, at, :], sems.at[k + m]
                            ).start()

                    k += 4
            if with_small:
                block = piece[r, len(kinds) * rows : len(kinds) * rows + 16, :].astype(F32)
                small_s[c] = block[0:8]
            return carry

        lax.fori_loop(0, piece.shape[0], body, 0)
    if with_small:
        for f in range(2):
            for i in range(8):
                smalls[i][f : f + 1, :] = small_s[f * NSMALL + i, 0:1, :]
            for j in range(4):
                smalls[8][f : f + 1, j * 512 : (j + 1) * 512] = small_s[f * NSMALL + 8 + j, 0:1, :]
    for k, target in enumerate(targets):
        pltpu.make_async_copy(target.at[e], target.at[e], sems.at[k]).wait()


def rounds_of(mesh_shape):
    dp, rep = mesh_shape["dp"], mesh_shape["rep"]
    core, *x = [1 << i for i in range(rep.bit_length() - 1)]
    y, *z = [rep << i for i in range(dp.bit_length() - 1)]
    return [core, *x, y, *z], [core, y, *x, *z]


def order_table(rounds, n):
    depth = len(rounds[0])
    table = np.zeros((n, n), np.int32)
    for d in range(n):
        for r in range(n):
            c = d ^ (rounds[0][0] if r >> (depth - 1) & 1 else 0)
            for k in range(1, depth):
                if r >> (depth - 1 - k) & 1:
                    c ^= rounds[c & 1][k]
            table[d, r] = c
    return table


def exchange(x, masks, n):
    return lax.ppermute(x, AXES, [(d, d ^ masks[d & 1]) for d in range(n)])


def total(parts):
    return sum(p.astype(F32) for p in parts).astype(B16)


def steps_of(rounds, pairs):
    even, odd = rounds
    steps, k = [], 0
    while k < len(even):
        if even[k] in pairs:
            steps.append(((even[k], odd[k]), (even[k + 1], odd[k + 1])))
            k += 2
        else:
            steps.append(((even[k], odd[k]),))
            k += 1
    return steps


def partners(step):
    if len(step) == 1:
        return [step[0]]
    high, low = step
    return [low, high, (low[0] ^ high[0], low[1] ^ high[1])]


def join_kernel(*refs):
    *parts, out = refs
    m = parts[0].shape[0]
    for i, part in enumerate(parts):
        out[i * m : (i + 1) * m] = part[...]


class Order:
    def __init__(self):
        self.token = None

    def fence(self, arrays):
        *arrays, self.token = lax.optimization_barrier((*arrays, self.token))
        return arrays

    def __call__(self, kernel, *operands, in_specs, out_specs, out_shape, **kwargs):
        skip = 0 if self.token is None else 1
        last = skip + len(operands) + len(out_shape)

        def body(*refs):
            kernel(*refs[skip:last], *refs[last + 1 :])

        aliases = kwargs.pop("input_output_aliases", {})
        call = pl.pallas_call(
            body,
            in_specs=[ANY] * skip + in_specs,
            out_specs=list(out_specs) + [ANY],
            out_shape=list(out_shape) + [shape((8, 128))],
            input_output_aliases={k + skip: v for k, v in aliases.items()},
            **kwargs,
        )
        *outs, self.token = call(*([self.token] if skip else []), *operands)
        return outs


class Sum:
    def __init__(self, order, halving, doubling, n, keep, send):
        self.order, self.n = order, n
        self.halving, self.doubling = list(halving), list(doubling)
        self.parts, self.m, self.pieces = [keep], keep.shape[0], None
        self.got, self.out, self.now = None, [send], self.halving.pop(0)

    def start(self):
        masks = partners(self.now)
        if self.pieces is None:
            self.got = [exchange(x, m, self.n) for x, m in zip(self.out, masks)]
        else:
            self.got = [exchange(x, m, self.n) for m in masks for x in self.out]

    def take(self):
        if self.pieces is None:
            self.parts += self.got
            if self.halving:
                self.now = self.halving.pop(0)
                ways = 2 ** len(self.now)
                q = self.m // ways
                self.out = [
                    total([p[i * q : (i + 1) * q] for p in self.parts]) for i in range(1, ways)
                ]
                self.m = q
                return True
            self.out = self.pieces = [total([p[:1] for p in self.parts])]
        else:
            self.pieces = self.pieces + self.got
            if not self.doubling:
                return False
            if len(self.doubling) > 1:
                self.pieces = [jnp.concatenate(self.pieces, 0)]
            self.out = self.pieces
        self.now = self.doubling.pop()
        return True


def tail_order(sums, ready):
    unit, x_y, z = 23.3, "xy", "z"

    def durations(item, units):
        left = []
        size = item.m / item.n
        for step in item.halving:
            size /= 2 ** len(step)
            left.append((z, 4 * size) if len(step) == 2 else (x_y, size))
        size = 1 / item.n
        for step in reversed(item.doubling):
            left.append((z, 4 * size) if len(step) == 2 else (x_y, size))
            size *= 2 ** len(step)
        left[-1] = ("core", left[-1][1] / 3)
        return [(kind, d * units * unit) for kind, d in left]

    todo = {k: durations(*v) for k, v in sums.items()}
    done_at = dict(ready)
    busy = {x_y: 0.0, z: 0.0, "core": 0.0}
    now, order = 0.0, []
    going = set(todo)
    while going:
        here = [k for k in going if done_at[k] <= now]
        if not here:
            now = min(done_at[k] for k in going)
            continue
        k = max(here, key=lambda k: sum(d for _, d in todo[k]) + 3 * len(todo[k]))
        order.append(k)
        if not todo[k]:
            going.remove(k)
            continue
        kind, d = todo[k].pop(0)
        now += 5.0 if kind == z else 3.0
        start = max(now, busy[kind])
        busy[kind] = done_at[k] = start + d
    return order


def advance(order, sums, starting=()):
    flat = [x for s in sums for x in s.got]
    if flat:
        flat = order.fence(flat)
    for s in sums:
        s.got, flat = flat[: len(s.got)], flat[len(s.got) :]
    for s in sums:
        s.going = s.take()
    going = [s for s in sums if s.going] + list(starting)
    if not going:
        return
    flat = order.fence([x for s in going for x in s.out])
    for s in going:
        s.out, flat = flat[: len(s.out)], flat[len(s.out) :]
        if s.pieces is not None:
            s.pieces = s.out
        s.start()


class Gather:
    def __init__(self, order, x, n):
        bits = [1 << i for i in reversed(range(n.bit_length() - 1))]
        assert len(bits) % 2 == 1
        self.order, self.n = order, n
        self.stages = [bits[i : i + 2] for i in range(0, len(bits), 2)]
        self.pieces = [x[None]]
        self.issue()

    def issue(self):
        (mine,) = self.order.fence(self.pieces)
        now = self.stages.pop(0)
        masks = now if len(now) == 1 else [now[0], now[1], now[0] | now[1]]
        self.pieces = [mine] + [
            lax.ppermute(mine, AXES, [(d, d ^ m) for d in range(self.n)]) for m in masks
        ]

    def step(self):
        m, rows, width = self.pieces[0].shape
        count = len(self.pieces)
        self.pieces = self.order(
            join_kernel,
            *self.order.fence(self.pieces),
            name="join",
            in_specs=[VMEM] * count,
            out_specs=[VMEM],
            out_shape=[shape((count * m, rows, width), B16)],
            compiler_params=params(62),
            cost_estimate=SHORT,
        )
        self.issue()

    def result(self):
        return self.order.fence(self.pieces)


def params(limit):
    return pltpu.CompilerParams(vmem_limit_bytes=limit * MIB)


LONG = pl.CostEstimate(flops=200_000_000_000, bytes_accessed=1000, transcendentals=0)


SHORT = pl.CostEstimate(flops=1000, bytes_accessed=1000, transcendentals=0)


def shape(dims, dtype=F32):
    return jax.ShapeDtypeStruct(dims, dtype)


def sem(count):
    return pltpu.SemaphoreType.DMA((count,))


def shards(
    mesh_shape,
    q_tokens,
    p_tokens,
    q_cotangent,
    p_cotangent,
    positives,
    counts,
    wq,
    bq,
    wk,
    wv,
    bv,
    wo,
    bo,
    g1,
    s1,
    wu,
    bu,
    wd,
    bd,
    g2,
    s2,
):
    n = mesh_shape["dp"] * mesh_shape["rep"]
    plane = rounds_of(mesh_shape)
    pairs = plane[0][-2:-1]
    me = lax.axis_index("dp") * mesh_shape["rep"] + lax.axis_index("rep")
    tables = np.concatenate([order_table(plane, n), np.arange(n, dtype=np.int32)[:, None]], 1)
    table = lax.dynamic_index_in_dim(jnp.asarray(tables), me, 0, False)
    qn, ql, h = q_tokens.shape
    pn, plen, _ = p_tokens.shape
    ff = wu.shape[2]
    qr, pr = qn * ql, pn * plen
    assert qn == 4 and pn == 4 and h == 512 and ff == 2048 and 24 <= n and 4 * n <= h
    q_x, p_x = q_tokens.reshape(qr, h), p_tokens.reshape(pr, h)
    q_cot, p_cot = q_cotangent.reshape(qr, h), p_cotangent.reshape(pr, h)
    order = Order()

    def whole(*dims):
        return pl.BlockSpec(dims, lambda b: (0,) * len(dims))

    one, wide = whole(2, h), whole(2, ff)
    seq_block = pl.BlockSpec((plen, h), lambda b: (b, 0))
    pq, pk, pv, qq, qk, qv, payload = order(
        front_kernel,
        positives, counts, bq, bv, bo, g1, s1, bu, bd, g2, s2, p_x, q_x, wq, wk, wv, wo, wu, wd,
        name="front",
        in_specs=[SMEM] * 2 + [VMEM] * 9 + [ANY] * 8,
        out_specs=[ANY] * 6 + [VMEM],
        out_shape=[shape((pr, h), B16)] * 3 + [shape((qr, h), B16)] * 3 + [shape((16, h), B16)],
        scratch_shapes=[
            pltpu.VMEM((pr, h), B16),
            pltpu.VMEM((qr, h), B16),
            pltpu.VMEM((2, 3, h, h), B16),
            pltpu.VMEM((2, h, h), B16),
            pltpu.VMEM((2, h, ff), B16),
            pltpu.VMEM((2, ff, h), B16),
            pltpu.VMEM((3, pr, h), B16),
            pltpu.VMEM((3, qr, h), B16),
            pltpu.VMEM((16, h), F32),
            sem(11),
            sem(6),
        ],
        compiler_params=params(62),
        cost_estimate=LONG,
    )
    gather = Gather(order, payload, n)

    def passages(kernel, name, at, count, operands, in_specs, outs, before, **kwargs):
        def spec(block):
            if not isinstance(block, tuple):
                return block
            axis = block.index(None) if None in block else len(block) - 2
            return pl.BlockSpec(
                block, lambda b: tuple(b + at if i == axis else 0 for i in range(len(block)))
            )

        n_in, n_before = len(operands), len(before)

        def body(*refs):
            kernel(*refs[:n_in], *refs[n_in + n_before :])

        return order(
            body,
            *operands,
            *before,
            name=name,
            grid=(count,),
            in_specs=[spec(x) for x in in_specs] + [ANY] * n_before,
            out_specs=[spec(block) for block, _ in outs],
            out_shape=[s for _, s in outs],
            input_output_aliases={n_in + i: i for i in range(n_before)},
            compiler_params=params(62),
            cost_estimate=LONG,
            **kwargs,
        )

    seq, seq_wide = (plen, h), (plen, ff)
    probs_block = (None, 2, 4 * plen, plen)

    def attention(at, count, before):
        return passages(
            passage_attention_kernel, "passage_attention", at, count,
            (pq, pk, pv, p_x, bo, wo),
            [seq] * 4 + [one, ANY],
            [
                (probs_block, shape((pn, 2, 4 * plen, plen), B16)),
                (seq, shape((pr, h), B16)),
                (seq, shape((pr, h))),
            ],
            before,
            scratch_shapes=[pltpu.VMEM((h, h), B16), pltpu.SemaphoreType.DMA],
        )

    part = attention(0, 2, [])
    gather.step()
    q_probs, q_att, q_first = order(
        functools.partial(question_attention_kernel, ql),
        qq, qk, qv, q_x, bo, wo,
        name="question_attention",
        grid=(1,),
        in_specs=[whole(qr, h)] * 4 + [one, pl.BlockSpec((None, h, h), lambda b: (0, 0, 0))],
        out_specs=[whole(2, 4 * qr, qr), whole(qr, h), whole(qr, h)],
        out_shape=[shape((2, 4 * qr, qr), B16), shape((qr, h), B16), shape((qr, h))],
        compiler_params=params(62),
        cost_estimate=LONG,
    )
    while gather.stages:
        gather.step()
    gathered = [x.reshape(-1, h) for x in gather.result()]

    rows = 2048 // n
    half = n // 2
    terms, d_cls_p, q_grad, small_q, q_out, q_keep, q_send = order(
        question_back_kernel,
        table, *gathered, q_x, q_cot, qq, qk, qv, q_probs, q_att, q_first,
        g1, s1, bu, bd, g2, s2, wq, wk, wv, wo, wu, wd,
        name="question_back",
        in_specs=[SMEM] + [VMEM] * 16 + [ANY] * 6,
        out_specs=[VMEM] * 5 + [ANY] * 2,
        out_shape=[
            shape((8, 128)),
            shape((8, h)),
            shape((qr, h)),
            shape((16, h)),
            shape((qr, h), B16),
            shape((half, 3 * rows, h), B16),
            shape((half, 3 * rows, h), B16),
        ],
        scratch_shapes=[
            pltpu.VMEM((3, h, h), B16),
            pltpu.VMEM((h, h), B16),
            pltpu.VMEM((h, ff), B16),
            pltpu.VMEM((ff, h), B16),
            pltpu.VMEM((qr, ff), B16),
            pltpu.VMEM((qr, ff), F32),
            pltpu.VMEM((qr, ff), B16),
            pltpu.VMEM((ff, h), B16),
            pltpu.VMEM((h, ff), B16),
            pltpu.VMEM((4 * h, h), B16),
            sem(6),
            sem(2),
        ],
        compiler_params=params(62),
        cost_estimate=LONG,
    )
    steps = steps_of(plane, pairs)
    q_sum = Sum(order, steps, steps, n, q_keep, q_send)
    advance(order, [], [q_sum])
    p_probs, p_att, p_first = attention(2, 2, part)
    advance(order, [q_sum])

    parts_of = 2
    two = (pr // parts_of, h)

    def rows_at(width):
        return pl.BlockSpec((pr // parts_of, width), lambda b: (jnp.minimum(b, parts_of - 1), 0))

    p_out, d_first, small_p, f_keep, f_send = order(
        functools.partial(passage_feed_kernel, parts_of),
        table, d_cls_p, p_cot, p_first, g1, s1, bu, bd, g2, s2, wu, wd,
        name="passage_feed",
        grid=(parts_of + 2,),
        in_specs=[SMEM, whole(8, h), rows_at(h), rows_at(h), one, one, wide, one, one, one, ANY, ANY],
        out_specs=[rows_at(h), rows_at(h), whole(16, h), ANY, ANY],
        out_shape=[shape((pr, h), B16), shape((pr, h)), shape((16, h))]
        + [shape((half, 2 * rows, h), B16)] * 2,
        scratch_shapes=[
            pltpu.VMEM((h, ff), B16),
            pltpu.VMEM((ff, h), B16),
            pltpu.VMEM((pr // parts_of, ff), F32),
            pltpu.VMEM((pr, ff), B16),
            pltpu.VMEM((pr, ff), B16),
            pltpu.VMEM((pr, h), B16),
            pltpu.VMEM((pr, h), B16),
            pltpu.VMEM((ff, h), B16),
            pltpu.VMEM((h, ff), B16),
            sem(2),
            sem(2),
        ],
        compiler_params=params(62),
        cost_estimate=LONG,
    )
    f_sum = Sum(order, steps, steps, n, f_keep, f_send)
    advance(order, [q_sum], [f_sum])
    p_grad, a_keep, a_send = order(
        passage_attention_back_kernel,
        table, small_q, small_p, d_first, pq, pk, pv, p_probs, p_x, p_att, wq, wk, wv, wo,
        name="passage_attention_back",
        grid=(pn,),
        in_specs=[SMEM, whole(16, h), whole(16, h)] + [seq_block] * 4
        + [pl.BlockSpec(probs_block, lambda b: (b, 0, 0, 0))] + [ANY] * 6,
        out_specs=[seq_block, ANY, ANY],
        out_shape=[shape((pr, h))] + [shape((half, rows + 16, h), B16)] * 2,
        scratch_shapes=[
            pltpu.VMEM((3, h, h), B16),
            pltpu.VMEM((h, h), B16),
            pltpu.VMEM((pr, h), B16),
            pltpu.VMEM((pr, h), B16),
            pltpu.VMEM((4, pr, h), B16),
            pltpu.VMEM((16, h), F32),
            pltpu.VMEM((n, 16, h), B16),
            pltpu.VMEM((4 * h, h), B16),
            sem(6),
            sem(2),
        ],
        compiler_params=params(62),
        cost_estimate=LONG,
    )
    a_sum = Sum(order, steps, steps, n, a_keep, a_send)
    advance(order, [q_sum, f_sum], [a_sum])

    def place(e, kinds, which, before, with_small):
        pieces = which.pieces
        starts, at = [], 0
        for piece in pieces:
            starts.append(at)
            at += piece.shape[0]
        dims = []
        for kind in kinds:
            dims += {"down": [(2, ff, h)], "up": [(2, h, ff)], "att": [(2, h, h)] * 4}[kind]
        outs = [shape(d) for d in dims]
        smalls = [shape((2, h))] * 8 + [shape((2, ff))] if with_small else []
        return order(
            functools.partial(
                place_kernel, e, kinds, tuple(starts), len(before), with_small
            ),
            table, *pieces, *before,
            name="place",
            in_specs=[SMEM] + [VMEM] * len(pieces) + [ANY] * len(before),
            out_specs=[ANY] * len(outs) + [VMEM] * len(smalls),
            out_shape=outs + smalls,
            input_output_aliases={1 + len(pieces) + i: i for i in range(len(before))},
            scratch_shapes=[pltpu.VMEM((n, rows, h), F32) for _ in kinds]
            + [sem(len(outs))]
            + ([pltpu.VMEM((n, 8, h), F32)] if with_small else []),
            compiler_params=params(40),
            cost_estimate=SHORT,
        )

    for name in tail_order(
        {"q": (q_sum, 3), "f": (f_sum, 2), "a": (a_sum, 1.25)}, {"q": 10.0, "f": 10.0, "a": 12.0}
    ):
        advance(order, [{"q": q_sum, "f": f_sum, "a": a_sum}[name]])
    down, up, gq, gk, gv, go = place(0, ("down", "up", "att"), q_sum, [], False)
    down, up = place(1, ("down", "up"), f_sum, [down, up], False)
    gq, gk, gv, go, *smalls = place(1, ("att",), a_sum, [gq, gk, gv, go], True)
    sbq, sbv, sbo, sg1, ss1, sbd, sg2, ss2, sbu = smalls
    return (
        q_out.reshape(qn, ql, h),
        p_out.reshape(pn, plen, h),
        terms[:qn, 0],
        q_grad.reshape(qn, ql, h),
        p_grad.reshape(pn, plen, h),
        gq, sbq, gk, gv, sbv, go, sbo, sg1, ss1, up, sbu, down, sbd, sg2, ss2,
    )


def solution(mesh):
    split = P(AXES)
    return jax.shard_map(
        functools.partial(shards, dict(mesh.shape)),
        mesh=mesh,
        in_specs=(split,) * 6 + (P(),) * 15,
        out_specs=(split,) * 5 + (P(),) * 15,
        check_vma=False,
    )
```

time: 304 us -> 248 us (0.82)
  local copies, waits for them, and re-layouts: 49.5 us -> 2.78 us
  waiting for transfers between devices: 112 us -> 74 us
  starting transfers between devices: 31.3 us -> 52.9 us
  other arithmetic: 7.95 us -> 16 us
    unnamed x156 -> x14, local copies, waits for them, and re-layouts: 47.5 us -> 0.96 us
    ppermute x40 -> x46, waiting for transfers between devices: 112 us -> 74 us  [the longest x39 73.4 us: exchange(): return lax.ppermute(x, AXES, [(d, d ^ masks[d & 1]) for d in range(n)])]
    ppermute x40 -> x46, starting transfers between devices: 31.3 us -> 52.9 us  [the longest x39 43.6 us: exchange(): return lax.ppermute(x, AXES, [(d, d ^ masks[d & 1]) for d in range(n)])]
    convert_element_type x15 -> x12, other arithmetic: 7.27 us -> 15.5 us  [total(): return sum((p.astype(F32) for p in parts)).astype(B16)]
    pallas_call x9 -> x12, Pallas kernels: 100 us -> 97.4 us  [__call__(): *outs, self.token = call(*([self.token] if skip else []), *operands)]
  transfers between devices with their start and end apart: 40 -> 46, of which waited for: 19 -> 21; matrix products, arithmetic and copies ran while one was open for 3% -> 3% of each run, Pallas kernels for 23% -> 24%
where the time goes in v2:
time: 248 us; the launch traced here: 244 us
  Pallas kernels  97.4 us (39%)
  waiting for transfers between devices  74 us (30%)
  starting transfers between devices  52.9 us (21%)
  other arithmetic  16 us (6%)
  local copies, waits for them, and re-layouts  2.78 us (1%)
    pallas_call x12, Pallas kernels, __call__(): *outs, self.token = call(*([self.token] if skip else []), *operands)  97.4 us
    ppermute x39, waiting for transfers between devices, exchange(): return lax.ppermute(x, AXES, [(d, d ^ masks[d & 1]) for d in range(n)])  73.4 us
    ppermute x39, starting transfers between devices, exchange(): return lax.ppermute(x, AXES, [(d, d ^ masks[d & 1]) for d in range(n)])  43.6 us
    convert_element_type x12, other arithmetic, total(): return sum((p.astype(F32) for p in parts)).astype(B16)  15.5 us
    ppermute x7, starting transfers between devices, issue(): lax.ppermute(mine, AXES, [(d, d ^ m) for d in range(self.n)])  9.25 us
  transfers between devices with their start and end apart: 46, of which 21 were waited for; matrix products, arithmetic and copies ran while one was open for 3% of the time, Pallas kernels for 24%

profile of v2, /device:TPU:0, one launch (start us, length us, event | category | flops | bytes accessed | tf_op | source)
XLA Modules:
  0.0 244.4 jit_solution(13274814616580577509)
XLA Ops:
  0.7 10.2 %front.1 = (bf16[1024,512]{1,0:T(8,128)(2,1)}, bf16[1024,512]{1,0:T(8,128)(2,1)}, bf16[1024,512]{1,0:T(8,128)(2,1)}, bf16[256,512]{1,0:T(8,128)(2,1)}, bf16[256,...) custom-call(s32[4,4]{1,0:T(4,128)} %refs_0_.1, s32[4]{0:T(128)} %refs_1_.1, ...), custom_call_target="tpu_custom_call" | custom-call | flops 199999995904 | bytes 1000 | tf_op jit(solution)/shard_map/front/pallas_call | solution.py:689
  10.8 5.1 %collective-permute-start.2 = (bf16[1,16,512]{2,1,0:T(8,128)(2,1)}, bf16[1,16,512]{2,1,0:T(8,128)(2,1)}, u32[]{:S(2)}, u32[]{:S(2)}) collective-permute-start(bf16[1,16,512]{2,1,0:T(8,128)(2,1)} %bitcast.13), channel_id=1, source_target_pairs={{0,24},{1,25},{2,26},{3,27},{4,28},{5,29},{6,30},{7,31},{8,16},{9,... | collective-permute-start | bytes 49160 | tf_op jit(solution)/shard_map/ppermute | solution.py:802
  16.6 6.3 %passage_attention.2 = (bf16[4,2,1024,256]{3,2,1,0:T(8,128)(2,1)}, bf16[1024,512]{1,0:T(8,128)(2,1)}, f32[1024,512]{1,0:T(8,128)}, f32[8,128]{1,0:T(8,128)}) custom-call(f32[8,128]{1,0:T(8,128)} %get-tuple-element.219.refs_0_, bf16[1024,512]{1,0:T(8,128)(2,1)} %get-tuple-element.220.refs_1_.refs_5_, bf16[1024,512]{1,0:T(8,128)(2,1)} %get-tuple-element.221.refs_2_.refs_6_, ...), custom_call_target="tpu_custom_call" | custom-call | flops 199999995904 | bytes 1000 | tf_op jit(solution)/shard_map/passage_attention/pallas_call | solution.py:689
  24.4 2.6 %collective-permute-start.5 = (bf16[4,16,512]{2,1,0:T(8,128)(2,1)}, bf16[4,16,512]{2,1,0:T(8,128)(2,1)}, u32[]{:S(2)}, u32[]{:S(2)}) collective-permute-start(bf16[4,16,512]{2,1,0:T(8,128)(2,1)} %get-tuple-element.236.refs_1_), channel_id=1, source_target_pairs={{0,6},{1,7},{2,4},{3,5},{4,2},{5,3},{6,0},{7,1},{8,14},{9,15},{10,... | collective-permute-start | bytes 196616 | tf_op jit(solution)/shard_map/ppermute | solution.py:802
  27.9 4.2 %question_attention.1 = (bf16[2,1024,256]{2,1,0:T(8,128)(2,1)}, bf16[256,512]{1,0:T(8,128)(2,1)}, f32[256,512]{1,0:T(8,128)}, f32[8,128]{1,0:T(8,128)}) custom-call(f32[8,128]{1,0:T(8,128)} %get-tuple-element.230.refs_0_, bf16[256,512]{1,0:T(8,128)(2,1)} %get-tuple-element.231.refs_1_.refs_6_, bf16[256,512]{1,0:T(8,128)(2,1)} %get-tuple-element.232.refs_2_.refs_7_, ...), custom_call_target="tpu_custom_call" | custom-call | flops 199999995904 | bytes 1000 | tf_op jit(solution)/shard_map/question_attention/pallas_call | solution.py:689
  32.1 1.6 join.3
  36.2 13.9 %question_back.1 = (f32[8,128]{1,0:T(8,128)}, f32[8,512]{1,0:T(8,128)}, f32[256,512]{1,0:T(8,128)}, f32[16,512]{1,0:T(8,128)}, bf16[256,512]{1,0:T(8,128)(2,1)},...) custom-call(f32[8,128]{1,0:T(8,128)} %get-tuple-element.242.refs_0_, ...), custom_call_target="tpu_custom_call" | custom-call | flops 199999995904 | bytes 1000 | tf_op jit(solution)/shard_map/question_back/pallas_call | solution.py:689
  50.3 6.4 %passage_attention.3 = (bf16[4,2,1024,256]{3,2,1,0:T(8,128)(2,1)}, bf16[1024,512]{1,0:T(8,128)(2,1)}, f32[1024,512]{1,0:T(8,128)}, f32[8,128]{1,0:T(8,128)}) custom-call(f32[8,128]{1,0:T(8,128)} %get-tuple-element.253.refs_0_, bf16[1024,512]{1,0:T(8,128)(2,1)} %get-tuple-element.220.refs_1_.refs_5_, ...), custom_call_target="tpu_custom_call", output_to_operand_aliasing={{0}: (7, {}), {1}: (8, {}), {2}: (9, {})} | custom-call | flops 199999995904 | bytes 1000 | tf_op jit(solution)/shard_map/passage_attention/pallas_call | solution.py:689
  56.7 3.5 %add_convert_fusion = bf16[8,192,512]{2,1,0:T(8,128)(2,1)} fusion(bf16[16,192,512]{2,1,0:T(8,128)(2,1)} %collective-permute-done.7, bf16[16,192,512]{2,1,0:T(8,128)(2,1)} %get-tuple-element.249), kind=kLoop, calls=%fused_computation | loop fusion | flops 3145728 | bytes 4718592 | tf_op jit(solution)/shard_map/convert_element_type | solution.py:635
  60.2 1.6 collective-permute-start.8
  61.8 24.5 %passage_feed.1 = (bf16[1024,512]{1,0:T(8,128)(2,1)}, f32[1024,512]{1,0:T(8,128)}, f32[16,512]{1,0:T(8,128)}, bf16[16,128,512]{2,1,0:T(8,128)(2,1)}, bf16[16,128,512]{2,1,0:T(8,128)(2,1)}, /*index=5*/f32[8,128]{1,0:T(8,128)}) custom-call(f32[8,128]{1,0:T(8,128)} %get-tuple-element.260.refs_0_, s32[33]{0:T(128)} %dynamic-slice_bitcast_fusion.refs_1_, ...), custom_call_target="tpu_custom_call" | custom-call | flops 199999995904 | bytes 1000 | tf_op jit(solution)/shard_map/passage_feed/pallas_call | solution.py:689
  86.3 2.8 %add_convert_fusion.2 = bf16[4,192,512]{2,1,0:T(8,128)(2,1)} fusion(bf16[8,192,512]{2,1,0:T(8,128)(2,1)} %collective-permute-done.8, bf16[16,192,512]{2,1,0:T(8,128)(2,1)} %collective-permute-done.7, bf16[16,192,512]{2,1,0:T(8,128)(2,1)} %get-tuple-element.249), kind=kLoop, calls=%fused_computation.3 | loop fusion | flops 2359296 | bytes 3145728 | tf_op jit(solution)/shard_map/convert_element_type | solution.py:635
  90.6 16.8 %passage_attention_back.1 = (f32[1024,512]{1,0:T(8,128)}, bf16[16,80,512]{2,1,0:T(8,128)(2,1)}, bf16[16,80,512]{2,1,0:T(8,128)(2,1)}, f32[8,128]{1,0:T(8,128)}) custom-call(f32[8,128]{1,0:T(8,128)} %get-tuple-element.271.refs_0_, s32[33]{0:T(128)} %dynamic-slice_bitcast_fusion.refs_1_, f32[16,512]{1,0:T(8,128)} %get-tuple-element.272.refs_2_, ...), custom_call_target="tpu_custom_call" | custom-call | flops 199999995904 | bytes 1000 | tf_op jit(solution)/shard_map/passage_attention_back/pallas_call | solution.py:689
  107.4 2.1 add_convert_fusion.7
  109.8 1.6 add_convert_fusion.1
  112.3 2.1 collective-permute-start.12
  114.4 2.0 collective-permute-start.13
  116.7 9.7 %collective-permute-done.15 = bf16[8,128,512]{2,1,0:T(8,128)(2,1)S(1)} collective-permute-done((bf16[8,128,512]{2,1,0:T(8,128)(2,1)S(1)}, bf16[8,128,512]{2,1,0:T(8,128)(2,1)S(1)}, u32[]{:S(2)}, u32[]{:S(2)}) %collective-permute-start.15) | collective-permute-done | bytes 1048608 | tf_op jit(solution)/shard_map/ppermute | solution.py:631
  127.6 2.2 collective-permute-done.14
  132.4 2.1 collective-permute-start.19
  134.6 3.7 %collective-permute-start.18 = (bf16[1,192,512]{2,1,0:T(8,128)(2,1)S(1)}, bf16[1,192,512]{2,1,0:T(8,128)(2,1)S(1)}, u32[]{:S(2)}, u32[]{:S(2)}) collective-permute-start(bf16[1,192,512]{2,1,0:T(8,128)(2,1)S(1)} %add_convert_fusion.6), channel_id=1, source_target_pairs={{0,8},{1,9},{2,10},{3,11},{4,12},{5,13},{6,14},{7,15},{8,0},{9,1},... | collective-permute-start | bytes 589832 | tf_op jit(solution)/shard_map/ppermute | solution.py:631
  141.9 3.3 %collective-permute-done.18 = bf16[1,192,512]{2,1,0:T(8,128)(2,1)S(1)} collective-permute-done((bf16[1,192,512]{2,1,0:T(8,128)(2,1)S(1)}, bf16[1,192,512]{2,1,0:T(8,128)(2,1)S(1)}, u32[]{:S(2)}, u32[]{:S(2)}) %collective-permute-start.18) | collective-permute-done | bytes 196640 | tf_op jit(solution)/shard_map/ppermute | solution.py:631
  145.2 8.4 %collective-permute-done.17 = bf16[1,192,512]{2,1,0:T(8,128)(2,1)S(1)} collective-permute-done((bf16[1,192,512]{2,1,0:T(8,128)(2,1)S(1)}, bf16[1,192,512]{2,1,0:T(8,128)(2,1)S(1)}, u32[]{:S(2)}, u32[]{:S(2)}) %collective-permute-start.17) | collective-permute-done | bytes 196640 | tf_op jit(solution)/shard_map/ppermute | solution.py:631
  154.1 2.4 collective-permute-start.24
  156.5 2.0 collective-permute-start.25
  158.6 6.6 %collective-permute-done.23 = bf16[1,128,512]{2,1,0:T(8,128)(2,1)S(1)} collective-permute-done((bf16[1,128,512]{2,1,0:T(8,128)(2,1)S(1)}, bf16[1,128,512]{2,1,0:T(8,128)(2,1)S(1)}, u32[]{:S(2)}, u32[]{:S(2)}) %collective-permute-start.23) | collective-permute-done | bytes 131104 | tf_op jit(solution)/shard_map/ppermute | solution.py:631
  166.5 1.7 collective-permute-start.37
  168.5 2.0 collective-permute-start.31
  170.5 2.2 collective-permute-start.30
  173.1 5.8 %collective-permute-done.21 = bf16[4,80,512]{2,1,0:T(8,128)(2,1)S(1)} collective-permute-done((bf16[4,80,512]{2,1,0:T(8,128)(2,1)S(1)}, bf16[4,80,512]{2,1,0:T(8,128)(2,1)S(1)}, u32[]{:S(2)}, u32[]{:S(2)}) %collective-permute-start.21) | collective-permute-done | bytes 327712 | tf_op jit(solution)/shard_map/ppermute | solution.py:631
  179.1 4.2 %collective-permute-done.29 = bf16[1,128,512]{2,1,0:T(8,128)(2,1)S(1)} collective-permute-done((bf16[1,128,512]{2,1,0:T(8,128)(2,1)S(1)}, bf16[1,128,512]{2,1,0:T(8,128)(2,1)S(1)}, u32[]{:S(2)}, u32[]{:S(2)}) %collective-permute-start.29) | collective-permute-done | bytes 131104 | tf_op jit(solution)/shard_map/ppermute | solution.py:631
  183.2 2.7 %collective-permute-start.27 = (bf16[1,80,512]{2,1,0:T(8,128)(2,1)S(1)}, bf16[1,80,512]{2,1,0:T(8,128)(2,1)S(1)}, u32[]{:S(2)}, u32[]{:S(2)}) collective-permute-start(bf16[1,80,512]{2,1,0:T(8,128)(2,1)S(1)} %get-tuple-element.334), channel_id=1, source_target_pairs={{0,8},{1,9},{2,10},{3,11},{4,12},{5,13},{6,14},{7,15},{8,0},{9,1},... | collective-permute-start | bytes 245768 | tf_op jit(solution)/shard_map/ppermute | solution.py:631
  185.9 1.7 collective-permute-start.28
  187.7 2.5 %collective-permute-done.26 = bf16[1,80,512]{2,1,0:T(8,128)(2,1)S(1)} collective-permute-done((bf16[1,80,512]{2,1,0:T(8,128)(2,1)S(1)}, bf16[1,80,512]{2,1,0:T(8,128)(2,1)S(1)}, u32[]{:S(2)}, u32[]{:S(2)}) %collective-permute-start.26) | collective-permute-done | bytes 81952 | tf_op jit(solution)/shard_map/ppermute | solution.py:631
  190.3 1.9 collective-permute-done.28
  192.3 1.8 collective-permute-start.34
  194.4 2.4 collective-permute-start.32
  196.8 1.7 collective-permute-start.36
  199.9 2.3 collective-permute-done.32
  202.8 3.4 %collective-permute-done.36 = bf16[4,128,512]{2,1,0:T(8,128)(2,1)S(1)} collective-permute-done((bf16[4,128,512]{2,1,0:T(8,128)(2,1)S(1)}, bf16[4,128,512]{2,1,0:T(8,128)(2,1)S(1)}, u32[]{:S(2)}, u32[]{:S(2)}) %collective-permute-start.36) | collective-permute-done | bytes 524320 | tf_op jit(solution)/shard_map/ppermute | solution.py:631
  206.9 1.5 collective-permute-start.35
  208.4 9.1 %collective-permute-done.35 = bf16[4,80,512]{2,1,0:T(8,128)(2,1)S(1)} collective-permute-done((bf16[4,80,512]{2,1,0:T(8,128)(2,1)S(1)}, bf16[4,80,512]{2,1,0:T(8,128)(2,1)S(1)}, u32[]{:S(2)}, u32[]{:S(2)}) %collective-permute-start.35) | collective-permute-done | bytes 327712 | tf_op jit(solution)/shard_map/ppermute | solution.py:631
  217.6 1.6 collective-permute-start.38
  219.2 2.6 %collective-permute-done.39.refs_3_ = bf16[8,128,512]{2,1,0:T(8,128)(2,1)S(1)} collective-permute-done((bf16[8,128,512]{2,1,0:T(8,128)(2,1)S(1)}, bf16[8,128,512]{2,1,0:T(8,128)(2,1)S(1)}, u32[]{:S(2)}, u32[]{:S(2)}) %collective-permute-start.39) | collective-permute-done | bytes 1048608 | tf_op jit(solution)/shard_map/ppermute | solution.py:631
  222.3 6.5 %collective-permute-done.38.refs_3_ = bf16[8,80,512]{2,1,0:T(8,128)(2,1)S(1)} collective-permute-done((bf16[8,80,512]{2,1,0:T(8,128)(2,1)S(1)}, bf16[8,80,512]{2,1,0:T(8,128)(2,1)S(1)}, u32[]{:S(2)}, u32[]{:S(2)}) %collective-permute-start.38) | collective-permute-done | bytes 655392 | tf_op jit(solution)/shard_map/ppermute | solution.py:631
  231.9 5.1 %place.3 = (f32[2,2048,512]{2,1,0:T(8,128)}, f32[2,512,2048]{2,1,0:T(8,128)}, f32[2,512,512]{2,1,0:T(8,128)}, f32[2,512,512]{2,1,0:T(8,128)}, f32[2,512,512]{2,1...) custom-call(f32[8,128]{1,0:T(8,128)S(1)} %copy-done.1, s32[33]{0:T(128)S(1)} %copy-done, ...), custom_call_target="tpu_custom_call" | custom-call | flops 1000 | bytes 1000 | tf_op jit(solution)/shard_map/place/pallas_call | solution.py:689
  236.9 3.8 %place.4 = (f32[2,2048,512]{2,1,0:T(8,128)}, f32[2,512,2048]{2,1,0:T(8,128)}, f32[8,128]{1,0:T(8,128)S(1)}) custom-call(f32[8,128]{1,0:T(8,128)S(1)} %get-tuple-element.385.refs_0_, s32[33]{0:T(128)S(1)} %copy-done, bf16[8,128,512]{2,1,0:T(8,128)(2,1)S(1)} %pad_maximum_fusion.1.refs_2_, ...), custom_call_target="tpu_custom_call", output_to_operand_aliasing={{0}: (6, {}), {1}: (7, {})} | custom-call | flops 1000 | bytes 1000 | tf_op jit(solution)/shard_map/place/pallas_call | solution.py:689
  240.8 3.2 %place.5 = (f32[2,512,512]{2,1,0:T(8,128)}, f32[2,512,512]{2,1,0:T(8,128)}, f32[2,512,512]{2,1,0:T(8,128)}, f32[2,512,512]{2,1,0:T(8,128)}, f32[2,512]{1,0:T(2,1...) custom-call(f32[8,128]{1,0:T(8,128)S(1)} %get-tuple-element.390.refs, ...), custom_call_target="tpu_custom_call", output_to_operand_aliasing={{0}: (6, {}), {1}: (7, {}), {2}: (8, {}), {3}: (9, {})} | custom-call | flops 1000 | bytes 1000 | tf_op jit(solution)/shard_map/place/pallas_call | solution.py:689
  (90 shorter events, 25.3 us)
Async XLA Ops:
  10.8 12.1 %collective-permute-start.2 = (bf16[1,16,512]{2,1,0:T(8,128)(2,1)}, bf16[1,16,512]{2,1,0:T(8,128)(2,1)}, u32[]{:S(2)}, u32[]{:S(2)}) collective-permute-start(bf16[1,16,512]{2,1,0:T(8,128)(2,1)} %bitcast.13), channel_id=1, source_target_pairs={{0,24},{1,25},{2,26},{3,27},{4,28},{5,29},{6,30},{7,31},{8,16},{9,... | collective-permute-start | bytes 49160 | tf_op jit(solution)/shard_map/ppermute | solution.py:802
  15.9 7.0 %collective-permute-start.1 = (bf16[1,16,512]{2,1,0:T(8,128)(2,1)}, bf16[1,16,512]{2,1,0:T(8,128)(2,1)}, u32[]{:S(2)}, u32[]{:S(2)}) collective-permute-start(bf16[1,16,512]{2,1,0:T(8,128)(2,1)} %bitcast.14), channel_id=1, source_target_pairs={{0,8},{1,9},{2,10},{3,11},{4,12},{5,13},{6,14},{7,15},{8,0},{9,1},... | collective-permute-start | bytes 49160 | tf_op jit(solution)/shard_map/ppermute | solution.py:802
  15.9 7.0 %collective-permute-start = (bf16[1,16,512]{2,1,0:T(8,128)(2,1)}, bf16[1,16,512]{2,1,0:T(8,128)(2,1)}, u32[]{:S(2)}, u32[]{:S(2)}) collective-permute-start(bf16[1,16,512]{2,1,0:T(8,128)(2,1)} %bitcast.15), channel_id=1, source_target_pairs={{0,16},{1,17},{2,18},{3,19},{4,20},{5,21},{6,22},{7,23},{8,24},{9,... | collective-permute-start | bytes 49160 | tf_op jit(solution)/shard_map/ppermute | solution.py:802
  24.4 7.7 %collective-permute-start.5 = (bf16[4,16,512]{2,1,0:T(8,128)(2,1)}, bf16[4,16,512]{2,1,0:T(8,128)(2,1)}, u32[]{:S(2)}, u32[]{:S(2)}) collective-permute-start(bf16[4,16,512]{2,1,0:T(8,128)(2,1)} %get-tuple-element.236.refs_1_), channel_id=1, source_target_pairs={{0,6},{1,7},{2,4},{3,5},{4,2},{5,3},{6,0},{7,1},{8,14},{9,15},{10,... | collective-permute-start | bytes 196616 | tf_op jit(solution)/shard_map/ppermute | solution.py:802
  27.0 5.1 %collective-permute-start.4 = (bf16[4,16,512]{2,1,0:T(8,128)(2,1)}, bf16[4,16,512]{2,1,0:T(8,128)(2,1)}, u32[]{:S(2)}, u32[]{:S(2)}) collective-permute-start(bf16[4,16,512]{2,1,0:T(8,128)(2,1)} %get-tuple-element.236.refs_1_), channel_id=1, source_target_pairs={{0,2},{1,3},{2,0},{3,1},{4,6},{5,7},{6,4},{7,5},{8,10},{9,11},{10,... | collective-permute-start | bytes 196616 | tf_op jit(solution)/shard_map/ppermute | solution.py:802
  27.5 4.6 %collective-permute-start.3 = (bf16[4,16,512]{2,1,0:T(8,128)(2,1)}, bf16[4,16,512]{2,1,0:T(8,128)(2,1)}, u32[]{:S(2)}, u32[]{:S(2)}) collective-permute-start(bf16[4,16,512]{2,1,0:T(8,128)(2,1)} %get-tuple-element.236.refs_1_), channel_id=1, source_target_pairs={{0,4},{1,5},{2,6},{3,7},{4,0},{5,1},{6,2},{7,3},{8,12},{9,13},{10,... | collective-permute-start | bytes 196616 | tf_op jit(solution)/shard_map/ppermute | solution.py:802
  33.7 1.7 collective-permute-start.6
  50.1 6.6 %collective-permute-start.7 = (bf16[16,192,512]{2,1,0:T(8,128)(2,1)}, bf16[16,192,512]{2,1,0:T(8,128)(2,1)}, u32[]{:S(2)}, u32[]{:S(2)}) collective-permute-start(bf16[16,192,512]{2,1,0:T(8,128)(2,1)} %get-tuple-element.252), channel_id=1, source_target_pairs={{0,1},{1,0},{2,3},{3,2},{4,5},{5,4},{6,7},{7,6},{8,9},{9,8},{10,11... | collective-permute-start | bytes 9437192 | tf_op jit(solution)/shard_map/ppermute | solution.py:631
  60.2 26.1 %collective-permute-start.8 = (bf16[8,192,512]{2,1,0:T(8,128)(2,1)}, bf16[8,192,512]{2,1,0:T(8,128)(2,1)}, u32[]{:S(2)}, u32[]{:S(2)}) collective-permute-start(bf16[8,192,512]{2,1,0:T(8,128)(2,1)} %add_convert_fusion), channel_id=1, source_target_pairs={{0,2},{1,5},{2,0},{3,7},{4,6},{5,1},{6,4},{7,3},{8,10},{9,13},{10,... | collective-permute-start | bytes 4718600 | tf_op jit(solution)/shard_map/ppermute | solution.py:631
  89.1 18.3 %collective-permute-start.9 = (bf16[4,192,512]{2,1,0:T(8,128)(2,1)}, bf16[4,192,512]{2,1,0:T(8,128)(2,1)}, u32[]{:S(2)}, u32[]{:S(2)}) collective-permute-start(bf16[4,192,512]{2,1,0:T(8,128)(2,1)} %add_convert_fusion.2), channel_id=1, source_target_pairs={{0,4},{1,3},{2,6},{3,1},{4,0},{5,7},{6,2},{7,5},{8,12},{9,11},{10,... | collective-permute-start | bytes 2359304 | tf_op jit(solution)/shard_map/ppermute | solution.py:631
  90.6 16.8 %collective-permute-start.10 = (bf16[16,128,512]{2,1,0:T(8,128)(2,1)}, bf16[16,128,512]{2,1,0:T(8,128)(2,1)}, u32[]{:S(2)}, u32[]{:S(2)}) collective-permute-start(bf16[16,128,512]{2,1,0:T(8,128)(2,1)} %get-tuple-element.280), channel_id=1, source_target_pairs={{0,1},{1,0},{2,3},{3,2},{4,5},{5,4},{6,7},{7,6},{8,9},{9,8},{10,11... | collective-permute-start | bytes 6291464 | tf_op jit(solution)/shard_map/ppermute | solution.py:631
  111.5 14.9 %collective-permute-start.15 = (bf16[8,128,512]{2,1,0:T(8,128)(2,1)S(1)}, bf16[8,128,512]{2,1,0:T(8,128)(2,1)S(1)}, u32[]{:S(2)}, u32[]{:S(2)}) collective-permute-start(bf16[8,128,512]{2,1,0:T(8,128)(2,1)S(1)} %add_convert_fusion.1), channel_id=1, source_target_pairs={{0,2},{1,5},{2,0},{3,7},{4,6},{5,1},{6,4},{7,3},{8,10},{9,13},{10,... | collective-permute-start | bytes 3145736 | tf_op jit(solution)/shard_map/ppermute | solution.py:631
  112.1 26.3 %collective-permute-start.11 = (bf16[16,80,512]{2,1,0:T(8,128)(2,1)S(1)}, bf16[16,80,512]{2,1,0:T(8,128)(2,1)S(1)}, u32[]{:S(2)}, u32[]{:S(2)}) collective-permute-start(bf16[16,80,512]{2,1,0:T(8,128)(2,1)S(1)} %copy-done.5), channel_id=1, source_target_pairs={{0,1},{1,0},{2,3},{3,2},{4,5},{5,4},{6,7},{7,6},{8,9},{9,8},{10,11... | collective-permute-start | bytes 3932168 | tf_op jit(solution)/shard_map/ppermute | solution.py:631
  112.3 15.3 %collective-permute-start.12 = (bf16[1,192,512]{2,1,0:T(8,128)(2,1)S(1)}, bf16[1,192,512]{2,1,0:T(8,128)(2,1)S(1)}, u32[]{:S(2)}, u32[]{:S(2)}) collective-permute-start(bf16[1,192,512]{2,1,0:T(8,128)(2,1)S(1)} %get-tuple-element.288), channel_id=1, source_target_pairs={{0,16},{1,17},{2,18},{3,19},{4,20},{5,21},{6,22},{7,23},{8,24},{9,... | collective-permute-start | bytes 589832 | tf_op jit(solution)/shard_map/ppermute | solution.py:631
  114.4 13.2 %collective-permute-start.13 = (bf16[1,192,512]{2,1,0:T(8,128)(2,1)S(1)}, bf16[1,192,512]{2,1,0:T(8,128)(2,1)S(1)}, u32[]{:S(2)}, u32[]{:S(2)}) collective-permute-start(bf16[1,192,512]{2,1,0:T(8,128)(2,1)S(1)} %get-tuple-element.289), channel_id=1, source_target_pairs={{0,8},{1,9},{2,10},{3,11},{4,12},{5,13},{6,14},{7,15},{8,0},{9,1},... | collective-permute-start | bytes 589832 | tf_op jit(solution)/shard_map/ppermute | solution.py:631
  116.4 13.4 %collective-permute-start.14 = (bf16[1,192,512]{2,1,0:T(8,128)(2,1)S(1)}, bf16[1,192,512]{2,1,0:T(8,128)(2,1)S(1)}, u32[]{:S(2)}, u32[]{:S(2)}) collective-permute-start(bf16[1,192,512]{2,1,0:T(8,128)(2,1)S(1)} %get-tuple-element.290), channel_id=1, source_target_pairs={{0,24},{1,25},{2,26},{3,27},{4,28},{5,29},{6,30},{7,31},{8,16},{9,... | collective-permute-start | bytes 589832 | tf_op jit(solution)/shard_map/ppermute | solution.py:631
  129.8 9.6 %collective-permute-start.20 = (bf16[4,128,512]{2,1,0:T(8,128)(2,1)S(1)}, bf16[4,128,512]{2,1,0:T(8,128)(2,1)S(1)}, u32[]{:S(2)}, u32[]{:S(2)}) collective-permute-start(bf16[4,128,512]{2,1,0:T(8,128)(2,1)S(1)} %add_convert_fusion.4), channel_id=1, source_target_pairs={{0,4},{1,3},{2,6},{3,1},{4,0},{5,7},{6,2},{7,5},{8,12},{9,11},{10,... | collective-permute-start | bytes 1572872 | tf_op jit(solution)/shard_map/ppermute | solution.py:631
  132.4 9.5 %collective-permute-start.19 = (bf16[1,192,512]{2,1,0:T(8,128)(2,1)S(1)}, bf16[1,192,512]{2,1,0:T(8,128)(2,1)S(1)}, u32[]{:S(2)}, u32[]{:S(2)}) collective-permute-start(bf16[1,192,512]{2,1,0:T(8,128)(2,1)S(1)} %add_convert_fusion.6), channel_id=1, source_target_pairs={{0,24},{1,25},{2,26},{3,27},{4,28},{5,29},{6,30},{7,31},{8,16},{9,... | collective-permute-start | bytes 589832 | tf_op jit(solution)/shard_map/ppermute | solution.py:631
  134.6 10.6 %collective-permute-start.18 = (bf16[1,192,512]{2,1,0:T(8,128)(2,1)S(1)}, bf16[1,192,512]{2,1,0:T(8,128)(2,1)S(1)}, u32[]{:S(2)}, u32[]{:S(2)}) collective-permute-start(bf16[1,192,512]{2,1,0:T(8,128)(2,1)S(1)} %add_convert_fusion.6), channel_id=1, source_target_pairs={{0,8},{1,9},{2,10},{3,11},{4,12},{5,13},{6,14},{7,15},{8,0},{9,1},... | collective-permute-start | bytes 589832 | tf_op jit(solution)/shard_map/ppermute | solution.py:631
  138.3 15.3 %collective-permute-start.17 = (bf16[1,192,512]{2,1,0:T(8,128)(2,1)S(1)}, bf16[1,192,512]{2,1,0:T(8,128)(2,1)S(1)}, u32[]{:S(2)}, u32[]{:S(2)}) collective-permute-start(bf16[1,192,512]{2,1,0:T(8,128)(2,1)S(1)} %add_convert_fusion.6), channel_id=1, source_target_pairs={{0,16},{1,17},{2,18},{3,19},{4,20},{5,21},{6,22},{7,23},{8,24},{9,... | collective-permute-start | bytes 589832 | tf_op jit(solution)/shard_map/ppermute | solution.py:631
  138.5 20.0 %collective-permute-start.16 = (bf16[8,80,512]{2,1,0:T(8,128)(2,1)S(1)}, bf16[8,80,512]{2,1,0:T(8,128)(2,1)S(1)}, u32[]{:S(2)}, u32[]{:S(2)}) collective-permute-start(bf16[8,80,512]{2,1,0:T(8,128)(2,1)S(1)} %add_convert_fusion.3), channel_id=1, source_target_pairs={{0,2},{1,5},{2,0},{3,7},{4,6},{5,1},{6,4},{7,3},{8,10},{9,13},{10,... | collective-permute-start | bytes 1966088 | tf_op jit(solution)/shard_map/ppermute | solution.py:631
  153.7 12.7 %collective-permute-start.22 = (bf16[4,192,512]{2,1,0:T(8,128)(2,1)S(1)}, bf16[4,192,512]{2,1,0:T(8,128)(2,1)S(1)}, u32[]{:S(2)}, u32[]{:S(2)}) collective-permute-start(bf16[4,192,512]{2,1,0:T(8,128)(2,1)S(1)} %pad_maximum_fusion.2), channel_id=1, source_target_pairs={{0,4},{1,3},{2,6},{3,1},{4,0},{5,7},{6,2},{7,5},{8,12},{9,11},{10,... | collective-permute-start | bytes 2359304 | tf_op jit(solution)/shard_map/ppermute | solution.py:631
  154.1 11.1 %collective-permute-start.23 = (bf16[1,128,512]{2,1,0:T(8,128)(2,1)S(1)}, bf16[1,128,512]{2,1,0:T(8,128)(2,1)S(1)}, u32[]{:S(2)}, u32[]{:S(2)}) collective-permute-start(bf16[1,128,512]{2,1,0:T(8,128)(2,1)S(1)} %get-tuple-element.319), channel_id=1, source_target_pairs={{0,16},{1,17},{2,18},{3,19},{4,20},{5,21},{6,22},{7,23},{8,24},{9,... | collective-permute-start | bytes 393224 | tf_op jit(solution)/shard_map/ppermute | solution.py:631
  154.1 11.2 %collective-permute-start.24 = (bf16[1,128,512]{2,1,0:T(8,128)(2,1)S(1)}, bf16[1,128,512]{2,1,0:T(8,128)(2,1)S(1)}, u32[]{:S(2)}, u32[]{:S(2)}) collective-permute-start(bf16[1,128,512]{2,1,0:T(8,128)(2,1)S(1)} %get-tuple-element.320), channel_id=1, source_target_pairs={{0,8},{1,9},{2,10},{3,11},{4,12},{5,13},{6,14},{7,15},{8,0},{9,1},... | collective-permute-start | bytes 393224 | tf_op jit(solution)/shard_map/ppermute | solution.py:631
  156.5 8.9 %collective-permute-start.25 = (bf16[1,128,512]{2,1,0:T(8,128)(2,1)S(1)}, bf16[1,128,512]{2,1,0:T(8,128)(2,1)S(1)}, u32[]{:S(2)}, u32[]{:S(2)}) collective-permute-start(bf16[1,128,512]{2,1,0:T(8,128)(2,1)S(1)} %get-tuple-element.321), channel_id=1, source_target_pairs={{0,24},{1,25},{2,26},{3,27},{4,28},{5,29},{6,30},{7,31},{8,16},{9,... | collective-permute-start | bytes 393224 | tf_op jit(solution)/shard_map/ppermute | solution.py:631
  166.5 35.7 %collective-permute-start.37 = (bf16[8,192,512]{2,1,0:T(8,128)(2,1)S(1)}, bf16[8,192,512]{2,1,0:T(8,128)(2,1)S(1)}, u32[]{:S(2)}, u32[]{:S(2)}) collective-permute-start(bf16[8,192,512]{2,1,0:T(8,128)(2,1)S(1)} %pad_maximum_fusion.refs_2_), channel_id=1, source_target_pairs={{0,2},{1,5},{2,0},{3,7},{4,6},{5,1},{6,4},{7,3},{8,10},{9,13},{10,... | collective-permute-start | bytes 4718600 | tf_op jit(solution)/shard_map/ppermute | solution.py:631
  168.3 10.6 %collective-permute-start.21 = (bf16[4,80,512]{2,1,0:T(8,128)(2,1)S(1)}, bf16[4,80,512]{2,1,0:T(8,128)(2,1)S(1)}, u32[]{:S(2)}, u32[]{:S(2)}) collective-permute-start(bf16[4,80,512]{2,1,0:T(8,128)(2,1)S(1)} %add_convert_fusion.5), channel_id=1, source_target_pairs={{0,4},{1,3},{2,6},{3,1},{4,0},{5,7},{6,2},{7,5},{8,12},{9,11},{10,... | collective-permute-start | bytes 983048 | tf_op jit(solution)/shard_map/ppermute | solution.py:631
  168.5 10.5 %collective-permute-start.31 = (bf16[1,128,512]{2,1,0:T(8,128)(2,1)S(1)}, bf16[1,128,512]{2,1,0:T(8,128)(2,1)S(1)}, u32[]{:S(2)}, u32[]{:S(2)}) collective-permute-start(bf16[1,128,512]{2,1,0:T(8,128)(2,1)S(1)} %add_convert_fusion.10), channel_id=1, source_target_pairs={{0,24},{1,25},{2,26},{3,27},{4,28},{5,29},{6,30},{7,31},{8,16},{9,... | collective-permute-start | bytes 393224 | tf_op jit(solution)/shard_map/ppermute | solution.py:631
  170.5 8.5 %collective-permute-start.30 = (bf16[1,128,512]{2,1,0:T(8,128)(2,1)S(1)}, bf16[1,128,512]{2,1,0:T(8,128)(2,1)S(1)}, u32[]{:S(2)}, u32[]{:S(2)}) collective-permute-start(bf16[1,128,512]{2,1,0:T(8,128)(2,1)S(1)} %add_convert_fusion.10), channel_id=1, source_target_pairs={{0,8},{1,9},{2,10},{3,11},{4,12},{5,13},{6,14},{7,15},{8,0},{9,1},... | collective-permute-start | bytes 393224 | tf_op jit(solution)/shard_map/ppermute | solution.py:631
  172.8 10.5 %collective-permute-start.29 = (bf16[1,128,512]{2,1,0:T(8,128)(2,1)S(1)}, bf16[1,128,512]{2,1,0:T(8,128)(2,1)S(1)}, u32[]{:S(2)}, u32[]{:S(2)}) collective-permute-start(bf16[1,128,512]{2,1,0:T(8,128)(2,1)S(1)} %add_convert_fusion.10), channel_id=1, source_target_pairs={{0,16},{1,17},{2,18},{3,19},{4,20},{5,21},{6,22},{7,23},{8,24},{9,... | collective-permute-start | bytes 393224 | tf_op jit(solution)/shard_map/ppermute | solution.py:631
  183.2 7.0 %collective-permute-start.26 = (bf16[1,80,512]{2,1,0:T(8,128)(2,1)S(1)}, bf16[1,80,512]{2,1,0:T(8,128)(2,1)S(1)}, u32[]{:S(2)}, u32[]{:S(2)}) collective-permute-start(bf16[1,80,512]{2,1,0:T(8,128)(2,1)S(1)} %get-tuple-element.333), channel_id=1, source_target_pairs={{0,16},{1,17},{2,18},{3,19},{4,20},{5,21},{6,22},{7,23},{8,24},{9,... | collective-permute-start | bytes 245768 | tf_op jit(solution)/shard_map/ppermute | solution.py:631
  183.2 7.0 %collective-permute-start.27 = (bf16[1,80,512]{2,1,0:T(8,128)(2,1)S(1)}, bf16[1,80,512]{2,1,0:T(8,128)(2,1)S(1)}, u32[]{:S(2)}, u32[]{:S(2)}) collective-permute-start(bf16[1,80,512]{2,1,0:T(8,128)(2,1)S(1)} %get-tuple-element.334), channel_id=1, source_target_pairs={{0,8},{1,9},{2,10},{3,11},{4,12},{5,13},{6,14},{7,15},{8,0},{9,1},... | collective-permute-start | bytes 245768 | tf_op jit(solution)/shard_map/ppermute | solution.py:631
  185.9 6.3 %collective-permute-start.28 = (bf16[1,80,512]{2,1,0:T(8,128)(2,1)S(1)}, bf16[1,80,512]{2,1,0:T(8,128)(2,1)S(1)}, u32[]{:S(2)}, u32[]{:S(2)}) collective-permute-start(bf16[1,80,512]{2,1,0:T(8,128)(2,1)S(1)} %get-tuple-element.335), channel_id=1, source_target_pairs={{0,24},{1,25},{2,26},{3,27},{4,28},{5,29},{6,30},{7,31},{8,16},{9,... | collective-permute-start | bytes 245768 | tf_op jit(solution)/shard_map/ppermute | solution.py:631
  192.3 39.5 %copy-start = (s32[33]{0:T(128)S(1)}, s32[33]{0:T(128)}, u32[]{:S(2)}) copy-start(s32[33]{0:T(128)} %dynamic-slice_bitcast_fusion.refs_1_) | copy-start | bytes 400
  192.3 39.5 %copy-start.1 = (f32[8,128]{1,0:T(8,128)S(1)}, f32[8,128]{1,0:T(8,128)}, u32[]{:S(2)}) copy-start(f32[8,128]{1,0:T(8,128)} %get-tuple-element.382.refs_0_) | copy-start | bytes 12292
  192.3 6.8 %collective-permute-start.34 = (bf16[1,80,512]{2,1,0:T(8,128)(2,1)S(1)}, bf16[1,80,512]{2,1,0:T(8,128)(2,1)S(1)}, u32[]{:S(2)}, u32[]{:S(2)}) collective-permute-start(bf16[1,80,512]{2,1,0:T(8,128)(2,1)S(1)} %add_convert_fusion.14), channel_id=1, source_target_pairs={{0,24},{1,25},{2,26},{3,27},{4,28},{5,29},{6,30},{7,31},{8,16},{9,... | collective-permute-start | bytes 245768 | tf_op jit(solution)/shard_map/ppermute | solution.py:631
  194.2 5.7 %collective-permute-start.33 = (bf16[1,80,512]{2,1,0:T(8,128)(2,1)S(1)}, bf16[1,80,512]{2,1,0:T(8,128)(2,1)S(1)}, u32[]{:S(2)}, u32[]{:S(2)}) collective-permute-start(bf16[1,80,512]{2,1,0:T(8,128)(2,1)S(1)} %add_convert_fusion.14), channel_id=1, source_target_pairs={{0,8},{1,9},{2,10},{3,11},{4,12},{5,13},{6,14},{7,15},{8,0},{9,1},... | collective-permute-start | bytes 245768 | tf_op jit(solution)/shard_map/ppermute | solution.py:631
  194.4 7.8 %collective-permute-start.32 = (bf16[1,80,512]{2,1,0:T(8,128)(2,1)S(1)}, bf16[1,80,512]{2,1,0:T(8,128)(2,1)S(1)}, u32[]{:S(2)}, u32[]{:S(2)}) collective-permute-start(bf16[1,80,512]{2,1,0:T(8,128)(2,1)S(1)} %add_convert_fusion.14), channel_id=1, source_target_pairs={{0,16},{1,17},{2,18},{3,19},{4,20},{5,21},{6,22},{7,23},{8,24},{9,... | collective-permute-start | bytes 245768 | tf_op jit(solution)/shard_map/ppermute | solution.py:631
  196.8 9.4 %collective-permute-start.36 = (bf16[4,128,512]{2,1,0:T(8,128)(2,1)S(1)}, bf16[4,128,512]{2,1,0:T(8,128)(2,1)S(1)}, u32[]{:S(2)}, u32[]{:S(2)}) collective-permute-start(bf16[4,128,512]{2,1,0:T(8,128)(2,1)S(1)} %pad_maximum_fusion.4), channel_id=1, source_target_pairs={{0,4},{1,3},{2,6},{3,1},{4,0},{5,7},{6,2},{7,5},{8,12},{9,11},{10,... | collective-permute-start | bytes 1572872 | tf_op jit(solution)/shard_map/ppermute | solution.py:631
  202.2 17.0 %collective-permute-start.40 = (bf16[8,192,512]{2,1,0:T(8,128)(2,1)S(1)}, bf16[8,192,512]{2,1,0:T(8,128)(2,1)S(1)}, u32[]{:S(2)}, u32[]{:S(2)}) collective-permute-start(bf16[8,192,512]{2,1,0:T(8,128)(2,1)S(1)} %pad_maximum_fusion.refs_2_), channel_id=1, source_target_pairs={{0,1},{1,0},{2,3},{3,2},{4,5},{5,4},{6,7},{7,6},{8,9},{9,8},{10,11... | collective-permute-start | bytes 4718600 | tf_op jit(solution)/shard_map/ppermute | solution.py:631
  202.3 16.9 %collective-permute-start.41 = (bf16[8,192,512]{2,1,0:T(8,128)(2,1)S(1)}, bf16[8,192,512]{2,1,0:T(8,128)(2,1)S(1)}, u32[]{:S(2)}, u32[]{:S(2)}) collective-permute-start(bf16[8,192,512]{2,1,0:T(8,128)(2,1)S(1)} %collective-permute-done.37.refs_3_), channel_id=1, source_target_pairs={{0,1},{1,0},{2,3},{3,2},{4,5},{5,4},{6,7},{7,6},{8,9},{9,8},{10,11... | collective-permute-start | bytes 4718600 | tf_op jit(solution)/shard_map/ppermute | solution.py:631
  206.3 15.5 %collective-permute-start.39 = (bf16[8,128,512]{2,1,0:T(8,128)(2,1)S(1)}, bf16[8,128,512]{2,1,0:T(8,128)(2,1)S(1)}, u32[]{:S(2)}, u32[]{:S(2)}) collective-permute-start(bf16[8,128,512]{2,1,0:T(8,128)(2,1)S(1)} %pad_maximum_fusion.1.refs_2_), channel_id=1, source_target_pairs={{0,2},{1,5},{2,0},{3,7},{4,6},{5,1},{6,4},{7,3},{8,10},{9,13},{10,... | collective-permute-start | bytes 3145736 | tf_op jit(solution)/shard_map/ppermute | solution.py:631
  206.9 10.6 %collective-permute-start.35 = (bf16[4,80,512]{2,1,0:T(8,128)(2,1)S(1)}, bf16[4,80,512]{2,1,0:T(8,128)(2,1)S(1)}, u32[]{:S(2)}, u32[]{:S(2)}) collective-permute-start(bf16[4,80,512]{2,1,0:T(8,128)(2,1)S(1)} %pad_maximum_fusion.5), channel_id=1, source_target_pairs={{0,4},{1,3},{2,6},{3,1},{4,0},{5,7},{6,2},{7,5},{8,12},{9,11},{10,... | collective-permute-start | bytes 983048 | tf_op jit(solution)/shard_map/ppermute | solution.py:631
  217.6 11.2 %collective-permute-start.38 = (bf16[8,80,512]{2,1,0:T(8,128)(2,1)S(1)}, bf16[8,80,512]{2,1,0:T(8,128)(2,1)S(1)}, u32[]{:S(2)}, u32[]{:S(2)}) collective-permute-start(bf16[8,80,512]{2,1,0:T(8,128)(2,1)S(1)} %pad_maximum_fusion.3.refs_2_), channel_id=1, source_target_pairs={{0,2},{1,5},{2,0},{3,7},{4,6},{5,1},{6,4},{7,3},{8,10},{9,13},{10,... | collective-permute-start | bytes 1966088 | tf_op jit(solution)/shard_map/ppermute | solution.py:631
  221.8 8.2 %collective-permute-start.44 = (bf16[8,128,512]{2,1,0:T(8,128)(2,1)S(1)}, bf16[8,128,512]{2,1,0:T(8,128)(2,1)S(1)}, u32[]{:S(2)}, u32[]{:S(2)}) collective-permute-start(bf16[8,128,512]{2,1,0:T(8,128)(2,1)S(1)} %pad_maximum_fusion.1.refs_2_), channel_id=1, source_target_pairs={{0,1},{1,0},{2,3},{3,2},{4,5},{5,4},{6,7},{7,6},{8,9},{9,8},{10,11... | collective-permute-start | bytes 3145736 | tf_op jit(solution)/shard_map/ppermute | solution.py:631
  221.8 8.2 %collective-permute-start.45 = (bf16[8,128,512]{2,1,0:T(8,128)(2,1)S(1)}, bf16[8,128,512]{2,1,0:T(8,128)(2,1)S(1)}, u32[]{:S(2)}, u32[]{:S(2)}) collective-permute-start(bf16[8,128,512]{2,1,0:T(8,128)(2,1)S(1)} %collective-permute-done.39.refs_3_), channel_id=1, source_target_pairs={{0,1},{1,0},{2,3},{3,2},{4,5},{5,4},{6,7},{7,6},{8,9},{9,8},{10,11... | collective-permute-start | bytes 3145736 | tf_op jit(solution)/shard_map/ppermute | solution.py:631
  228.8 2.1 collective-permute-start.42
  228.8 3.0 %collective-permute-start.43 = (bf16[8,80,512]{2,1,0:T(8,128)(2,1)S(1)}, bf16[8,80,512]{2,1,0:T(8,128)(2,1)S(1)}, u32[]{:S(2)}, u32[]{:S(2)}) collective-permute-start(bf16[8,80,512]{2,1,0:T(8,128)(2,1)S(1)} %collective-permute-done.38.refs_3_), channel_id=1, source_target_pairs={{0,1},{1,0},{2,3},{3,2},{4,5},{5,4},{6,7},{7,6},{8,9},{9,8},{10,11... | collective-permute-start | bytes 1966088 | tf_op jit(solution)/shard_map/ppermute | solution.py:631
  (5 other events, 69.5 us)

commit v3 on v2

--- a/solution.py
+++ b/solution.py
@@ -22,6 +22,10 @@
 ANY = pl.BlockSpec(memory_space=pl.ANY)
 SMEM = pl.BlockSpec(memory_space=pltpu.SMEM)
 VMEM = pl.BlockSpec(memory_space=pltpu.VMEM)
+PLAN = (
+    "attention", "q", "feed", "q", "back", "q+f", "f", "q", "a", "f", "q", "a", "f", "q", "a", "f",
+    "a", "a", "q", "f", "a", "q", "place_q", "f", "a", "f", "place_f", "a",
+)
 SMALL = ("b_query", "b_value", "b_out", "gain_one", "shift_one", "b_down", "gain_two", "shift_two")
 NSMALL = 12
 
@@ -662,6 +666,21 @@
         out[i * m : (i + 1) * m] = part[...]
 
 
+def joined(order, pieces, limit=24):
+    m, rows, width = pieces[0].shape
+    count = len(pieces)
+    return order(
+        join_kernel,
+        *pieces,
+        name="join",
+        in_specs=[VMEM] * count,
+        out_specs=[VMEM],
+        out_shape=[shape((count * m, rows, width), B16)],
+        compiler_params=params(limit),
+        cost_estimate=SHORT,
+    )
+
+
 class Order:
     def __init__(self):
         self.token = None
@@ -696,6 +715,7 @@
         self.halving, self.doubling = list(halving), list(doubling)
         self.parts, self.m, self.pieces = [keep], keep.shape[0], None
         self.got, self.out, self.now = None, [send], self.halving.pop(0)
+        self.going = True
 
     def start(self):
         masks = partners(self.now)
@@ -728,61 +748,59 @@
         return True
 
 
-def tail_order(sums, ready):
-    unit, x_y, z = 23.3, "xy", "z"
-
-    def durations(item, units):
-        left = []
-        size = item.m / item.n
-        for step in item.halving:
-            size /= 2 ** len(step)
-            left.append((z, 4 * size) if len(step) == 2 else (x_y, size))
-        size = 1 / item.n
-        for step in reversed(item.doubling):
-            left.append((z, 4 * size) if len(step) == 2 else (x_y, size))
-            size *= 2 ** len(step)
-        left[-1] = ("core", left[-1][1] / 3)
-        return [(kind, d * units * unit) for kind, d in left]
-
-    todo = {k: durations(*v) for k, v in sums.items()}
-    done_at = dict(ready)
-    busy = {x_y: 0.0, z: 0.0, "core": 0.0}
-    now, order = 0.0, []
-    going = set(todo)
-    while going:
-        here = [k for k in going if done_at[k] <= now]
-        if not here:
-            now = min(done_at[k] for k in going)
-            continue
-        k = max(here, key=lambda k: sum(d for _, d in todo[k]) + 3 * len(todo[k]))
-        order.append(k)
-        if not todo[k]:
-            going.remove(k)
-            continue
-        kind, d = todo[k].pop(0)
-        now += 5.0 if kind == z else 3.0
-        start = max(now, busy[kind])
-        busy[kind] = done_at[k] = start + d
-    return order
-
-
-def advance(order, sums, starting=()):
-    flat = [x for s in sums for x in s.got]
-    if flat:
-        flat = order.fence(flat)
-    for s in sums:
-        s.got, flat = flat[: len(s.got)], flat[len(s.got) :]
-    for s in sums:
-        s.going = s.take()
-    going = [s for s in sums if s.going] + list(starting)
-    if not going:
-        return
-    flat = order.fence([x for s in going for x in s.out])
-    for s in going:
-        s.out, flat = flat[: len(s.out)], flat[len(s.out) :]
-        if s.pieces is not None:
-            s.pieces = s.out
-        s.start()
+class Plan:
+    def __init__(self, order):
+        self.order, self.sums, self.starting = order, {}, []
+        self.fresh = True
+
+    def add(self, name, item):
+        self.sums[name] = item
+        self.starting.append(item)
+
+    def flush(self):
+        if not self.starting:
+            return
+        flat = self.order.fence([x for s in self.starting for x in s.out])
+        for s in self.starting:
+            s.out, flat = flat[: len(s.out)], flat[len(s.out) :]
+            if s.pieces is not None:
+                s.pieces = s.out
+        for s in self.starting:
+            s.start()
+        self.starting = []
+
+    def step(self, names):
+        if not self.fresh:
+            self.flush()
+        items = [self.sums[name] for name in names if self.sums[name].going]
+        flat = self.order.fence([x for s in items for x in s.got])
+        for s in items:
+            s.got, flat = flat[: len(s.got)], flat[len(s.got) :]
+        for s in items:
+            s.going = s.take()
+            if s.going:
+                self.starting.append(s)
+        self.fresh = False
+
+    def run(self, names, kernels, places):
+        for name in names:
+            if name in kernels:
+                self.flush()
+                kernels[name]()
+                self.fresh = True
+            elif name in places:
+                self.flush()
+                if not self.sums[name[-1]].going:
+                    places.pop(name)()
+            else:
+                self.step(name.split("+"))
+        while any(s.going for s in self.sums.values()):
+            for name, item in self.sums.items():
+                if item.going:
+                    self.step([name])
+        self.flush()
+        for place in places.values():
+            place()
 
 
 class Gather:
@@ -803,18 +821,7 @@
         ]
 
     def step(self):
-        m, rows, width = self.pieces[0].shape
-        count = len(self.pieces)
-        self.pieces = self.order(
-            join_kernel,
-            *self.order.fence(self.pieces),
-            name="join",
-            in_specs=[VMEM] * count,
-            out_specs=[VMEM],
-            out_shape=[shape((count * m, rows, width), B16)],
-            compiler_params=params(62),
-            cost_estimate=SHORT,
-        )
+        self.pieces = joined(self.order, self.order.fence(self.pieces), 62)
         self.issue()
 
     def result(self):
@@ -1007,10 +1014,12 @@
         cost_estimate=LONG,
     )
     steps = steps_of(plane, pairs)
-    q_sum = Sum(order, steps, steps, n, q_keep, q_send)
-    advance(order, [], [q_sum])
-    p_probs, p_att, p_first = attention(2, 2, part)
-    advance(order, [q_sum])
+    plan = Plan(order)
+    plan.add("q", Sum(order, steps, steps, n, q_keep, q_send))
+    r = {}
+
+    def run_attention():
+        r["p_probs"], r["p_att"], r["p_first"] = attention(2, 2, part)
 
     parts_of = 2
     two = (pr // parts_of, h)
@@ -1018,62 +1027,63 @@
     def rows_at(width):
         return pl.BlockSpec((pr // parts_of, width), lambda b: (jnp.minimum(b, parts_of - 1), 0))
 
-    p_out, d_first, small_p, f_keep, f_send = order(
-        functools.partial(passage_feed_kernel, parts_of),
-        table, d_cls_p, p_cot, p_first, g1, s1, bu, bd, g2, s2, wu, wd,
-        name="passage_feed",
-        grid=(parts_of + 2,),
-        in_specs=[SMEM, whole(8, h), rows_at(h), rows_at(h), one, one, wide, one, one, one, ANY, ANY],
-        out_specs=[rows_at(h), rows_at(h), whole(16, h), ANY, ANY],
-        out_shape=[shape((pr, h), B16), shape((pr, h)), shape((16, h))]
-        + [shape((half, 2 * rows, h), B16)] * 2,
-        scratch_shapes=[
-            pltpu.VMEM((h, ff), B16),
-            pltpu.VMEM((ff, h), B16),
-            pltpu.VMEM((pr // parts_of, ff), F32),
-            pltpu.VMEM((pr, ff), B16),
-            pltpu.VMEM((pr, ff), B16),
-            pltpu.VMEM((pr, h), B16),
-            pltpu.VMEM((pr, h), B16),
-            pltpu.VMEM((ff, h), B16),
-            pltpu.VMEM((h, ff), B16),
-            sem(2),
-            sem(2),
-        ],
-        compiler_params=params(62),
-        cost_estimate=LONG,
-    )
-    f_sum = Sum(order, steps, steps, n, f_keep, f_send)
-    advance(order, [q_sum], [f_sum])
-    p_grad, a_keep, a_send = order(
-        passage_attention_back_kernel,
-        table, small_q, small_p, d_first, pq, pk, pv, p_probs, p_x, p_att, wq, wk, wv, wo,
-        name="passage_attention_back",
-        grid=(pn,),
-        in_specs=[SMEM, whole(16, h), whole(16, h)] + [seq_block] * 4
-        + [pl.BlockSpec(probs_block, lambda b: (b, 0, 0, 0))] + [ANY] * 6,
-        out_specs=[seq_block, ANY, ANY],
-        out_shape=[shape((pr, h))] + [shape((half, rows + 16, h), B16)] * 2,
-        scratch_shapes=[
-            pltpu.VMEM((3, h, h), B16),
-            pltpu.VMEM((h, h), B16),
-            pltpu.VMEM((pr, h), B16),
-            pltpu.VMEM((pr, h), B16),
-            pltpu.VMEM((4, pr, h), B16),
-            pltpu.VMEM((16, h), F32),
-            pltpu.VMEM((n, 16, h), B16),
-            pltpu.VMEM((4 * h, h), B16),
-            sem(6),
-            sem(2),
-        ],
-        compiler_params=params(62),
-        cost_estimate=LONG,
-    )
-    a_sum = Sum(order, steps, steps, n, a_keep, a_send)
-    advance(order, [q_sum, f_sum], [a_sum])
+    def run_feed():
+        r["p_out"], r["d_first"], r["small_p"], *out = order(
+            functools.partial(passage_feed_kernel, parts_of),
+            table, d_cls_p, p_cot, r["p_first"], g1, s1, bu, bd, g2, s2, wu, wd,
+            name="passage_feed",
+            grid=(parts_of + 2,),
+            in_specs=[SMEM, whole(8, h), rows_at(h), rows_at(h), one, one, wide, one, one, one, ANY, ANY],
+            out_specs=[rows_at(h), rows_at(h), whole(16, h), ANY, ANY],
+            out_shape=[shape((pr, h), B16), shape((pr, h)), shape((16, h))]
+            + [shape((half, 2 * rows, h), B16)] * 2,
+            scratch_shapes=[
+                pltpu.VMEM((h, ff), B16),
+                pltpu.VMEM((ff, h), B16),
+                pltpu.VMEM((pr // parts_of, ff), F32),
+                pltpu.VMEM((pr, ff), B16),
+                pltpu.VMEM((pr, ff), B16),
+                pltpu.VMEM((pr, h), B16),
+                pltpu.VMEM((pr, h), B16),
+                pltpu.VMEM((ff, h), B16),
+                pltpu.VMEM((h, ff), B16),
+                sem(2),
+                sem(2),
+            ],
+            compiler_params=params(62),
+            cost_estimate=LONG,
+        )
+        plan.add("f", Sum(order, steps, steps, n, *out))
+
+    def run_back():
+        r["p_grad"], *out = order(
+            passage_attention_back_kernel,
+            table, small_q, r["small_p"], r["d_first"], pq, pk, pv, r["p_probs"], p_x, r["p_att"], wq, wk, wv, wo,
+            name="passage_attention_back",
+            grid=(pn,),
+            in_specs=[SMEM, whole(16, h), whole(16, h)] + [seq_block] * 4
+            + [pl.BlockSpec(probs_block, lambda b: (b, 0, 0, 0))] + [ANY] * 6,
+            out_specs=[seq_block, ANY, ANY],
+            out_shape=[shape((pr, h))] + [shape((half, rows + 16, h), B16)] * 2,
+            scratch_shapes=[
+                pltpu.VMEM((3, h, h), B16),
+                pltpu.VMEM((h, h), B16),
+                pltpu.VMEM((pr, h), B16),
+                pltpu.VMEM((pr, h), B16),
+                pltpu.VMEM((4, pr, h), B16),
+                pltpu.VMEM((16, h), F32),
+                pltpu.VMEM((n, 16, h), B16),
+                pltpu.VMEM((4 * h, h), B16),
+                sem(6),
+                sem(2),
+            ],
+            compiler_params=params(62),
+            cost_estimate=LONG,
+        )
+        plan.add("a", Sum(order, steps, steps, n, *out))
 
     def place(e, kinds, which, before, with_small):
-        pieces = which.pieces
+        pieces = plan.sums[which].pieces
         starts, at = [], 0
         for piece in pieces:
             starts.append(at)
@@ -1100,20 +1110,26 @@
             cost_estimate=SHORT,
         )
 
-    for name in tail_order(
-        {"q": (q_sum, 3), "f": (f_sum, 2), "a": (a_sum, 1.25)}, {"q": 10.0, "f": 10.0, "a": 12.0}
-    ):
-        advance(order, [{"q": q_sum, "f": f_sum, "a": a_sum}[name]])
-    down, up, gq, gk, gv, go = place(0, ("down", "up", "att"), q_sum, [], False)
-    down, up = place(1, ("down", "up"), f_sum, [down, up], False)
-    gq, gk, gv, go, *smalls = place(1, ("att",), a_sum, [gq, gk, gv, go], True)
+    def place_q():
+        r["q_down"], r["q_up"], *r["q_att"] = place(0, ("down", "up", "att"), "q", [], False)
+
+    def place_f():
+        r["down"], r["up"] = place(1, ("down", "up"), "f", [r["q_down"], r["q_up"]], False)
+
+    def place_a():
+        r["att"] = place(1, ("att",), "a", r["q_att"], True)
+
+    kernels = {"attention": run_attention, "feed": run_feed, "back": run_back}
+    plan.run(PLAN, kernels, {"place_q": place_q, "place_f": place_f, "place_a": place_a})
+    down, up = r["down"], r["up"]
+    gq, gk, gv, go, *smalls = r["att"]
     sbq, sbv, sbo, sg1, ss1, sbd, sg2, ss2, sbu = smalls
     return (
         q_out.reshape(qn, ql, h),
-        p_out.reshape(pn, plen, h),
+        r["p_out"].reshape(pn, plen, h),
         terms[:qn, 0],
         q_grad.reshape(qn, ql, h),
-        p_grad.reshape(pn, plen, h),
+        r["p_grad"].reshape(pn, plen, h),
         gq, sbq, gk, gv, sbv, go, sbo, sg1, ss1, up, sbu, down, sbd, sg2, ss2,
     )
 

time: 248 us -> 242 us (0.976)
  waiting for transfers between devices: 74 us -> 66.6 us
    ppermute x39, waiting for transfers between devices: 73.4 us -> 65.1 us  [exchange(): return lax.ppermute(x, AXES, [(d, d ^ masks[d & 1]) for d in range(n)])]
  transfers between devices with their start and end apart: 46 -> 46, of which waited for: 21 -> 18; matrix products, arithmetic and copies ran while one was open for 3% -> 3% of each run, Pallas kernels for 24% -> 28%
where the time goes in v3:
time: 242 us; the launch traced here: 238 us
  Pallas kernels  97.4 us (40%)
  waiting for transfers between devices  66.6 us (28%)
  starting transfers between devices  53.6 us (22%)
  other arithmetic  16 us (7%)
  local copies, waits for them, and re-layouts  2.78 us (1%)
    pallas_call x12, Pallas kernels, __call__(): *outs, self.token = call(*([self.token] if skip else []), *operands)  97.4 us
    ppermute x39, waiting for transfers between devices, exchange(): return lax.ppermute(x, AXES, [(d, d ^ masks[d & 1]) for d in range(n)])  65.1 us
    ppermute x39, starting transfers between devices, exchange(): return lax.ppermute(x, AXES, [(d, d ^ masks[d & 1]) for d in range(n)])  44.4 us
    convert_element_type x12, other arithmetic, total(): return sum((p.astype(F32) for p in parts)).astype(B16)  15.5 us
    ppermute x7, starting transfers between devices, issue(): lax.ppermute(mine, AXES, [(d, d ^ m) for d in range(self.n)])  9.17 us
  transfers between devices with their start and end apart: 46, of which 18 were waited for; matrix products, arithmetic and copies ran while one was open for 3% of the time, Pallas kernels for 28%

profile of v3, /device:TPU:0, one launch (start us, length us, event | category | flops | bytes accessed | tf_op | source)
XLA Modules:
  0.0 237.8 jit_solution(170328001789382426)
XLA Ops:
  0.7 10.2 %front.1 = (bf16[1024,512]{1,0:T(8,128)(2,1)}, bf16[1024,512]{1,0:T(8,128)(2,1)}, bf16[1024,512]{1,0:T(8,128)(2,1)}, bf16[256,512]{1,0:T(8,128)(2,1)}, bf16[256,...) custom-call(s32[4,4]{1,0:T(4,128)} %refs_0_.1, s32[4]{0:T(128)} %refs_1_.1, ...), custom_call_target="tpu_custom_call" | custom-call | flops 199999995904 | bytes 1000 | tf_op jit(solution)/shard_map/front/pallas_call | solution.py:708
  10.8 4.1 %collective-permute-start = (bf16[1,16,512]{2,1,0:T(8,128)(2,1)}, bf16[1,16,512]{2,1,0:T(8,128)(2,1)}, u32[]{:S(2)}, u32[]{:S(2)}) collective-permute-start(bf16[1,16,512]{2,1,0:T(8,128)(2,1)} %bitcast.13), channel_id=1, source_target_pairs={{0,16},{1,17},{2,18},{3,19},{4,20},{5,21},{6,22},{7,23},{8,24},{9,... | collective-permute-start | bytes 49160 | tf_op jit(solution)/shard_map/ppermute | solution.py:820
  14.9 1.6 collective-permute-start.1
  16.5 6.4 %passage_attention.2 = (bf16[4,2,1024,256]{3,2,1,0:T(8,128)(2,1)}, bf16[1024,512]{1,0:T(8,128)(2,1)}, f32[1024,512]{1,0:T(8,128)}, f32[8,128]{1,0:T(8,128)}) custom-call(f32[8,128]{1,0:T(8,128)} %get-tuple-element.219.refs_0_, bf16[1024,512]{1,0:T(8,128)(2,1)} %get-tuple-element.220.refs_1_.refs_5_, bf16[1024,512]{1,0:T(8,128)(2,1)} %get-tuple-element.221.refs_2_.refs_6_, ...), custom_call_target="tpu_custom_call" | custom-call | flops 199999995904 | bytes 1000 | tf_op jit(solution)/shard_map/passage_attention/pallas_call | solution.py:708
  22.9 1.4 join.2
  24.3 1.7 collective-permute-start.3
  26.0 1.5 collective-permute-start.4
  27.8 4.2 %question_attention.1 = (bf16[2,1024,256]{2,1,0:T(8,128)(2,1)}, bf16[256,512]{1,0:T(8,128)(2,1)}, f32[256,512]{1,0:T(8,128)}, f32[8,128]{1,0:T(8,128)}) custom-call(f32[8,128]{1,0:T(8,128)} %get-tuple-element.230.refs_0_, bf16[256,512]{1,0:T(8,128)(2,1)} %get-tuple-element.231.refs_1_.refs_6_, bf16[256,512]{1,0:T(8,128)(2,1)} %get-tuple-element.232.refs_2_.refs_7_, ...), custom_call_target="tpu_custom_call" | custom-call | flops 199999995904 | bytes 1000 | tf_op jit(solution)/shard_map/question_attention/pallas_call | solution.py:708
  33.0 1.6 join.3
  37.1 13.9 %question_back.1 = (f32[8,128]{1,0:T(8,128)}, f32[8,512]{1,0:T(8,128)}, f32[256,512]{1,0:T(8,128)}, f32[16,512]{1,0:T(8,128)}, bf16[256,512]{1,0:T(8,128)(2,1)},...) custom-call(f32[8,128]{1,0:T(8,128)} %get-tuple-element.242.refs_0_, ...), custom_call_target="tpu_custom_call" | custom-call | flops 199999995904 | bytes 1000 | tf_op jit(solution)/shard_map/question_back/pallas_call | solution.py:708
  51.2 6.4 %passage_attention.3 = (bf16[4,2,1024,256]{3,2,1,0:T(8,128)(2,1)}, bf16[1024,512]{1,0:T(8,128)(2,1)}, f32[1024,512]{1,0:T(8,128)}, f32[8,128]{1,0:T(8,128)}) custom-call(f32[8,128]{1,0:T(8,128)} %get-tuple-element.253.refs_0_, bf16[1024,512]{1,0:T(8,128)(2,1)} %get-tuple-element.220.refs_1_.refs_5_, ...), custom_call_target="tpu_custom_call", output_to_operand_aliasing={{0}: (7, {}), {1}: (8, {}), {2}: (9, {})} | custom-call | flops 199999995904 | bytes 1000 | tf_op jit(solution)/shard_map/passage_attention/pallas_call | solution.py:708
  57.6 3.5 %add_convert_fusion = bf16[8,192,512]{2,1,0:T(8,128)(2,1)} fusion(bf16[16,192,512]{2,1,0:T(8,128)(2,1)} %collective-permute-done.7, bf16[16,192,512]{2,1,0:T(8,128)(2,1)} %get-tuple-element.249), kind=kLoop, calls=%fused_computation | loop fusion | flops 3145728 | bytes 4718592 | tf_op jit(solution)/shard_map/convert_element_type | solution.py:639
  61.8 24.5 %passage_feed.1 = (bf16[1024,512]{1,0:T(8,128)(2,1)}, f32[1024,512]{1,0:T(8,128)}, f32[16,512]{1,0:T(8,128)}, bf16[16,128,512]{2,1,0:T(8,128)(2,1)}, bf16[16,128,512]{2,1,0:T(8,128)(2,1)}, /*index=5*/f32[8,128]{1,0:T(8,128)}) custom-call(f32[8,128]{1,0:T(8,128)} %get-tuple-element.260.refs_0_, s32[33]{0:T(128)} %dynamic-slice_bitcast_fusion.refs_1_, ...), custom_call_target="tpu_custom_call" | custom-call | flops 199999995904 | bytes 1000 | tf_op jit(solution)/shard_map/passage_feed/pallas_call | solution.py:708
  86.3 2.8 %add_convert_fusion.2 = bf16[4,192,512]{2,1,0:T(8,128)(2,1)} fusion(bf16[8,192,512]{2,1,0:T(8,128)(2,1)} %collective-permute-done.8, bf16[16,192,512]{2,1,0:T(8,128)(2,1)} %collective-permute-done.7, bf16[16,192,512]{2,1,0:T(8,128)(2,1)} %get-tuple-element.249), kind=kLoop, calls=%fused_computation.3 | loop fusion | flops 2359296 | bytes 3145728 | tf_op jit(solution)/shard_map/convert_element_type | solution.py:639
  89.2 1.4 collective-permute-start.9
  90.6 16.8 %passage_attention_back.1 = (f32[1024,512]{1,0:T(8,128)}, bf16[16,80,512]{2,1,0:T(8,128)(2,1)}, bf16[16,80,512]{2,1,0:T(8,128)(2,1)}, f32[8,128]{1,0:T(8,128)}) custom-call(f32[8,128]{1,0:T(8,128)} %get-tuple-element.271.refs_0_, s32[33]{0:T(128)} %dynamic-slice_bitcast_fusion.refs_1_, f32[16,512]{1,0:T(8,128)} %get-tuple-element.272.refs_2_, ...), custom_call_target="tpu_custom_call" | custom-call | flops 199999995904 | bytes 1000 | tf_op jit(solution)/shard_map/passage_attention_back/pallas_call | solution.py:708
  107.4 2.1 add_convert_fusion.7
  109.8 1.6 add_convert_fusion.1
  112.1 1.7 collective-permute-start.12
  113.8 2.5 %collective-permute-start.13 = (bf16[1,192,512]{2,1,0:T(8,128)(2,1)S(1)}, bf16[1,192,512]{2,1,0:T(8,128)(2,1)S(1)}, u32[]{:S(2)}, u32[]{:S(2)}) collective-permute-start(bf16[1,192,512]{2,1,0:T(8,128)(2,1)S(1)} %get-tuple-element.289), channel_id=1, source_target_pairs={{0,8},{1,9},{2,10},{3,11},{4,12},{5,13},{6,14},{7,15},{8,0},{9,1},... | collective-permute-start | bytes 589832 | tf_op jit(solution)/shard_map/ppermute | solution.py:635
  116.5 9.8 %collective-permute-done.15 = bf16[8,128,512]{2,1,0:T(8,128)(2,1)S(1)} collective-permute-done((bf16[8,128,512]{2,1,0:T(8,128)(2,1)S(1)}, bf16[8,128,512]{2,1,0:T(8,128)(2,1)S(1)}, u32[]{:S(2)}, u32[]{:S(2)}) %collective-permute-start.15) | collective-permute-done | bytes 1048608 | tf_op jit(solution)/shard_map/ppermute | solution.py:635
  127.6 2.3 collective-permute-done.14
  129.9 1.5 collective-permute-start.20
  131.4 1.4 add_convert_fusion.6
  132.8 4.9 %collective-permute-start.17 = (bf16[1,192,512]{2,1,0:T(8,128)(2,1)S(1)}, bf16[1,192,512]{2,1,0:T(8,128)(2,1)S(1)}, u32[]{:S(2)}, u32[]{:S(2)}) collective-permute-start(bf16[1,192,512]{2,1,0:T(8,128)(2,1)S(1)} %add_convert_fusion.6), channel_id=1, source_target_pairs={{0,16},{1,17},{2,18},{3,19},{4,20},{5,21},{6,22},{7,23},{8,24},{9,... | collective-permute-start | bytes 589832 | tf_op jit(solution)/shard_map/ppermute | solution.py:635
  137.7 1.5 collective-permute-start.19
  141.3 10.4 %collective-permute-done.17 = bf16[1,192,512]{2,1,0:T(8,128)(2,1)S(1)} collective-permute-done((bf16[1,192,512]{2,1,0:T(8,128)(2,1)S(1)}, bf16[1,192,512]{2,1,0:T(8,128)(2,1)S(1)}, u32[]{:S(2)}, u32[]{:S(2)}) %collective-permute-start.17) | collective-permute-done | bytes 196640 | tf_op jit(solution)/shard_map/ppermute | solution.py:635
  152.5 3.4 %collective-permute-start.23 = (bf16[1,128,512]{2,1,0:T(8,128)(2,1)S(1)}, bf16[1,128,512]{2,1,0:T(8,128)(2,1)S(1)}, u32[]{:S(2)}, u32[]{:S(2)}) collective-permute-start(bf16[1,128,512]{2,1,0:T(8,128)(2,1)S(1)} %get-tuple-element.319), channel_id=1, source_target_pairs={{0,16},{1,17},{2,18},{3,19},{4,20},{5,21},{6,22},{7,23},{8,24},{9,... | collective-permute-start | bytes 393224 | tf_op jit(solution)/shard_map/ppermute | solution.py:635
  156.5 2.4 collective-permute-start.25
  159.0 1.5 collective-permute-done.23
  161.8 5.3 %collective-permute-done.25 = bf16[1,128,512]{2,1,0:T(8,128)(2,1)S(1)} collective-permute-done((bf16[1,128,512]{2,1,0:T(8,128)(2,1)S(1)}, bf16[1,128,512]{2,1,0:T(8,128)(2,1)S(1)}, u32[]{:S(2)}, u32[]{:S(2)}) %collective-permute-start.25) | collective-permute-done | bytes 131104 | tf_op jit(solution)/shard_map/ppermute | solution.py:635
  168.3 1.5 collective-permute-start.37
  170.4 2.1 collective-permute-start.29
  172.5 2.3 collective-permute-start.31
  174.8 5.7 %collective-permute-done.21 = bf16[4,80,512]{2,1,0:T(8,128)(2,1)S(1)} collective-permute-done((bf16[4,80,512]{2,1,0:T(8,128)(2,1)S(1)}, bf16[4,80,512]{2,1,0:T(8,128)(2,1)S(1)}, u32[]{:S(2)}, u32[]{:S(2)}) %collective-permute-start.21) | collective-permute-done | bytes 327712 | tf_op jit(solution)/shard_map/ppermute | solution.py:635
  182.3 2.8 %collective-permute-start.26 = (bf16[1,80,512]{2,1,0:T(8,128)(2,1)S(1)}, bf16[1,80,512]{2,1,0:T(8,128)(2,1)S(1)}, u32[]{:S(2)}, u32[]{:S(2)}) collective-permute-start(bf16[1,80,512]{2,1,0:T(8,128)(2,1)S(1)} %get-tuple-element.333), channel_id=1, source_target_pairs={{0,16},{1,17},{2,18},{3,19},{4,20},{5,21},{6,22},{7,23},{8,24},{9,... | collective-permute-start | bytes 245768 | tf_op jit(solution)/shard_map/ppermute | solution.py:635
  185.2 1.9 collective-permute-start.28
  187.2 3.8 %collective-permute-done.26 = bf16[1,80,512]{2,1,0:T(8,128)(2,1)S(1)} collective-permute-done((bf16[1,80,512]{2,1,0:T(8,128)(2,1)S(1)}, bf16[1,80,512]{2,1,0:T(8,128)(2,1)S(1)}, u32[]{:S(2)}, u32[]{:S(2)}) %collective-permute-start.26) | collective-permute-done | bytes 81952 | tf_op jit(solution)/shard_map/ppermute | solution.py:635
  192.1 1.6 collective-permute-start.32
  194.5 2.0 collective-permute-start.34
  197.9 2.2 collective-permute-done.32
  201.6 4.5 %collective-permute-done.36 = bf16[4,128,512]{2,1,0:T(8,128)(2,1)S(1)} collective-permute-done((bf16[4,128,512]{2,1,0:T(8,128)(2,1)S(1)}, bf16[4,128,512]{2,1,0:T(8,128)(2,1)S(1)}, u32[]{:S(2)}, u32[]{:S(2)}) %collective-permute-start.36) | collective-permute-done | bytes 524320 | tf_op jit(solution)/shard_map/ppermute | solution.py:635
  206.3 1.5 collective-permute-start.39
  208.2 10.3 %collective-permute-done.35 = bf16[4,80,512]{2,1,0:T(8,128)(2,1)S(1)} collective-permute-done((bf16[4,80,512]{2,1,0:T(8,128)(2,1)S(1)}, bf16[4,80,512]{2,1,0:T(8,128)(2,1)S(1)}, u32[]{:S(2)}, u32[]{:S(2)}) %collective-permute-start.35) | collective-permute-done | bytes 327712 | tf_op jit(solution)/shard_map/ppermute | solution.py:635
  219.2 5.1 %place.3 = (f32[2,2048,512]{2,1,0:T(8,128)}, f32[2,512,2048]{2,1,0:T(8,128)}, f32[2,512,512]{2,1,0:T(8,128)}, f32[2,512,512]{2,1,0:T(8,128)}, f32[2,512,512]{2,1...) custom-call(f32[8,128]{1,0:T(8,128)S(1)} %copy-done.1, s32[33]{0:T(128)S(1)} %copy-done, ...), custom_call_target="tpu_custom_call" | custom-call | flops 1000 | bytes 1000 | tf_op jit(solution)/shard_map/place/pallas_call | solution.py:708
  224.8 4.3 %collective-permute-done.38.refs_3_ = bf16[8,80,512]{2,1,0:T(8,128)(2,1)S(1)} collective-permute-done((bf16[8,80,512]{2,1,0:T(8,128)(2,1)S(1)}, bf16[8,80,512]{2,1,0:T(8,128)(2,1)S(1)}, u32[]{:S(2)}, u32[]{:S(2)}) %collective-permute-start.38) | collective-permute-done | bytes 655392 | tf_op jit(solution)/shard_map/ppermute | solution.py:635
  230.3 3.8 %place.4 = (f32[2,2048,512]{2,1,0:T(8,128)}, f32[2,512,2048]{2,1,0:T(8,128)}, f32[8,128]{1,0:T(8,128)S(1)}) custom-call(f32[8,128]{1,0:T(8,128)S(1)} %get-tuple-element.384.refs_0_, s32[33]{0:T(128)S(1)} %copy-done, bf16[8,128,512]{2,1,0:T(8,128)(2,1)S(1)} %pad_maximum_fusion.1.refs_2_, ...), custom_call_target="tpu_custom_call", output_to_operand_aliasing={{0}: (6, {}), {1}: (7, {})} | custom-call | flops 1000 | bytes 1000 | tf_op jit(solution)/shard_map/place/pallas_call | solution.py:708
  234.2 3.2 %place.5 = (f32[2,512,512]{2,1,0:T(8,128)}, f32[2,512,512]{2,1,0:T(8,128)}, f32[2,512,512]{2,1,0:T(8,128)}, f32[2,512,512]{2,1,0:T(8,128)}, f32[2,512]{1,0:T(2,1...) custom-call(f32[8,128]{1,0:T(8,128)S(1)} %get-tuple-element.390.refs, ...), custom_call_target="tpu_custom_call", output_to_operand_aliasing={{0}: (6, {}), {1}: (7, {}), {2}: (8, {}), {3}: (9, {})} | custom-call | flops 1000 | bytes 1000 | tf_op jit(solution)/shard_map/place/pallas_call | solution.py:708
  (90 shorter events, 23.5 us)
Async XLA Ops:
  10.8 12.1 %collective-permute-start = (bf16[1,16,512]{2,1,0:T(8,128)(2,1)}, bf16[1,16,512]{2,1,0:T(8,128)(2,1)}, u32[]{:S(2)}, u32[]{:S(2)}) collective-permute-start(bf16[1,16,512]{2,1,0:T(8,128)(2,1)} %bitcast.13), channel_id=1, source_target_pairs={{0,16},{1,17},{2,18},{3,19},{4,20},{5,21},{6,22},{7,23},{8,24},{9,... | collective-permute-start | bytes 49160 | tf_op jit(solution)/shard_map/ppermute | solution.py:820
  14.9 8.0 %collective-permute-start.1 = (bf16[1,16,512]{2,1,0:T(8,128)(2,1)}, bf16[1,16,512]{2,1,0:T(8,128)(2,1)}, u32[]{:S(2)}, u32[]{:S(2)}) collective-permute-start(bf16[1,16,512]{2,1,0:T(8,128)(2,1)} %bitcast.14), channel_id=1, source_target_pairs={{0,8},{1,9},{2,10},{3,11},{4,12},{5,13},{6,14},{7,15},{8,0},{9,1},... | collective-permute-start | bytes 49160 | tf_op jit(solution)/shard_map/ppermute | solution.py:820
  16.5 6.4 %collective-permute-start.2 = (bf16[1,16,512]{2,1,0:T(8,128)(2,1)}, bf16[1,16,512]{2,1,0:T(8,128)(2,1)}, u32[]{:S(2)}, u32[]{:S(2)}) collective-permute-start(bf16[1,16,512]{2,1,0:T(8,128)(2,1)} %bitcast.15), channel_id=1, source_target_pairs={{0,24},{1,25},{2,26},{3,27},{4,28},{5,29},{6,30},{7,31},{8,16},{9,... | collective-permute-start | bytes 49160 | tf_op jit(solution)/shard_map/ppermute | solution.py:820
  24.3 7.7 %collective-permute-start.3 = (bf16[4,16,512]{2,1,0:T(8,128)(2,1)}, bf16[4,16,512]{2,1,0:T(8,128)(2,1)}, u32[]{:S(2)}, u32[]{:S(2)}) collective-permute-start(bf16[4,16,512]{2,1,0:T(8,128)(2,1)} %get-tuple-element.236.refs_1_), channel_id=1, source_target_pairs={{0,4},{1,5},{2,6},{3,7},{4,0},{5,1},{6,2},{7,3},{8,12},{9,13},{10,... | collective-permute-start | bytes 196616 | tf_op jit(solution)/shard_map/ppermute | solution.py:820
  26.0 6.0 %collective-permute-start.4 = (bf16[4,16,512]{2,1,0:T(8,128)(2,1)}, bf16[4,16,512]{2,1,0:T(8,128)(2,1)}, u32[]{:S(2)}, u32[]{:S(2)}) collective-permute-start(bf16[4,16,512]{2,1,0:T(8,128)(2,1)} %get-tuple-element.236.refs_1_), channel_id=1, source_target_pairs={{0,2},{1,3},{2,0},{3,1},{4,6},{5,7},{6,4},{7,5},{8,10},{9,11},{10,... | collective-permute-start | bytes 196616 | tf_op jit(solution)/shard_map/ppermute | solution.py:820
  27.5 5.5 %collective-permute-start.5 = (bf16[4,16,512]{2,1,0:T(8,128)(2,1)}, bf16[4,16,512]{2,1,0:T(8,128)(2,1)}, u32[]{:S(2)}, u32[]{:S(2)}) collective-permute-start(bf16[4,16,512]{2,1,0:T(8,128)(2,1)} %get-tuple-element.236.refs_1_), channel_id=1, source_target_pairs={{0,6},{1,7},{2,4},{3,5},{4,2},{5,3},{6,0},{7,1},{8,14},{9,15},{10,... | collective-permute-start | bytes 196616 | tf_op jit(solution)/shard_map/ppermute | solution.py:820
  34.7 1.7 collective-permute-start.6
  51.0 6.6 %collective-permute-start.7 = (bf16[16,192,512]{2,1,0:T(8,128)(2,1)}, bf16[16,192,512]{2,1,0:T(8,128)(2,1)}, u32[]{:S(2)}, u32[]{:S(2)}) collective-permute-start(bf16[16,192,512]{2,1,0:T(8,128)(2,1)} %get-tuple-element.252), channel_id=1, source_target_pairs={{0,1},{1,0},{2,3},{3,2},{4,5},{5,4},{6,7},{7,6},{8,9},{9,8},{10,11... | collective-permute-start | bytes 9437192 | tf_op jit(solution)/shard_map/ppermute | solution.py:635
  61.1 25.2 %collective-permute-start.8 = (bf16[8,192,512]{2,1,0:T(8,128)(2,1)}, bf16[8,192,512]{2,1,0:T(8,128)(2,1)}, u32[]{:S(2)}, u32[]{:S(2)}) collective-permute-start(bf16[8,192,512]{2,1,0:T(8,128)(2,1)} %add_convert_fusion), channel_id=1, source_target_pairs={{0,2},{1,5},{2,0},{3,7},{4,6},{5,1},{6,4},{7,3},{8,10},{9,13},{10,... | collective-permute-start | bytes 4718600 | tf_op jit(solution)/shard_map/ppermute | solution.py:635
  89.1 18.3 %collective-permute-start.10 = (bf16[16,128,512]{2,1,0:T(8,128)(2,1)}, bf16[16,128,512]{2,1,0:T(8,128)(2,1)}, u32[]{:S(2)}, u32[]{:S(2)}) collective-permute-start(bf16[16,128,512]{2,1,0:T(8,128)(2,1)} %get-tuple-element.281), channel_id=1, source_target_pairs={{0,1},{1,0},{2,3},{3,2},{4,5},{5,4},{6,7},{7,6},{8,9},{9,8},{10,11... | collective-permute-start | bytes 6291464 | tf_op jit(solution)/shard_map/ppermute | solution.py:635
  89.2 18.2 %collective-permute-start.9 = (bf16[4,192,512]{2,1,0:T(8,128)(2,1)}, bf16[4,192,512]{2,1,0:T(8,128)(2,1)}, u32[]{:S(2)}, u32[]{:S(2)}) collective-permute-start(bf16[4,192,512]{2,1,0:T(8,128)(2,1)} %add_convert_fusion.2), channel_id=1, source_target_pairs={{0,4},{1,3},{2,6},{3,1},{4,0},{5,7},{6,2},{7,5},{8,12},{9,11},{10,... | collective-permute-start | bytes 2359304 | tf_op jit(solution)/shard_map/ppermute | solution.py:635
  111.4 27.8 %copy-start.3 = (bf16[16,80,512]{2,1,0:T(8,128)(2,1)S(1)}, bf16[16,80,512]{2,1,0:T(8,128)(2,1)}, u32[]{:S(2)}) copy-start(bf16[16,80,512]{2,1,0:T(8,128)(2,1)} %get-tuple-element.278) | copy-start | bytes 3932164
  111.4 14.9 %collective-permute-start.15 = (bf16[8,128,512]{2,1,0:T(8,128)(2,1)S(1)}, bf16[8,128,512]{2,1,0:T(8,128)(2,1)S(1)}, u32[]{:S(2)}, u32[]{:S(2)}) collective-permute-start(bf16[8,128,512]{2,1,0:T(8,128)(2,1)S(1)} %add_convert_fusion.1), channel_id=1, source_target_pairs={{0,2},{1,5},{2,0},{3,7},{4,6},{5,1},{6,4},{7,3},{8,10},{9,13},{10,... | collective-permute-start | bytes 3145736 | tf_op jit(solution)/shard_map/ppermute | solution.py:635
  112.1 27.1 %collective-permute-start.11 = (bf16[16,80,512]{2,1,0:T(8,128)(2,1)S(1)}, bf16[16,80,512]{2,1,0:T(8,128)(2,1)S(1)}, u32[]{:S(2)}, u32[]{:S(2)}) collective-permute-start(bf16[16,80,512]{2,1,0:T(8,128)(2,1)S(1)} %copy-done.5), channel_id=1, source_target_pairs={{0,1},{1,0},{2,3},{3,2},{4,5},{5,4},{6,7},{7,6},{8,9},{9,8},{10,11... | collective-permute-start | bytes 3932168 | tf_op jit(solution)/shard_map/ppermute | solution.py:635
  112.1 15.4 %collective-permute-start.12 = (bf16[1,192,512]{2,1,0:T(8,128)(2,1)S(1)}, bf16[1,192,512]{2,1,0:T(8,128)(2,1)S(1)}, u32[]{:S(2)}, u32[]{:S(2)}) collective-permute-start(bf16[1,192,512]{2,1,0:T(8,128)(2,1)S(1)} %get-tuple-element.288), channel_id=1, source_target_pairs={{0,16},{1,17},{2,18},{3,19},{4,20},{5,21},{6,22},{7,23},{8,24},{9,... | collective-permute-start | bytes 589832 | tf_op jit(solution)/shard_map/ppermute | solution.py:635
  113.8 13.7 %collective-permute-start.13 = (bf16[1,192,512]{2,1,0:T(8,128)(2,1)S(1)}, bf16[1,192,512]{2,1,0:T(8,128)(2,1)S(1)}, u32[]{:S(2)}, u32[]{:S(2)}) collective-permute-start(bf16[1,192,512]{2,1,0:T(8,128)(2,1)S(1)} %get-tuple-element.289), channel_id=1, source_target_pairs={{0,8},{1,9},{2,10},{3,11},{4,12},{5,13},{6,14},{7,15},{8,0},{9,1},... | collective-permute-start | bytes 589832 | tf_op jit(solution)/shard_map/ppermute | solution.py:635
  116.3 13.6 %collective-permute-start.14 = (bf16[1,192,512]{2,1,0:T(8,128)(2,1)S(1)}, bf16[1,192,512]{2,1,0:T(8,128)(2,1)S(1)}, u32[]{:S(2)}, u32[]{:S(2)}) collective-permute-start(bf16[1,192,512]{2,1,0:T(8,128)(2,1)S(1)} %get-tuple-element.290), channel_id=1, source_target_pairs={{0,24},{1,25},{2,26},{3,27},{4,28},{5,29},{6,30},{7,31},{8,16},{9,... | collective-permute-start | bytes 589832 | tf_op jit(solution)/shard_map/ppermute | solution.py:635
  129.9 10.2 %collective-permute-start.20 = (bf16[4,128,512]{2,1,0:T(8,128)(2,1)S(1)}, bf16[4,128,512]{2,1,0:T(8,128)(2,1)S(1)}, u32[]{:S(2)}, u32[]{:S(2)}) collective-permute-start(bf16[4,128,512]{2,1,0:T(8,128)(2,1)S(1)} %add_convert_fusion.4), channel_id=1, source_target_pairs={{0,4},{1,3},{2,6},{3,1},{4,0},{5,7},{6,2},{7,5},{8,12},{9,11},{10,... | collective-permute-start | bytes 1572872 | tf_op jit(solution)/shard_map/ppermute | solution.py:635
  132.8 18.8 %collective-permute-start.17 = (bf16[1,192,512]{2,1,0:T(8,128)(2,1)S(1)}, bf16[1,192,512]{2,1,0:T(8,128)(2,1)S(1)}, u32[]{:S(2)}, u32[]{:S(2)}) collective-permute-start(bf16[1,192,512]{2,1,0:T(8,128)(2,1)S(1)} %add_convert_fusion.6), channel_id=1, source_target_pairs={{0,16},{1,17},{2,18},{3,19},{4,20},{5,21},{6,22},{7,23},{8,24},{9,... | collective-permute-start | bytes 589832 | tf_op jit(solution)/shard_map/ppermute | solution.py:635
  137.7 13.9 %collective-permute-start.18 = (bf16[1,192,512]{2,1,0:T(8,128)(2,1)S(1)}, bf16[1,192,512]{2,1,0:T(8,128)(2,1)S(1)}, u32[]{:S(2)}, u32[]{:S(2)}) collective-permute-start(bf16[1,192,512]{2,1,0:T(8,128)(2,1)S(1)} %add_convert_fusion.6), channel_id=1, source_target_pairs={{0,8},{1,9},{2,10},{3,11},{4,12},{5,13},{6,14},{7,15},{8,0},{9,1},... | collective-permute-start | bytes 589832 | tf_op jit(solution)/shard_map/ppermute | solution.py:635
  137.7 13.9 %collective-permute-start.19 = (bf16[1,192,512]{2,1,0:T(8,128)(2,1)S(1)}, bf16[1,192,512]{2,1,0:T(8,128)(2,1)S(1)}, u32[]{:S(2)}, u32[]{:S(2)}) collective-permute-start(bf16[1,192,512]{2,1,0:T(8,128)(2,1)S(1)} %add_convert_fusion.6), channel_id=1, source_target_pairs={{0,24},{1,25},{2,26},{3,27},{4,28},{5,29},{6,30},{7,31},{8,16},{9,... | collective-permute-start | bytes 589832 | tf_op jit(solution)/shard_map/ppermute | solution.py:635
  139.4 19.5 %collective-permute-start.16 = (bf16[8,80,512]{2,1,0:T(8,128)(2,1)S(1)}, bf16[8,80,512]{2,1,0:T(8,128)(2,1)S(1)}, u32[]{:S(2)}, u32[]{:S(2)}) collective-permute-start(bf16[8,80,512]{2,1,0:T(8,128)(2,1)S(1)} %add_convert_fusion.3), channel_id=1, source_target_pairs={{0,2},{1,5},{2,0},{3,7},{4,6},{5,1},{6,4},{7,3},{8,10},{9,13},{10,... | collective-permute-start | bytes 1966088 | tf_op jit(solution)/shard_map/ppermute | solution.py:635
  151.8 16.4 %collective-permute-start.22 = (bf16[4,192,512]{2,1,0:T(8,128)(2,1)S(1)}, bf16[4,192,512]{2,1,0:T(8,128)(2,1)S(1)}, u32[]{:S(2)}, u32[]{:S(2)}) collective-permute-start(bf16[4,192,512]{2,1,0:T(8,128)(2,1)S(1)} %pad_maximum_fusion.2), channel_id=1, source_target_pairs={{0,4},{1,3},{2,6},{3,1},{4,0},{5,7},{6,2},{7,5},{8,12},{9,11},{10,... | collective-permute-start | bytes 2359304 | tf_op jit(solution)/shard_map/ppermute | solution.py:635
  152.5 8.0 %collective-permute-start.23 = (bf16[1,128,512]{2,1,0:T(8,128)(2,1)S(1)}, bf16[1,128,512]{2,1,0:T(8,128)(2,1)S(1)}, u32[]{:S(2)}, u32[]{:S(2)}) collective-permute-start(bf16[1,128,512]{2,1,0:T(8,128)(2,1)S(1)} %get-tuple-element.319), channel_id=1, source_target_pairs={{0,16},{1,17},{2,18},{3,19},{4,20},{5,21},{6,22},{7,23},{8,24},{9,... | collective-permute-start | bytes 393224 | tf_op jit(solution)/shard_map/ppermute | solution.py:635
  155.9 5.9 %collective-permute-start.24 = (bf16[1,128,512]{2,1,0:T(8,128)(2,1)S(1)}, bf16[1,128,512]{2,1,0:T(8,128)(2,1)S(1)}, u32[]{:S(2)}, u32[]{:S(2)}) collective-permute-start(bf16[1,128,512]{2,1,0:T(8,128)(2,1)S(1)} %get-tuple-element.320), channel_id=1, source_target_pairs={{0,8},{1,9},{2,10},{3,11},{4,12},{5,13},{6,14},{7,15},{8,0},{9,1},... | collective-permute-start | bytes 393224 | tf_op jit(solution)/shard_map/ppermute | solution.py:635
  156.5 10.6 %collective-permute-start.25 = (bf16[1,128,512]{2,1,0:T(8,128)(2,1)S(1)}, bf16[1,128,512]{2,1,0:T(8,128)(2,1)S(1)}, u32[]{:S(2)}, u32[]{:S(2)}) collective-permute-start(bf16[1,128,512]{2,1,0:T(8,128)(2,1)S(1)} %get-tuple-element.321), channel_id=1, source_target_pairs={{0,24},{1,25},{2,26},{3,27},{4,28},{5,29},{6,30},{7,31},{8,16},{9,... | collective-permute-start | bytes 393224 | tf_op jit(solution)/shard_map/ppermute | solution.py:635
  168.3 32.7 %collective-permute-start.37 = (bf16[8,192,512]{2,1,0:T(8,128)(2,1)S(1)}, bf16[8,192,512]{2,1,0:T(8,128)(2,1)S(1)}, u32[]{:S(2)}, u32[]{:S(2)}) collective-permute-start(bf16[8,192,512]{2,1,0:T(8,128)(2,1)S(1)} %pad_maximum_fusion.refs_2_), channel_id=1, source_target_pairs={{0,2},{1,5},{2,0},{3,7},{4,6},{5,1},{6,4},{7,3},{8,10},{9,13},{10,... | collective-permute-start | bytes 4718600 | tf_op jit(solution)/shard_map/ppermute | solution.py:635
  169.8 10.7 %collective-permute-start.21 = (bf16[4,80,512]{2,1,0:T(8,128)(2,1)S(1)}, bf16[4,80,512]{2,1,0:T(8,128)(2,1)S(1)}, u32[]{:S(2)}, u32[]{:S(2)}) collective-permute-start(bf16[4,80,512]{2,1,0:T(8,128)(2,1)S(1)} %add_convert_fusion.5), channel_id=1, source_target_pairs={{0,4},{1,3},{2,6},{3,1},{4,0},{5,7},{6,2},{7,5},{8,12},{9,11},{10,... | collective-permute-start | bytes 983048 | tf_op jit(solution)/shard_map/ppermute | solution.py:635
  170.4 11.6 %collective-permute-start.29 = (bf16[1,128,512]{2,1,0:T(8,128)(2,1)S(1)}, bf16[1,128,512]{2,1,0:T(8,128)(2,1)S(1)}, u32[]{:S(2)}, u32[]{:S(2)}) collective-permute-start(bf16[1,128,512]{2,1,0:T(8,128)(2,1)S(1)} %add_convert_fusion.10), channel_id=1, source_target_pairs={{0,16},{1,17},{2,18},{3,19},{4,20},{5,21},{6,22},{7,23},{8,24},{9,... | collective-permute-start | bytes 393224 | tf_op jit(solution)/shard_map/ppermute | solution.py:635
  172.5 9.8 %collective-permute-start.30 = (bf16[1,128,512]{2,1,0:T(8,128)(2,1)S(1)}, bf16[1,128,512]{2,1,0:T(8,128)(2,1)S(1)}, u32[]{:S(2)}, u32[]{:S(2)}) collective-permute-start(bf16[1,128,512]{2,1,0:T(8,128)(2,1)S(1)} %add_convert_fusion.10), channel_id=1, source_target_pairs={{0,8},{1,9},{2,10},{3,11},{4,12},{5,13},{6,14},{7,15},{8,0},{9,1},... | collective-permute-start | bytes 393224 | tf_op jit(solution)/shard_map/ppermute | solution.py:635
  172.5 9.8 %collective-permute-start.31 = (bf16[1,128,512]{2,1,0:T(8,128)(2,1)S(1)}, bf16[1,128,512]{2,1,0:T(8,128)(2,1)S(1)}, u32[]{:S(2)}, u32[]{:S(2)}) collective-permute-start(bf16[1,128,512]{2,1,0:T(8,128)(2,1)S(1)} %add_convert_fusion.10), channel_id=1, source_target_pairs={{0,24},{1,25},{2,26},{3,27},{4,28},{5,29},{6,30},{7,31},{8,16},{9,... | collective-permute-start | bytes 393224 | tf_op jit(solution)/shard_map/ppermute | solution.py:635
  182.3 8.7 %collective-permute-start.26 = (bf16[1,80,512]{2,1,0:T(8,128)(2,1)S(1)}, bf16[1,80,512]{2,1,0:T(8,128)(2,1)S(1)}, u32[]{:S(2)}, u32[]{:S(2)}) collective-permute-start(bf16[1,80,512]{2,1,0:T(8,128)(2,1)S(1)} %get-tuple-element.333), channel_id=1, source_target_pairs={{0,16},{1,17},{2,18},{3,19},{4,20},{5,21},{6,22},{7,23},{8,24},{9,... | collective-permute-start | bytes 245768 | tf_op jit(solution)/shard_map/ppermute | solution.py:635
  185.1 5.9 %collective-permute-start.27 = (bf16[1,80,512]{2,1,0:T(8,128)(2,1)S(1)}, bf16[1,80,512]{2,1,0:T(8,128)(2,1)S(1)}, u32[]{:S(2)}, u32[]{:S(2)}) collective-permute-start(bf16[1,80,512]{2,1,0:T(8,128)(2,1)S(1)} %get-tuple-element.334), channel_id=1, source_target_pairs={{0,8},{1,9},{2,10},{3,11},{4,12},{5,13},{6,14},{7,15},{8,0},{9,1},... | collective-permute-start | bytes 245768 | tf_op jit(solution)/shard_map/ppermute | solution.py:635
  185.2 6.8 %collective-permute-start.28 = (bf16[1,80,512]{2,1,0:T(8,128)(2,1)S(1)}, bf16[1,80,512]{2,1,0:T(8,128)(2,1)S(1)}, u32[]{:S(2)}, u32[]{:S(2)}) collective-permute-start(bf16[1,80,512]{2,1,0:T(8,128)(2,1)S(1)} %get-tuple-element.335), channel_id=1, source_target_pairs={{0,24},{1,25},{2,26},{3,27},{4,28},{5,29},{6,30},{7,31},{8,16},{9,... | collective-permute-start | bytes 245768 | tf_op jit(solution)/shard_map/ppermute | solution.py:635
  192.1 27.1 %copy-start = (s32[33]{0:T(128)S(1)}, s32[33]{0:T(128)}, u32[]{:S(2)}) copy-start(s32[33]{0:T(128)} %dynamic-slice_bitcast_fusion.refs_1_) | copy-start | bytes 400
  192.1 8.0 %collective-permute-start.32 = (bf16[1,80,512]{2,1,0:T(8,128)(2,1)S(1)}, bf16[1,80,512]{2,1,0:T(8,128)(2,1)S(1)}, u32[]{:S(2)}, u32[]{:S(2)}) collective-permute-start(bf16[1,80,512]{2,1,0:T(8,128)(2,1)S(1)} %add_convert_fusion.14), channel_id=1, source_target_pairs={{0,16},{1,17},{2,18},{3,19},{4,20},{5,21},{6,22},{7,23},{8,24},{9,... | collective-permute-start | bytes 245768 | tf_op jit(solution)/shard_map/ppermute | solution.py:635
  193.7 6.4 %collective-permute-start.33 = (bf16[1,80,512]{2,1,0:T(8,128)(2,1)S(1)}, bf16[1,80,512]{2,1,0:T(8,128)(2,1)S(1)}, u32[]{:S(2)}, u32[]{:S(2)}) collective-permute-start(bf16[1,80,512]{2,1,0:T(8,128)(2,1)S(1)} %add_convert_fusion.14), channel_id=1, source_target_pairs={{0,8},{1,9},{2,10},{3,11},{4,12},{5,13},{6,14},{7,15},{8,0},{9,1},... | collective-permute-start | bytes 245768 | tf_op jit(solution)/shard_map/ppermute | solution.py:635
  194.5 6.4 %collective-permute-start.34 = (bf16[1,80,512]{2,1,0:T(8,128)(2,1)S(1)}, bf16[1,80,512]{2,1,0:T(8,128)(2,1)S(1)}, u32[]{:S(2)}, u32[]{:S(2)}) collective-permute-start(bf16[1,80,512]{2,1,0:T(8,128)(2,1)S(1)} %add_convert_fusion.14), channel_id=1, source_target_pairs={{0,24},{1,25},{2,26},{3,27},{4,28},{5,29},{6,30},{7,31},{8,16},{9,... | collective-permute-start | bytes 245768 | tf_op jit(solution)/shard_map/ppermute | solution.py:635
  196.6 9.6 %collective-permute-start.36 = (bf16[4,128,512]{2,1,0:T(8,128)(2,1)S(1)}, bf16[4,128,512]{2,1,0:T(8,128)(2,1)S(1)}, u32[]{:S(2)}, u32[]{:S(2)}) collective-permute-start(bf16[4,128,512]{2,1,0:T(8,128)(2,1)S(1)} %pad_maximum_fusion.4), channel_id=1, source_target_pairs={{0,4},{1,3},{2,6},{3,1},{4,0},{5,7},{6,2},{7,5},{8,12},{9,11},{10,... | collective-permute-start | bytes 1572872 | tf_op jit(solution)/shard_map/ppermute | solution.py:635
  201.1 18.1 %collective-permute-start.40 = (bf16[8,192,512]{2,1,0:T(8,128)(2,1)S(1)}, bf16[8,192,512]{2,1,0:T(8,128)(2,1)S(1)}, u32[]{:S(2)}, u32[]{:S(2)}) collective-permute-start(bf16[8,192,512]{2,1,0:T(8,128)(2,1)S(1)} %pad_maximum_fusion.refs_2_), channel_id=1, source_target_pairs={{0,1},{1,0},{2,3},{3,2},{4,5},{5,4},{6,7},{7,6},{8,9},{9,8},{10,11... | collective-permute-start | bytes 4718600 | tf_op jit(solution)/shard_map/ppermute | solution.py:635
  201.1 18.0 %collective-permute-start.41 = (bf16[8,192,512]{2,1,0:T(8,128)(2,1)S(1)}, bf16[8,192,512]{2,1,0:T(8,128)(2,1)S(1)}, u32[]{:S(2)}, u32[]{:S(2)}) collective-permute-start(bf16[8,192,512]{2,1,0:T(8,128)(2,1)S(1)} %collective-permute-done.37.refs_3_), channel_id=1, source_target_pairs={{0,1},{1,0},{2,3},{3,2},{4,5},{5,4},{6,7},{7,6},{8,9},{9,8},{10,11... | collective-permute-start | bytes 4718600 | tf_op jit(solution)/shard_map/ppermute | solution.py:635
  206.3 18.0 %collective-permute-start.39 = (bf16[8,128,512]{2,1,0:T(8,128)(2,1)S(1)}, bf16[8,128,512]{2,1,0:T(8,128)(2,1)S(1)}, u32[]{:S(2)}, u32[]{:S(2)}) collective-permute-start(bf16[8,128,512]{2,1,0:T(8,128)(2,1)S(1)} %pad_maximum_fusion.1.refs_2_), channel_id=1, source_target_pairs={{0,2},{1,5},{2,0},{3,7},{4,6},{5,1},{6,4},{7,3},{8,10},{9,13},{10,... | collective-permute-start | bytes 3145736 | tf_op jit(solution)/shard_map/ppermute | solution.py:635
  207.8 10.6 %collective-permute-start.35 = (bf16[4,80,512]{2,1,0:T(8,128)(2,1)S(1)}, bf16[4,80,512]{2,1,0:T(8,128)(2,1)S(1)}, u32[]{:S(2)}, u32[]{:S(2)}) collective-permute-start(bf16[4,80,512]{2,1,0:T(8,128)(2,1)S(1)} %pad_maximum_fusion.5), channel_id=1, source_target_pairs={{0,4},{1,3},{2,6},{3,1},{4,0},{5,7},{6,2},{7,5},{8,12},{9,11},{10,... | collective-permute-start | bytes 983048 | tf_op jit(solution)/shard_map/ppermute | solution.py:635
  218.5 10.7 %collective-permute-start.38 = (bf16[8,80,512]{2,1,0:T(8,128)(2,1)S(1)}, bf16[8,80,512]{2,1,0:T(8,128)(2,1)S(1)}, u32[]{:S(2)}, u32[]{:S(2)}) collective-permute-start(bf16[8,80,512]{2,1,0:T(8,128)(2,1)S(1)} %pad_maximum_fusion.3.refs_2_), channel_id=1, source_target_pairs={{0,2},{1,5},{2,0},{3,7},{4,6},{5,1},{6,4},{7,3},{8,10},{9,13},{10,... | collective-permute-start | bytes 1966088 | tf_op jit(solution)/shard_map/ppermute | solution.py:635
  224.3 6.1 %collective-permute-start.44 = (bf16[8,128,512]{2,1,0:T(8,128)(2,1)S(1)}, bf16[8,128,512]{2,1,0:T(8,128)(2,1)S(1)}, u32[]{:S(2)}, u32[]{:S(2)}) collective-permute-start(bf16[8,128,512]{2,1,0:T(8,128)(2,1)S(1)} %pad_maximum_fusion.1.refs_2_), channel_id=1, source_target_pairs={{0,1},{1,0},{2,3},{3,2},{4,5},{5,4},{6,7},{7,6},{8,9},{9,8},{10,11... | collective-permute-start | bytes 3145736 | tf_op jit(solution)/shard_map/ppermute | solution.py:635
  224.4 6.0 %collective-permute-start.45 = (bf16[8,128,512]{2,1,0:T(8,128)(2,1)S(1)}, bf16[8,128,512]{2,1,0:T(8,128)(2,1)S(1)}, u32[]{:S(2)}, u32[]{:S(2)}) collective-permute-start(bf16[8,128,512]{2,1,0:T(8,128)(2,1)S(1)} %collective-permute-done.39.refs_3_), channel_id=1, source_target_pairs={{0,1},{1,0},{2,3},{3,2},{4,5},{5,4},{6,7},{7,6},{8,9},{9,8},{10,11... | collective-permute-start | bytes 3145736 | tf_op jit(solution)/shard_map/ppermute | solution.py:635
  229.2 5.0 %collective-permute-start.42 = (bf16[8,80,512]{2,1,0:T(8,128)(2,1)S(1)}, bf16[8,80,512]{2,1,0:T(8,128)(2,1)S(1)}, u32[]{:S(2)}, u32[]{:S(2)}) collective-permute-start(bf16[8,80,512]{2,1,0:T(8,128)(2,1)S(1)} %pad_maximum_fusion.3.refs_2_), channel_id=1, source_target_pairs={{0,1},{1,0},{2,3},{3,2},{4,5},{5,4},{6,7},{7,6},{8,9},{9,8},{10,11... | collective-permute-start | bytes 1966088 | tf_op jit(solution)/shard_map/ppermute | solution.py:635
  229.2 5.0 %collective-permute-start.43 = (bf16[8,80,512]{2,1,0:T(8,128)(2,1)S(1)}, bf16[8,80,512]{2,1,0:T(8,128)(2,1)S(1)}, u32[]{:S(2)}, u32[]{:S(2)}) collective-permute-start(bf16[8,80,512]{2,1,0:T(8,128)(2,1)S(1)} %collective-permute-done.38.refs_3_), channel_id=1, source_target_pairs={{0,1},{1,0},{2,3},{3,2},{4,5},{5,4},{6,7},{7,6},{8,9},{9,8},{10,11... | collective-permute-start | bytes 1966088 | tf_op jit(solution)/shard_map/ppermute | solution.py:635
  (5 other events, 43.9 us)

commit v4 on v3

--- a/solution.py
+++ b/solution.py
@@ -23,8 +23,8 @@
 SMEM = pl.BlockSpec(memory_space=pltpu.SMEM)
 VMEM = pl.BlockSpec(memory_space=pltpu.VMEM)
 PLAN = (
-    "attention", "q", "feed", "q", "back", "q+f", "f", "q", "a", "f", "q", "a", "f", "q", "a", "f",
-    "a", "a", "q", "f", "a", "q", "place_q", "f", "a", "f", "place_f", "a",
+    "attention", "q", "feed", "q", "back", "q+f", "q", "f", "a", "q", "f", "q", "a", "f", "q", "a",
+    "f", "a", "f", "a", "q", "a", "f", "q", "place_q", "a", "f", "place_f", "a",
 )
 SMALL = ("b_query", "b_value", "b_out", "gain_one", "shift_one", "b_down", "gain_two", "shift_two")
 NSMALL = 12
@@ -183,6 +183,10 @@
         ],
         0,
     )
+
+
+def own_index(n):
+    return lax.axis_index("dp") * lax.axis_size("rep") + lax.axis_index("rep")
 
 
 def row(ref, e):
@@ -287,10 +291,11 @@
     blocks = 2 * half
     rows = grads.shape[0] * grads.shape[1] // (width * blocks)
     across = grads.shape[1] // width
+    me = own_index(blocks)
 
     def start(out, base, sem):
         def body(r, carry):
-            c = table[base + r]
+            c = table[me, base + r]
             src = grads.at[
                 pl.ds(pl.multiple_of(c // across * rows, rows), rows),
                 pl.ds(pl.multiple_of(c % across * width, width), width),
@@ -298,7 +303,7 @@
             pltpu.make_async_copy(src, out.at[r, pl.ds(offset, rows), :], sem).start()
             return carry
 
-        lax.fori_loop(0, half, body, 0)
+        lax.fori_loop(0, half, body, 0, unroll=True)
 
     start(send, half, sem_send)
     start(keep, 0, sem_keep)
@@ -372,7 +377,7 @@
     length = x.shape[0] // count
     width = x.shape[1]
     loss, d_q, d_p = contrast(
-        (gathered_a, gathered_b), table[n], 2.0 / float(np.sqrt(width))
+        (gathered_a, gathered_b), own_index(n), 2.0 / float(np.sqrt(width))
     )
     terms[...] = loss
     d_cls_p[...] = d_p
@@ -419,37 +424,62 @@
 
 
 def passage_feed_kernel(
-    steps, table, d_cls, cot, first, g1, s1, bu, bd, g2, s2, wu, wd,
+    steps, table, d_cls, g1, s1, bu, bd, g2, s2, cot, first, wu, wd,
     out, d_first, small, keep, send,
-    wu_s, wd_s, slope_s, act_s, inner_s, down_s, low_s, g_down, g_up, sems, out_sems,
+    cot_s, first_s, out_s, d_first_s,
+    wu_s, wd_s, slope_s, act_s, inner_s, down_s, low_s, g_down, g_up, sems, back_sems, out_sems,
 ):
     b = pl.program_id(0)
     sems_out = (out_sems.at[0], out_sems.at[1])
     rows = 2048 // (2 * keep.shape[0])
     total_rows = act_s.shape[0]
     per = 4 // steps
+    length = total_rows // steps
+
+    def part(i):
+        return pl.ds(pl.multiple_of(i * length, length), length)
+
+    def load(i):
+        return [
+            pltpu.make_async_copy(first.at[part(i), :], first_s.at[part(i), :], sems.at[2 + 2 * i]),
+            pltpu.make_async_copy(cot.at[part(i), :], cot_s.at[part(i), :], sems.at[3 + 2 * i]),
+        ]
+
+    def store(i):
+        return [
+            pltpu.make_async_copy(out_s.at[part(i), :], out.at[part(i), :], back_sems.at[2 * i]),
+            pltpu.make_async_copy(
+                d_first_s.at[part(i), :], d_first.at[part(i), :], back_sems.at[2 * i + 1]
+            ),
+        ]
 
     @pl.when(b < steps)
     def _():
-        copies = [
+        weights = [
             pltpu.make_async_copy(src, dst, sems.at[i])
             for i, (src, dst) in enumerate(((wu.at[1], wu_s), (wd.at[1], wd_s)))
         ]
 
         @pl.when(b == 0)
         def _():
-            for c in copies:
+            begin = load(0)
+            for c in begin + weights + [c for i in range(1, steps) for c in load(i)]:
                 c.start()
             small[...] = jnp.zeros_like(small)
-            for c in copies:
+            for c in begin + weights:
                 c.wait()
 
-        place = lax.broadcasted_iota(I32, cot.shape, 0)
-        d_out = cot[...].astype(F32)
+        @pl.when(b > 0)
+        def _():
+            for c in load(b):
+                c.wait()
+
+        mine = part(b)
+        place = lax.broadcasted_iota(I32, (length, cot_s.shape[1]), 0)
+        d_out = cot_s[mine, :].astype(F32)
         for i in range(per):
-            mine = d_cls[pl.ds(b * per + i, 1), :]
-            d_out = d_out + jnp.where(place == i * (cot.shape[0] // per), mine, 0.0)
-        mine = pl.ds(pl.multiple_of(b * cot.shape[0], cot.shape[0]), cot.shape[0])
+            extra = d_cls[pl.ds(b * per + i, 1), :]
+            d_out = d_out + jnp.where(place == i * (length // per), extra, 0.0)
 
         def keep_act(at, value):
             act_s[mine, at] = value
@@ -457,12 +487,14 @@
         def keep_inner(at, value):
             inner_s[mine, at] = value
 
-        out[...], down_s[mine, :], d_first[...], low_s[mine, :], sums = feed_both(
-            first[...], wu_s, row(bu, 1), wd_s, row(bd, 1), row(g1, 1), row(s1, 1), row(g2, 1),
-            row(s2, 1), d_out, slope_s, keep_act, keep_inner,
+        out_s[mine, :], down_s[mine, :], d_first_s[mine, :], low_s[mine, :], sums = feed_both(
+            first_s[mine, :], wu_s, row(bu, 1), wd_s, row(bd, 1), row(g1, 1), row(s1, 1),
+            row(g2, 1), row(s2, 1), d_out, slope_s, keep_act, keep_inner,
         )
         for i, value in enumerate(sums):
             small[3 + i : 4 + i, :] += value
+        for c in store(b):
+            c.start()
 
     @pl.when(b == steps)
     def _():
@@ -473,6 +505,9 @@
     def _():
         g_up[...] = dot_tn(low_s[...], inner_s[...]).astype(B16)
         send_unit(True, g_up, table, keep, send, rows, *sems_out)
+        for i in range(steps):
+            for c in store(i):
+                c.wait()
         wait_units(keep, send, *sems_out)
 
 
@@ -527,15 +562,16 @@
         for e, ref in enumerate((small_q, small)):
             for i in range(NSMALL):
                 sent_s[e * NSMALL + i] = jnp.where(top, ref[i : i + 1, :], 0.0).astype(B16)
+        me = own_index(n)
         for base, out, sem in ((n // 2, send, out_sems.at[1]), (0, keep, out_sems.at[0])):
 
             def body(r, carry, base=base, out=out, sem=sem):
                 pltpu.make_async_copy(
-                    sent_s.at[table[base + r]], out.at[r, pl.ds(rows, 16), :], sem
+                    sent_s.at[table[me, base + r]], out.at[r, pl.ds(rows, 16), :], sem
                 ).start()
                 return carry
 
-            lax.fori_loop(0, n // 2, body, 0)
+            lax.fori_loop(0, n // 2, body, 0, unroll=True)
         for c in copies[4:]:
             c.wait()
         for i in range(3):
@@ -557,10 +593,11 @@
     small_s = scratch[len(kinds) + 1] if with_small else None
     n = starts[-1] + pieces[-1].shape[0]
     rows = 2048 // n
+    me = own_index(n)
     for piece, start in zip(pieces, starts):
 
         def body(r, carry, piece=piece, start=start):
-            c = table[start + r]
+            c = table[me, start + r]
             k = 0
             for u, kind in enumerate(kinds):
                 stage = stages[u].at[start + r]
@@ -600,7 +637,7 @@
                 small_s[c] = block[0:8]
             return carry
 
-        lax.fori_loop(0, piece.shape[0], body, 0)
+        lax.fori_loop(0, piece.shape[0], body, 0, unroll=True)
     if with_small:
         for f in range(2):
             for i in range(8):
@@ -615,7 +652,7 @@
     dp, rep = mesh_shape["dp"], mesh_shape["rep"]
     core, *x = [1 << i for i in range(rep.bit_length() - 1)]
     y, *z = [rep << i for i in range(dp.bit_length() - 1)]
-    return [core, *x, y, *z], [core, y, *x, *z]
+    return ([core, *x, y, *z], [core, y, *x, *z]), ([core, *x, y, *z], [core, y, *z, *x])
 
 
 def order_table(rounds, n):
@@ -871,11 +908,10 @@
     s2,
 ):
     n = mesh_shape["dp"] * mesh_shape["rep"]
-    plane = rounds_of(mesh_shape)
+    plane, mixed = rounds_of(mesh_shape)
     pairs = plane[0][-2:-1]
-    me = lax.axis_index("dp") * mesh_shape["rep"] + lax.axis_index("rep")
-    tables = np.concatenate([order_table(plane, n), np.arange(n, dtype=np.int32)[:, None]], 1)
-    table = lax.dynamic_index_in_dim(jnp.asarray(tables), me, 0, False)
+    table = jnp.asarray(order_table(plane, n))
+    mixed_table = jnp.asarray(order_table(mixed, n))
     qn, ql, h = q_tokens.shape
     pn, plen, _ = p_tokens.shape
     ff = wu.shape[2]
@@ -982,7 +1018,7 @@
     half = n // 2
     terms, d_cls_p, q_grad, small_q, q_out, q_keep, q_send = order(
         question_back_kernel,
-        table, *gathered, q_x, q_cot, qq, qk, qv, q_probs, q_att, q_first,
+        mixed_table, *gathered, q_x, q_cot, qq, qk, qv, q_probs, q_att, q_first,
         g1, s1, bu, bd, g2, s2, wq, wk, wv, wo, wu, wd,
         name="question_back",
         in_specs=[SMEM] + [VMEM] * 16 + [ANY] * 6,
@@ -1015,29 +1051,28 @@
     )
     steps = steps_of(plane, pairs)
     plan = Plan(order)
-    plan.add("q", Sum(order, steps, steps, n, q_keep, q_send))
+    plan.add("q", Sum(order, steps_of(mixed, ()), steps, n, q_keep, q_send))
     r = {}
 
     def run_attention():
         r["p_probs"], r["p_att"], r["p_first"] = attention(2, 2, part)
 
     parts_of = 2
-    two = (pr // parts_of, h)
-
-    def rows_at(width):
-        return pl.BlockSpec((pr // parts_of, width), lambda b: (jnp.minimum(b, parts_of - 1), 0))
-
     def run_feed():
         r["p_out"], r["d_first"], r["small_p"], *out = order(
             functools.partial(passage_feed_kernel, parts_of),
-            table, d_cls_p, p_cot, r["p_first"], g1, s1, bu, bd, g2, s2, wu, wd,
+            table, d_cls_p, g1, s1, bu, bd, g2, s2, p_cot, r["p_first"], wu, wd,
             name="passage_feed",
             grid=(parts_of + 2,),
-            in_specs=[SMEM, whole(8, h), rows_at(h), rows_at(h), one, one, wide, one, one, one, ANY, ANY],
-            out_specs=[rows_at(h), rows_at(h), whole(16, h), ANY, ANY],
+            in_specs=[SMEM, whole(8, h), one, one, wide, one, one, one] + [ANY] * 4,
+            out_specs=[ANY, ANY, whole(16, h), ANY, ANY],
             out_shape=[shape((pr, h), B16), shape((pr, h)), shape((16, h))]
             + [shape((half, 2 * rows, h), B16)] * 2,
             scratch_shapes=[
+                pltpu.VMEM((pr, h), B16),
+                pltpu.VMEM((pr, h), F32),
+                pltpu.VMEM((pr, h), B16),
+                pltpu.VMEM((pr, h), F32),
                 pltpu.VMEM((h, ff), B16),
                 pltpu.VMEM((ff, h), B16),
                 pltpu.VMEM((pr // parts_of, ff), F32),
@@ -1047,7 +1082,8 @@
                 pltpu.VMEM((pr, h), B16),
                 pltpu.VMEM((ff, h), B16),
                 pltpu.VMEM((h, ff), B16),
-                sem(2),
+                sem(2 + 2 * parts_of),
+                sem(2 * parts_of),
                 sem(2),
             ],
             compiler_params=params(62),

time: 242 us -> 236 us (0.975)
  waiting for transfers between devices: 66.6 us -> 62.3 us
    ppermute x39 -> x38, waiting for transfers between devices: 65.1 us -> 60.5 us  [exchange(): return lax.ppermute(x, AXES, [(d, d ^ masks[d & 1]) for d in range(n)])]
    convert_element_type x12 -> x13, other arithmetic: 15.5 us -> 16.7 us  [total(): return sum((p.astype(F32) for p in parts)).astype(B16)]
    ppermute x39 -> x38, starting transfers between devices: 44.4 us -> 43.6 us  [exchange(): return lax.ppermute(x, AXES, [(d, d ^ masks[d & 1]) for d in range(n)])]
  transfers between devices with their start and end apart: 46 -> 45, of which waited for: 18 -> 17; matrix products, arithmetic and copies ran while one was open for 3% -> 3% of each run, Pallas kernels for 28% -> 29%
where the time goes in v4:
time: 236 us; the launch traced here: 232 us
  Pallas kernels  96.6 us (41%)
  waiting for transfers between devices  62.3 us (26%)
  starting transfers between devices  52.9 us (22%)
  other arithmetic  17.2 us (7%)
    pallas_call x12, Pallas kernels, __call__(): *outs, self.token = call(*([self.token] if skip else []), *operands)  96.6 us
    ppermute x38, waiting for transfers between devices, exchange(): return lax.ppermute(x, AXES, [(d, d ^ masks[d & 1]) for d in range(n)])  60.5 us
    ppermute x38, starting transfers between devices, exchange(): return lax.ppermute(x, AXES, [(d, d ^ masks[d & 1]) for d in range(n)])  43.6 us
    convert_element_type x13, other arithmetic, total(): return sum((p.astype(F32) for p in parts)).astype(B16)  16.7 us
    ppermute x7, starting transfers between devices, issue(): lax.ppermute(mine, AXES, [(d, d ^ m) for d in range(self.n)])  9.25 us
  transfers between devices with their start and end apart: 45, of which 17 were waited for; matrix products, arithmetic and copies ran while one was open for 3% of the time, Pallas kernels for 29%

profile of v4, /device:TPU:0, one launch (start us, length us, event | category | flops | bytes accessed | tf_op | source)
XLA Modules:
  0.0 231.8 jit_solution(6026701625686596944)
XLA Ops:
  0.7 10.2 %front.1 = (bf16[1024,512]{1,0:T(8,128)(2,1)}, bf16[1024,512]{1,0:T(8,128)(2,1)}, bf16[1024,512]{1,0:T(8,128)(2,1)}, bf16[256,512]{1,0:T(8,128)(2,1)}, bf16[256,...) custom-call(s32[4,4]{1,0:T(4,128)} %refs_0_.1, s32[4]{0:T(128)} %refs_1_.7, ...), custom_call_target="tpu_custom_call" | custom-call | flops 199999995904 | bytes 1000 | tf_op jit(solution)/shard_map/front/pallas_call | solution.py:745
  10.8 5.1 %collective-permute-start.2 = (bf16[1,16,512]{2,1,0:T(8,128)(2,1)}, bf16[1,16,512]{2,1,0:T(8,128)(2,1)}, u32[]{:S(2)}, u32[]{:S(2)}) collective-permute-start(bf16[1,16,512]{2,1,0:T(8,128)(2,1)} %bitcast.11), channel_id=1, source_target_pairs={{0,24},{1,25},{2,26},{3,27},{4,28},{5,29},{6,30},{7,31},{8,16},{9,... | collective-permute-start | bytes 49160 | tf_op jit(solution)/shard_map/ppermute | solution.py:857
  16.6 6.3 %passage_attention.2 = (bf16[4,2,1024,256]{3,2,1,0:T(8,128)(2,1)}, bf16[1024,512]{1,0:T(8,128)(2,1)}, f32[1024,512]{1,0:T(8,128)}, f32[8,128]{1,0:T(8,128)}) custom-call(f32[8,128]{1,0:T(8,128)} %get-tuple-element.219.refs_0_, bf16[1024,512]{1,0:T(8,128)(2,1)} %get-tuple-element.220.refs_1_.refs_5_, bf16[1024,512]{1,0:T(8,128)(2,1)} %get-tuple-element.221.refs_2_.refs_6_, ...), custom_call_target="tpu_custom_call" | custom-call | flops 199999995904 | bytes 1000 | tf_op jit(solution)/shard_map/passage_attention/pallas_call | solution.py:745
  23.0 1.4 join.2
  24.4 2.6 %collective-permute-start.5 = (bf16[4,16,512]{2,1,0:T(8,128)(2,1)}, bf16[4,16,512]{2,1,0:T(8,128)(2,1)}, u32[]{:S(2)}, u32[]{:S(2)}) collective-permute-start(bf16[4,16,512]{2,1,0:T(8,128)(2,1)} %get-tuple-element.236.refs_1_), channel_id=1, source_target_pairs={{0,6},{1,7},{2,4},{3,5},{4,2},{5,3},{6,0},{7,1},{8,14},{9,15},{10,... | collective-permute-start | bytes 196616 | tf_op jit(solution)/shard_map/ppermute | solution.py:857
  27.9 4.2 %question_attention.1 = (bf16[2,1024,256]{2,1,0:T(8,128)(2,1)}, bf16[256,512]{1,0:T(8,128)(2,1)}, f32[256,512]{1,0:T(8,128)}, f32[8,128]{1,0:T(8,128)}) custom-call(f32[8,128]{1,0:T(8,128)} %get-tuple-element.230.refs_0_, bf16[256,512]{1,0:T(8,128)(2,1)} %get-tuple-element.231.refs_1_.refs_6_, bf16[256,512]{1,0:T(8,128)(2,1)} %get-tuple-element.232.refs_2_.refs_7_, ...), custom_call_target="tpu_custom_call" | custom-call | flops 199999995904 | bytes 1000 | tf_op jit(solution)/shard_map/question_attention/pallas_call | solution.py:745
  32.1 1.6 join.3
  33.7 1.7 collective-permute-done.6
  36.2 13.1 %question_back.1 = (f32[8,128]{1,0:T(8,128)}, f32[8,512]{1,0:T(8,128)}, f32[256,512]{1,0:T(8,128)}, f32[16,512]{1,0:T(8,128)}, bf16[256,512]{1,0:T(8,128)(2,1)},...) custom-call(f32[8,128]{1,0:T(8,128)} %get-tuple-element.242.refs_0_, ...), custom_call_target="tpu_custom_call" | custom-call | flops 199999995904 | bytes 1000 | tf_op jit(solution)/shard_map/question_back/pallas_call | solution.py:745
  49.4 6.4 %passage_attention.3 = (bf16[4,2,1024,256]{3,2,1,0:T(8,128)(2,1)}, bf16[1024,512]{1,0:T(8,128)(2,1)}, f32[1024,512]{1,0:T(8,128)}, f32[8,128]{1,0:T(8,128)}) custom-call(f32[8,128]{1,0:T(8,128)} %get-tuple-element.253.refs_0_, bf16[1024,512]{1,0:T(8,128)(2,1)} %get-tuple-element.220.refs_1_.refs_5_, ...), custom_call_target="tpu_custom_call", output_to_operand_aliasing={{0}: (7, {}), {1}: (8, {}), {2}: (9, {})} | custom-call | flops 199999995904 | bytes 1000 | tf_op jit(solution)/shard_map/passage_attention/pallas_call | solution.py:745
  55.8 3.5 %add_convert_fusion = bf16[8,192,512]{2,1,0:T(8,128)(2,1)} fusion(bf16[16,192,512]{2,1,0:T(8,128)(2,1)} %collective-permute-done.7, bf16[16,192,512]{2,1,0:T(8,128)(2,1)} %get-tuple-element.249), kind=kLoop, calls=%fused_computation | loop fusion | flops 3145728 | bytes 4718592 | tf_op jit(solution)/shard_map/convert_element_type | solution.py:676
  59.4 1.6 collective-permute-start.8
  61.0 23.6 %passage_feed.1 = (bf16[1024,512]{1,0:T(8,128)(2,1)}, f32[1024,512]{1,0:T(8,128)}, f32[16,512]{1,0:T(8,128)}, bf16[16,128,512]{2,1,0:T(8,128)(2,1)}, bf16[16,128,512]{2,1,0:T(8,128)(2,1)}, /*index=5*/f32[8,128]{1,0:T(8,128)}) custom-call(f32[8,128]{1,0:T(8,128)} %get-tuple-element.260.refs_0_, s32[32,32]{1,0:T(8,128)} %constant.4.clone.refs_1_, ...), custom_call_target="tpu_custom_call" | custom-call | flops 199999995904 | bytes 1000 | tf_op jit(solution)/shard_map/passage_feed/pallas_call | solution.py:745
  84.6 2.8 %add_convert_fusion.2 = bf16[4,192,512]{2,1,0:T(8,128)(2,1)} fusion(bf16[8,192,512]{2,1,0:T(8,128)(2,1)} %collective-permute-done.8, bf16[16,192,512]{2,1,0:T(8,128)(2,1)} %collective-permute-done.7, bf16[16,192,512]{2,1,0:T(8,128)(2,1)} %get-tuple-element.249), kind=kLoop, calls=%fused_computation.3 | loop fusion | flops 2359296 | bytes 3145728 | tf_op jit(solution)/shard_map/convert_element_type | solution.py:676
  87.4 1.5 collective-permute-start.9
  88.9 16.9 %passage_attention_back.1 = (f32[1024,512]{1,0:T(8,128)}, bf16[16,80,512]{2,1,0:T(8,128)(2,1)}, bf16[16,80,512]{2,1,0:T(8,128)(2,1)}, f32[8,128]{1,0:T(8,128)}) custom-call(f32[8,128]{1,0:T(8,128)} %get-tuple-element.271.refs_0_, s32[32,32]{1,0:T(8,128)} %constant.4.clone.refs_1_, f32[16,512]{1,0:T(8,128)} %get-tuple-element.272.refs_2_, ...), custom_call_target="tpu_custom_call" | custom-call | flops 199999995904 | bytes 1000 | tf_op jit(solution)/shard_map/passage_attention_back/pallas_call | solution.py:745
  105.9 1.7 add_convert_fusion.5
  107.5 2.0 add_convert_fusion.1
  111.6 9.1 %collective-permute-done.13 = bf16[2,192,512]{2,1,0:T(8,128)(2,1)S(1)} collective-permute-done((bf16[2,192,512]{2,1,0:T(8,128)(2,1)S(1)}, bf16[2,192,512]{2,1,0:T(8,128)(2,1)S(1)}, u32[]{:S(2)}, u32[]{:S(2)}) %collective-permute-start.13) | collective-permute-done | bytes 393248 | tf_op jit(solution)/shard_map/ppermute | solution.py:672
  122.0 3.5 %collective-permute-start.15 = (bf16[1,192,512]{2,1,0:T(8,128)(2,1)S(1)}, bf16[1,192,512]{2,1,0:T(8,128)(2,1)S(1)}, u32[]{:S(2)}, u32[]{:S(2)}) collective-permute-start(bf16[1,192,512]{2,1,0:T(8,128)(2,1)S(1)} %add_convert_fusion.8), channel_id=1, source_target_pairs={{0,16},{1,3},{2,18},{3,1},{4,20},{5,7},{6,22},{7,5},{8,24},{9,11},... | collective-permute-start | bytes 589832 | tf_op jit(solution)/shard_map/ppermute | solution.py:672
  128.2 3.1 %collective-permute-done.15 = bf16[1,192,512]{2,1,0:T(8,128)(2,1)S(1)} collective-permute-done((bf16[1,192,512]{2,1,0:T(8,128)(2,1)S(1)}, bf16[1,192,512]{2,1,0:T(8,128)(2,1)S(1)}, u32[]{:S(2)}, u32[]{:S(2)}) %collective-permute-start.15) | collective-permute-done | bytes 196640 | tf_op jit(solution)/shard_map/ppermute | solution.py:672
  131.3 1.4 add_convert_fusion.7
  132.7 3.9 %collective-permute-start.18 = (bf16[1,192,512]{2,1,0:T(8,128)(2,1)S(1)}, bf16[1,192,512]{2,1,0:T(8,128)(2,1)S(1)}, u32[]{:S(2)}, u32[]{:S(2)}) collective-permute-start(bf16[1,192,512]{2,1,0:T(8,128)(2,1)S(1)} %add_convert_fusion.7), channel_id=1, source_target_pairs={{0,24},{1,25},{2,26},{3,27},{4,28},{5,29},{6,30},{7,31},{8,16},{9,... | collective-permute-start | bytes 589832 | tf_op jit(solution)/shard_map/ppermute | solution.py:672
  137.2 2.3 collective-permute-start.14
  140.8 1.7 collective-permute-done.18
  142.5 3.3 %collective-permute-done.17 = bf16[1,192,512]{2,1,0:T(8,128)(2,1)S(1)} collective-permute-done((bf16[1,192,512]{2,1,0:T(8,128)(2,1)S(1)}, bf16[1,192,512]{2,1,0:T(8,128)(2,1)S(1)}, u32[]{:S(2)}, u32[]{:S(2)}) %collective-permute-start.17) | collective-permute-done | bytes 196640 | tf_op jit(solution)/shard_map/ppermute | solution.py:672
  145.8 4.2 %collective-permute-done.16 = bf16[1,192,512]{2,1,0:T(8,128)(2,1)S(1)} collective-permute-done((bf16[1,192,512]{2,1,0:T(8,128)(2,1)S(1)}, bf16[1,192,512]{2,1,0:T(8,128)(2,1)S(1)}, u32[]{:S(2)}, u32[]{:S(2)}) %collective-permute-start.16) | collective-permute-done | bytes 196640 | tf_op jit(solution)/shard_map/ppermute | solution.py:672
  151.4 3.3 %collective-permute-start.23 = (bf16[1,128,512]{2,1,0:T(8,128)(2,1)S(1)}, bf16[1,128,512]{2,1,0:T(8,128)(2,1)S(1)}, u32[]{:S(2)}, u32[]{:S(2)}) collective-permute-start(bf16[1,128,512]{2,1,0:T(8,128)(2,1)S(1)} %get-tuple-element.320), channel_id=1, source_target_pairs={{0,8},{1,9},{2,10},{3,11},{4,12},{5,13},{6,14},{7,15},{8,0},{9,1},... | collective-permute-start | bytes 393224 | tf_op jit(solution)/shard_map/ppermute | solution.py:672
  155.9 6.1 %collective-permute-done.22 = bf16[1,128,512]{2,1,0:T(8,128)(2,1)S(1)} collective-permute-done((bf16[1,128,512]{2,1,0:T(8,128)(2,1)S(1)}, bf16[1,128,512]{2,1,0:T(8,128)(2,1)S(1)}, u32[]{:S(2)}, u32[]{:S(2)}) %collective-permute-start.22) | collective-permute-done | bytes 131104 | tf_op jit(solution)/shard_map/ppermute | solution.py:672
  165.0 3.1 %collective-permute-start.30 = (bf16[1,128,512]{2,1,0:T(8,128)(2,1)S(1)}, bf16[1,128,512]{2,1,0:T(8,128)(2,1)S(1)}, u32[]{:S(2)}, u32[]{:S(2)}) collective-permute-start(bf16[1,128,512]{2,1,0:T(8,128)(2,1)S(1)} %add_convert_fusion.9), channel_id=1, source_target_pairs={{0,24},{1,25},{2,26},{3,27},{4,28},{5,29},{6,30},{7,31},{8,16},{9,... | collective-permute-start | bytes 393224 | tf_op jit(solution)/shard_map/ppermute | solution.py:672
  169.4 5.1 %collective-permute-done.20 = bf16[4,80,512]{2,1,0:T(8,128)(2,1)S(1)} collective-permute-done((bf16[4,80,512]{2,1,0:T(8,128)(2,1)S(1)}, bf16[4,80,512]{2,1,0:T(8,128)(2,1)S(1)}, u32[]{:S(2)}, u32[]{:S(2)}) %collective-permute-start.20) | collective-permute-done | bytes 327712 | tf_op jit(solution)/shard_map/ppermute | solution.py:672
  174.7 3.6 %collective-permute-done.28 = bf16[1,128,512]{2,1,0:T(8,128)(2,1)S(1)} collective-permute-done((bf16[1,128,512]{2,1,0:T(8,128)(2,1)S(1)}, bf16[1,128,512]{2,1,0:T(8,128)(2,1)S(1)}, u32[]{:S(2)}, u32[]{:S(2)}) %collective-permute-start.28) | collective-permute-done | bytes 131104 | tf_op jit(solution)/shard_map/ppermute | solution.py:672
  178.6 1.4 collective-permute-start.25
  180.0 2.2 collective-permute-start.26
  183.0 3.7 %collective-permute-done.25 = bf16[1,80,512]{2,1,0:T(8,128)(2,1)S(1)} collective-permute-done((bf16[1,80,512]{2,1,0:T(8,128)(2,1)S(1)}, bf16[1,80,512]{2,1,0:T(8,128)(2,1)S(1)}, u32[]{:S(2)}, u32[]{:S(2)}) %collective-permute-start.25) | collective-permute-done | bytes 81952 | tf_op jit(solution)/shard_map/ppermute | solution.py:672
  187.1 1.4 collective-permute-done.27
  188.5 1.9 collective-permute-start.33
  191.0 2.0 collective-permute-start.31
  193.1 1.8 collective-permute-done.33
  194.9 1.7 collective-permute-done.32
  197.2 1.4 collective-permute-start.40
  198.6 1.5 collective-permute-start.35
  200.1 9.2 %collective-permute-done.35 = bf16[4,80,512]{2,1,0:T(8,128)(2,1)S(1)} collective-permute-done((bf16[4,80,512]{2,1,0:T(8,128)(2,1)S(1)}, bf16[4,80,512]{2,1,0:T(8,128)(2,1)S(1)}, u32[]{:S(2)}, u32[]{:S(2)}) %collective-permute-start.35) | collective-permute-done | bytes 327712 | tf_op jit(solution)/shard_map/ppermute | solution.py:672
  209.3 1.4 collective-permute-start.37
  210.6 4.9 %collective-permute-done.40.refs_3_ = bf16[8,128,512]{2,1,0:T(8,128)(2,1)S(1)} collective-permute-done((bf16[8,128,512]{2,1,0:T(8,128)(2,1)S(1)}, bf16[8,128,512]{2,1,0:T(8,128)(2,1)S(1)}, u32[]{:S(2)}, u32[]{:S(2)}) %collective-permute-start.40) | collective-permute-done | bytes 1048608 | tf_op jit(solution)/shard_map/ppermute | solution.py:672
  216.1 5.3 %place.3 = (f32[2,2048,512]{2,1,0:T(8,128)}, f32[2,512,2048]{2,1,0:T(8,128)}, f32[2,512,512]{2,1,0:T(8,128)}, f32[2,512,512]{2,1,0:T(8,128)}, f32[2,512,512]{2,1...) custom-call(f32[8,128]{1,0:T(8,128)S(1)} %copy-done.1, s32[32,32]{1,0:T(8,128)S(1)} %copy-done, ...), custom_call_target="tpu_custom_call" | custom-call | flops 1000 | bytes 1000 | tf_op jit(solution)/shard_map/place/pallas_call | solution.py:745
  223.7 4.1 %place.4 = (f32[2,2048,512]{2,1,0:T(8,128)}, f32[2,512,2048]{2,1,0:T(8,128)}, f32[8,128]{1,0:T(8,128)S(1)}) custom-call(f32[8,128]{1,0:T(8,128)S(1)} %get-tuple-element.384.refs_0_, s32[32,32]{1,0:T(8,128)S(1)} %copy-done, bf16[8,128,512]{2,1,0:T(8,128)(2,1)S(1)} %pad_maximum_fusion.1.refs_2_, ...), custom_call_target="tpu_custom_call", output_to_operand_aliasing={{0}: (6, {}), {1}: (7, {})} | custom-call | flops 1000 | bytes 1000 | tf_op jit(solution)/shard_map/place/pallas_call | solution.py:745
  227.8 3.5 %place.5 = (f32[2,512,512]{2,1,0:T(8,128)}, f32[2,512,512]{2,1,0:T(8,128)}, f32[2,512,512]{2,1,0:T(8,128)}, f32[2,512,512]{2,1,0:T(8,128)}, f32[2,512]{1,0:T(2,1...) custom-call(f32[8,128]{1,0:T(8,128)S(1)} %get-tuple-element.390.refs, ...), custom_call_target="tpu_custom_call", output_to_operand_aliasing={{0}: (6, {}), {1}: (7, {}), {2}: (8, {}), {3}: (9, {})} | custom-call | flops 1000 | bytes 1000 | tf_op jit(solution)/shard_map/place/pallas_call | solution.py:745
  (88 shorter events, 23.0 us)
Async XLA Ops:
  10.8 12.1 %collective-permute-start.2 = (bf16[1,16,512]{2,1,0:T(8,128)(2,1)}, bf16[1,16,512]{2,1,0:T(8,128)(2,1)}, u32[]{:S(2)}, u32[]{:S(2)}) collective-permute-start(bf16[1,16,512]{2,1,0:T(8,128)(2,1)} %bitcast.11), channel_id=1, source_target_pairs={{0,24},{1,25},{2,26},{3,27},{4,28},{5,29},{6,30},{7,31},{8,16},{9,... | collective-permute-start | bytes 49160 | tf_op jit(solution)/shard_map/ppermute | solution.py:857
  15.9 7.0 %collective-permute-start.1 = (bf16[1,16,512]{2,1,0:T(8,128)(2,1)}, bf16[1,16,512]{2,1,0:T(8,128)(2,1)}, u32[]{:S(2)}, u32[]{:S(2)}) collective-permute-start(bf16[1,16,512]{2,1,0:T(8,128)(2,1)} %bitcast.12), channel_id=1, source_target_pairs={{0,8},{1,9},{2,10},{3,11},{4,12},{5,13},{6,14},{7,15},{8,0},{9,1},... | collective-permute-start | bytes 49160 | tf_op jit(solution)/shard_map/ppermute | solution.py:857
  15.9 7.0 %collective-permute-start = (bf16[1,16,512]{2,1,0:T(8,128)(2,1)}, bf16[1,16,512]{2,1,0:T(8,128)(2,1)}, u32[]{:S(2)}, u32[]{:S(2)}) collective-permute-start(bf16[1,16,512]{2,1,0:T(8,128)(2,1)} %bitcast.13), channel_id=1, source_target_pairs={{0,16},{1,17},{2,18},{3,19},{4,20},{5,21},{6,22},{7,23},{8,24},{9,... | collective-permute-start | bytes 49160 | tf_op jit(solution)/shard_map/ppermute | solution.py:857
  24.4 7.7 %collective-permute-start.5 = (bf16[4,16,512]{2,1,0:T(8,128)(2,1)}, bf16[4,16,512]{2,1,0:T(8,128)(2,1)}, u32[]{:S(2)}, u32[]{:S(2)}) collective-permute-start(bf16[4,16,512]{2,1,0:T(8,128)(2,1)} %get-tuple-element.236.refs_1_), channel_id=1, source_target_pairs={{0,6},{1,7},{2,4},{3,5},{4,2},{5,3},{6,0},{7,1},{8,14},{9,15},{10,... | collective-permute-start | bytes 196616 | tf_op jit(solution)/shard_map/ppermute | solution.py:857
  27.0 5.1 %collective-permute-start.4 = (bf16[4,16,512]{2,1,0:T(8,128)(2,1)}, bf16[4,16,512]{2,1,0:T(8,128)(2,1)}, u32[]{:S(2)}, u32[]{:S(2)}) collective-permute-start(bf16[4,16,512]{2,1,0:T(8,128)(2,1)} %get-tuple-element.236.refs_1_), channel_id=1, source_target_pairs={{0,2},{1,3},{2,0},{3,1},{4,6},{5,7},{6,4},{7,5},{8,10},{9,11},{10,... | collective-permute-start | bytes 196616 | tf_op jit(solution)/shard_map/ppermute | solution.py:857
  27.5 4.6 %collective-permute-start.3 = (bf16[4,16,512]{2,1,0:T(8,128)(2,1)}, bf16[4,16,512]{2,1,0:T(8,128)(2,1)}, u32[]{:S(2)}, u32[]{:S(2)}) collective-permute-start(bf16[4,16,512]{2,1,0:T(8,128)(2,1)} %get-tuple-element.236.refs_1_), channel_id=1, source_target_pairs={{0,4},{1,5},{2,6},{3,7},{4,0},{5,1},{6,2},{7,3},{8,12},{9,13},{10,... | collective-permute-start | bytes 196616 | tf_op jit(solution)/shard_map/ppermute | solution.py:857
  33.7 1.7 collective-permute-start.6
  49.3 6.6 %collective-permute-start.7 = (bf16[16,192,512]{2,1,0:T(8,128)(2,1)}, bf16[16,192,512]{2,1,0:T(8,128)(2,1)}, u32[]{:S(2)}, u32[]{:S(2)}) collective-permute-start(bf16[16,192,512]{2,1,0:T(8,128)(2,1)} %get-tuple-element.252), channel_id=1, source_target_pairs={{0,1},{1,0},{2,3},{3,2},{4,5},{5,4},{6,7},{7,6},{8,9},{9,8},{10,11... | collective-permute-start | bytes 9437192 | tf_op jit(solution)/shard_map/ppermute | solution.py:672
  59.4 25.2 %collective-permute-start.8 = (bf16[8,192,512]{2,1,0:T(8,128)(2,1)}, bf16[8,192,512]{2,1,0:T(8,128)(2,1)}, u32[]{:S(2)}, u32[]{:S(2)}) collective-permute-start(bf16[8,192,512]{2,1,0:T(8,128)(2,1)} %add_convert_fusion), channel_id=1, source_target_pairs={{0,2},{1,5},{2,0},{3,7},{4,6},{5,1},{6,4},{7,3},{8,10},{9,13},{10,... | collective-permute-start | bytes 4718600 | tf_op jit(solution)/shard_map/ppermute | solution.py:672
  87.4 18.4 %collective-permute-start.9 = (bf16[4,192,512]{2,1,0:T(8,128)(2,1)}, bf16[4,192,512]{2,1,0:T(8,128)(2,1)}, u32[]{:S(2)}, u32[]{:S(2)}) collective-permute-start(bf16[4,192,512]{2,1,0:T(8,128)(2,1)} %add_convert_fusion.2), channel_id=1, source_target_pairs={{0,4},{1,9},{2,6},{3,11},{4,0},{5,13},{6,2},{7,15},{8,12},{9,1},{1... | collective-permute-start | bytes 2359304 | tf_op jit(solution)/shard_map/ppermute | solution.py:672
  88.9 16.9 %collective-permute-start.10 = (bf16[16,128,512]{2,1,0:T(8,128)(2,1)}, bf16[16,128,512]{2,1,0:T(8,128)(2,1)}, u32[]{:S(2)}, u32[]{:S(2)}) collective-permute-start(bf16[16,128,512]{2,1,0:T(8,128)(2,1)} %get-tuple-element.281), channel_id=1, source_target_pairs={{0,1},{1,0},{2,3},{3,2},{4,5},{5,4},{6,7},{7,6},{8,9},{9,8},{10,11... | collective-permute-start | bytes 6291464 | tf_op jit(solution)/shard_map/ppermute | solution.py:672
  109.5 18.5 %copy-start.3 = (bf16[16,80,512]{2,1,0:T(8,128)(2,1)S(1)}, bf16[16,80,512]{2,1,0:T(8,128)(2,1)}, u32[]{:S(2)}) copy-start(bf16[16,80,512]{2,1,0:T(8,128)(2,1)} %get-tuple-element.278) | copy-start | bytes 3932164
  109.5 16.0 %collective-permute-start.12 = (bf16[8,128,512]{2,1,0:T(8,128)(2,1)S(1)}, bf16[8,128,512]{2,1,0:T(8,128)(2,1)S(1)}, u32[]{:S(2)}, u32[]{:S(2)}) collective-permute-start(bf16[8,128,512]{2,1,0:T(8,128)(2,1)S(1)} %add_convert_fusion.1), channel_id=1, source_target_pairs={{0,2},{1,5},{2,0},{3,7},{4,6},{5,1},{6,4},{7,3},{8,10},{9,13},{10,... | collective-permute-start | bytes 3145736 | tf_op jit(solution)/shard_map/ppermute | solution.py:672
  110.6 17.4 %collective-permute-start.11 = (bf16[16,80,512]{2,1,0:T(8,128)(2,1)S(1)}, bf16[16,80,512]{2,1,0:T(8,128)(2,1)S(1)}, u32[]{:S(2)}, u32[]{:S(2)}) collective-permute-start(bf16[16,80,512]{2,1,0:T(8,128)(2,1)S(1)} %copy-done.5), channel_id=1, source_target_pairs={{0,1},{1,0},{2,3},{3,2},{4,5},{5,4},{6,7},{7,6},{8,9},{9,8},{10,11... | collective-permute-start | bytes 3932168 | tf_op jit(solution)/shard_map/ppermute | solution.py:672
  110.6 10.0 %collective-permute-start.13 = (bf16[2,192,512]{2,1,0:T(8,128)(2,1)S(1)}, bf16[2,192,512]{2,1,0:T(8,128)(2,1)S(1)}, u32[]{:S(2)}, u32[]{:S(2)}) collective-permute-start(bf16[2,192,512]{2,1,0:T(8,128)(2,1)S(1)} %add_convert_fusion.5), channel_id=1, source_target_pairs={{0,8},{1,17},{2,10},{3,19},{4,12},{5,21},{6,14},{7,23},{8,0},{9,25... | collective-permute-start | bytes 1179656 | tf_op jit(solution)/shard_map/ppermute | solution.py:672
  122.0 9.3 %collective-permute-start.15 = (bf16[1,192,512]{2,1,0:T(8,128)(2,1)S(1)}, bf16[1,192,512]{2,1,0:T(8,128)(2,1)S(1)}, u32[]{:S(2)}, u32[]{:S(2)}) collective-permute-start(bf16[1,192,512]{2,1,0:T(8,128)(2,1)S(1)} %add_convert_fusion.8), channel_id=1, source_target_pairs={{0,16},{1,3},{2,18},{3,1},{4,20},{5,7},{6,22},{7,5},{8,24},{9,11},... | collective-permute-start | bytes 589832 | tf_op jit(solution)/shard_map/ppermute | solution.py:672
  126.8 12.7 %collective-permute-start.19 = (bf16[4,128,512]{2,1,0:T(8,128)(2,1)S(1)}, bf16[4,128,512]{2,1,0:T(8,128)(2,1)S(1)}, u32[]{:S(2)}, u32[]{:S(2)}) collective-permute-start(bf16[4,128,512]{2,1,0:T(8,128)(2,1)S(1)} %add_convert_fusion.4), channel_id=1, source_target_pairs={{0,4},{1,3},{2,6},{3,1},{4,0},{5,7},{6,2},{7,5},{8,12},{9,11},{10,... | collective-permute-start | bytes 1572872 | tf_op jit(solution)/shard_map/ppermute | solution.py:672
  132.7 9.8 %collective-permute-start.18 = (bf16[1,192,512]{2,1,0:T(8,128)(2,1)S(1)}, bf16[1,192,512]{2,1,0:T(8,128)(2,1)S(1)}, u32[]{:S(2)}, u32[]{:S(2)}) collective-permute-start(bf16[1,192,512]{2,1,0:T(8,128)(2,1)S(1)} %add_convert_fusion.7), channel_id=1, source_target_pairs={{0,24},{1,25},{2,26},{3,27},{4,28},{5,29},{6,30},{7,31},{8,16},{9,... | collective-permute-start | bytes 589832 | tf_op jit(solution)/shard_map/ppermute | solution.py:672
  136.6 9.2 %collective-permute-start.17 = (bf16[1,192,512]{2,1,0:T(8,128)(2,1)S(1)}, bf16[1,192,512]{2,1,0:T(8,128)(2,1)S(1)}, u32[]{:S(2)}, u32[]{:S(2)}) collective-permute-start(bf16[1,192,512]{2,1,0:T(8,128)(2,1)S(1)} %add_convert_fusion.7), channel_id=1, source_target_pairs={{0,8},{1,9},{2,10},{3,11},{4,12},{5,13},{6,14},{7,15},{8,0},{9,1},... | collective-permute-start | bytes 589832 | tf_op jit(solution)/shard_map/ppermute | solution.py:672
  136.6 13.5 %collective-permute-start.16 = (bf16[1,192,512]{2,1,0:T(8,128)(2,1)S(1)}, bf16[1,192,512]{2,1,0:T(8,128)(2,1)S(1)}, u32[]{:S(2)}, u32[]{:S(2)}) collective-permute-start(bf16[1,192,512]{2,1,0:T(8,128)(2,1)S(1)} %add_convert_fusion.7), channel_id=1, source_target_pairs={{0,16},{1,17},{2,18},{3,19},{4,20},{5,21},{6,22},{7,23},{8,24},{9,... | collective-permute-start | bytes 589832 | tf_op jit(solution)/shard_map/ppermute | solution.py:672
  137.2 18.5 %collective-permute-start.14 = (bf16[8,80,512]{2,1,0:T(8,128)(2,1)S(1)}, bf16[8,80,512]{2,1,0:T(8,128)(2,1)S(1)}, u32[]{:S(2)}, u32[]{:S(2)}) collective-permute-start(bf16[8,80,512]{2,1,0:T(8,128)(2,1)S(1)} %add_convert_fusion.3), channel_id=1, source_target_pairs={{0,2},{1,5},{2,0},{3,7},{4,6},{5,1},{6,4},{7,3},{8,10},{9,13},{10,... | collective-permute-start | bytes 1966088 | tf_op jit(solution)/shard_map/ppermute | solution.py:672
  150.1 12.9 %collective-permute-start.21 = (bf16[4,192,512]{2,1,0:T(8,128)(2,1)S(1)}, bf16[4,192,512]{2,1,0:T(8,128)(2,1)S(1)}, u32[]{:S(2)}, u32[]{:S(2)}) collective-permute-start(bf16[4,192,512]{2,1,0:T(8,128)(2,1)S(1)} %pad_maximum_fusion.2), channel_id=1, source_target_pairs={{0,4},{1,3},{2,6},{3,1},{4,0},{5,7},{6,2},{7,5},{8,12},{9,11},{10,... | collective-permute-start | bytes 2359304 | tf_op jit(solution)/shard_map/ppermute | solution.py:672
  151.4 10.6 %collective-permute-start.22 = (bf16[1,128,512]{2,1,0:T(8,128)(2,1)S(1)}, bf16[1,128,512]{2,1,0:T(8,128)(2,1)S(1)}, u32[]{:S(2)}, u32[]{:S(2)}) collective-permute-start(bf16[1,128,512]{2,1,0:T(8,128)(2,1)S(1)} %get-tuple-element.319), channel_id=1, source_target_pairs={{0,16},{1,17},{2,18},{3,19},{4,20},{5,21},{6,22},{7,23},{8,24},{9,... | collective-permute-start | bytes 393224 | tf_op jit(solution)/shard_map/ppermute | solution.py:672
  151.4 10.6 %collective-permute-start.23 = (bf16[1,128,512]{2,1,0:T(8,128)(2,1)S(1)}, bf16[1,128,512]{2,1,0:T(8,128)(2,1)S(1)}, u32[]{:S(2)}, u32[]{:S(2)}) collective-permute-start(bf16[1,128,512]{2,1,0:T(8,128)(2,1)S(1)} %get-tuple-element.320), channel_id=1, source_target_pairs={{0,8},{1,9},{2,10},{3,11},{4,12},{5,13},{6,14},{7,15},{8,0},{9,1},... | collective-permute-start | bytes 393224 | tf_op jit(solution)/shard_map/ppermute | solution.py:672
  154.7 7.3 %collective-permute-start.24 = (bf16[1,128,512]{2,1,0:T(8,128)(2,1)S(1)}, bf16[1,128,512]{2,1,0:T(8,128)(2,1)S(1)}, u32[]{:S(2)}, u32[]{:S(2)}) collective-permute-start(bf16[1,128,512]{2,1,0:T(8,128)(2,1)S(1)} %get-tuple-element.321), channel_id=1, source_target_pairs={{0,24},{1,25},{2,26},{3,27},{4,28},{5,29},{6,30},{7,31},{8,16},{9,... | collective-permute-start | bytes 393224 | tf_op jit(solution)/shard_map/ppermute | solution.py:672
  163.2 33.5 %collective-permute-start.36 = (bf16[8,192,512]{2,1,0:T(8,128)(2,1)S(1)}, bf16[8,192,512]{2,1,0:T(8,128)(2,1)S(1)}, u32[]{:S(2)}, u32[]{:S(2)}) collective-permute-start(bf16[8,192,512]{2,1,0:T(8,128)(2,1)S(1)} %pad_maximum_fusion.refs_2_), channel_id=1, source_target_pairs={{0,2},{1,5},{2,0},{3,7},{4,6},{5,1},{6,4},{7,3},{8,10},{9,13},{10,... | collective-permute-start | bytes 4718600 | tf_op jit(solution)/shard_map/ppermute | solution.py:672
  163.9 10.6 %collective-permute-start.20 = (bf16[4,80,512]{2,1,0:T(8,128)(2,1)S(1)}, bf16[4,80,512]{2,1,0:T(8,128)(2,1)S(1)}, u32[]{:S(2)}, u32[]{:S(2)}) collective-permute-start(bf16[4,80,512]{2,1,0:T(8,128)(2,1)S(1)} %add_convert_fusion.6), channel_id=1, source_target_pairs={{0,4},{1,3},{2,6},{3,1},{4,0},{5,7},{6,2},{7,5},{8,12},{9,11},{10,... | collective-permute-start | bytes 983048 | tf_op jit(solution)/shard_map/ppermute | solution.py:672
  165.0 9.6 %collective-permute-start.30 = (bf16[1,128,512]{2,1,0:T(8,128)(2,1)S(1)}, bf16[1,128,512]{2,1,0:T(8,128)(2,1)S(1)}, u32[]{:S(2)}, u32[]{:S(2)}) collective-permute-start(bf16[1,128,512]{2,1,0:T(8,128)(2,1)S(1)} %add_convert_fusion.9), channel_id=1, source_target_pairs={{0,24},{1,25},{2,26},{3,27},{4,28},{5,29},{6,30},{7,31},{8,16},{9,... | collective-permute-start | bytes 393224 | tf_op jit(solution)/shard_map/ppermute | solution.py:672
  168.1 6.5 %collective-permute-start.29 = (bf16[1,128,512]{2,1,0:T(8,128)(2,1)S(1)}, bf16[1,128,512]{2,1,0:T(8,128)(2,1)S(1)}, u32[]{:S(2)}, u32[]{:S(2)}) collective-permute-start(bf16[1,128,512]{2,1,0:T(8,128)(2,1)S(1)} %add_convert_fusion.9), channel_id=1, source_target_pairs={{0,8},{1,9},{2,10},{3,11},{4,12},{5,13},{6,14},{7,15},{8,0},{9,1},... | collective-permute-start | bytes 393224 | tf_op jit(solution)/shard_map/ppermute | solution.py:672
  168.1 10.1 %collective-permute-start.28 = (bf16[1,128,512]{2,1,0:T(8,128)(2,1)S(1)}, bf16[1,128,512]{2,1,0:T(8,128)(2,1)S(1)}, u32[]{:S(2)}, u32[]{:S(2)}) collective-permute-start(bf16[1,128,512]{2,1,0:T(8,128)(2,1)S(1)} %add_convert_fusion.9), channel_id=1, source_target_pairs={{0,16},{1,17},{2,18},{3,19},{4,20},{5,21},{6,22},{7,23},{8,24},{9,... | collective-permute-start | bytes 393224 | tf_op jit(solution)/shard_map/ppermute | solution.py:672
  178.3 14.6 %collective-permute-start.34 = (bf16[4,128,512]{2,1,0:T(8,128)(2,1)S(1)}, bf16[4,128,512]{2,1,0:T(8,128)(2,1)S(1)}, u32[]{:S(2)}, u32[]{:S(2)}) collective-permute-start(bf16[4,128,512]{2,1,0:T(8,128)(2,1)S(1)} %pad_maximum_fusion.4), channel_id=1, source_target_pairs={{0,4},{1,3},{2,6},{3,1},{4,0},{5,7},{6,2},{7,5},{8,12},{9,11},{10,... | collective-permute-start | bytes 1572872 | tf_op jit(solution)/shard_map/ppermute | solution.py:672
  178.6 8.1 %collective-permute-start.25 = (bf16[1,80,512]{2,1,0:T(8,128)(2,1)S(1)}, bf16[1,80,512]{2,1,0:T(8,128)(2,1)S(1)}, u32[]{:S(2)}, u32[]{:S(2)}) collective-permute-start(bf16[1,80,512]{2,1,0:T(8,128)(2,1)S(1)} %get-tuple-element.333), channel_id=1, source_target_pairs={{0,16},{1,17},{2,18},{3,19},{4,20},{5,21},{6,22},{7,23},{8,24},{9,... | collective-permute-start | bytes 245768 | tf_op jit(solution)/shard_map/ppermute | solution.py:672
  180.0 7.1 %collective-permute-start.26 = (bf16[1,80,512]{2,1,0:T(8,128)(2,1)S(1)}, bf16[1,80,512]{2,1,0:T(8,128)(2,1)S(1)}, u32[]{:S(2)}, u32[]{:S(2)}) collective-permute-start(bf16[1,80,512]{2,1,0:T(8,128)(2,1)S(1)} %get-tuple-element.334), channel_id=1, source_target_pairs={{0,8},{1,9},{2,10},{3,11},{4,12},{5,13},{6,14},{7,15},{8,0},{9,1},... | collective-permute-start | bytes 245768 | tf_op jit(solution)/shard_map/ppermute | solution.py:672
  182.2 6.2 %collective-permute-start.27 = (bf16[1,80,512]{2,1,0:T(8,128)(2,1)S(1)}, bf16[1,80,512]{2,1,0:T(8,128)(2,1)S(1)}, u32[]{:S(2)}, u32[]{:S(2)}) collective-permute-start(bf16[1,80,512]{2,1,0:T(8,128)(2,1)S(1)} %get-tuple-element.335), channel_id=1, source_target_pairs={{0,24},{1,25},{2,26},{3,27},{4,28},{5,29},{6,30},{7,31},{8,16},{9,... | collective-permute-start | bytes 245768 | tf_op jit(solution)/shard_map/ppermute | solution.py:672
  188.5 27.6 %copy-start = (s32[32,32]{1,0:T(8,128)S(1)}, s32[32,32]{1,0:T(8,128)}, u32[]{:S(2)}) copy-start(s32[32,32]{1,0:T(8,128)} %constant.4.clone.refs_1_) | copy-start | bytes 12292
  188.5 27.5 %copy-start.1 = (f32[8,128]{1,0:T(8,128)S(1)}, f32[8,128]{1,0:T(8,128)}, u32[]{:S(2)}) copy-start(f32[8,128]{1,0:T(8,128)} %get-tuple-element.373.refs_0_) | copy-start | bytes 12292
  188.5 6.4 %collective-permute-start.33 = (bf16[1,80,512]{2,1,0:T(8,128)(2,1)S(1)}, bf16[1,80,512]{2,1,0:T(8,128)(2,1)S(1)}, u32[]{:S(2)}, u32[]{:S(2)}) collective-permute-start(bf16[1,80,512]{2,1,0:T(8,128)(2,1)S(1)} %add_convert_fusion.13), channel_id=1, source_target_pairs={{0,24},{1,25},{2,26},{3,27},{4,28},{5,29},{6,30},{7,31},{8,16},{9,... | collective-permute-start | bytes 245768 | tf_op jit(solution)/shard_map/ppermute | solution.py:672
  190.4 6.2 %collective-permute-start.32 = (bf16[1,80,512]{2,1,0:T(8,128)(2,1)S(1)}, bf16[1,80,512]{2,1,0:T(8,128)(2,1)S(1)}, u32[]{:S(2)}, u32[]{:S(2)}) collective-permute-start(bf16[1,80,512]{2,1,0:T(8,128)(2,1)S(1)} %add_convert_fusion.13), channel_id=1, source_target_pairs={{0,8},{1,9},{2,10},{3,11},{4,12},{5,13},{6,14},{7,15},{8,0},{9,1},... | collective-permute-start | bytes 245768 | tf_op jit(solution)/shard_map/ppermute | solution.py:672
  191.0 5.6 %collective-permute-start.31 = (bf16[1,80,512]{2,1,0:T(8,128)(2,1)S(1)}, bf16[1,80,512]{2,1,0:T(8,128)(2,1)S(1)}, u32[]{:S(2)}, u32[]{:S(2)}) collective-permute-start(bf16[1,80,512]{2,1,0:T(8,128)(2,1)S(1)} %add_convert_fusion.13), channel_id=1, source_target_pairs={{0,16},{1,17},{2,18},{3,19},{4,20},{5,21},{6,22},{7,23},{8,24},{9,... | collective-permute-start | bytes 245768 | tf_op jit(solution)/shard_map/ppermute | solution.py:672
  196.6 19.4 %collective-permute-start.38 = (bf16[8,192,512]{2,1,0:T(8,128)(2,1)S(1)}, bf16[8,192,512]{2,1,0:T(8,128)(2,1)S(1)}, u32[]{:S(2)}, u32[]{:S(2)}) collective-permute-start(bf16[8,192,512]{2,1,0:T(8,128)(2,1)S(1)} %pad_maximum_fusion.refs_2_), channel_id=1, source_target_pairs={{0,1},{1,0},{2,3},{3,2},{4,5},{5,4},{6,7},{7,6},{8,9},{9,8},{10,11... | collective-permute-start | bytes 4718600 | tf_op jit(solution)/shard_map/ppermute | solution.py:672
  196.7 19.3 %collective-permute-start.39 = (bf16[8,192,512]{2,1,0:T(8,128)(2,1)S(1)}, bf16[8,192,512]{2,1,0:T(8,128)(2,1)S(1)}, u32[]{:S(2)}, u32[]{:S(2)}) collective-permute-start(bf16[8,192,512]{2,1,0:T(8,128)(2,1)S(1)} %collective-permute-done.36.refs_3_), channel_id=1, source_target_pairs={{0,1},{1,0},{2,3},{3,2},{4,5},{5,4},{6,7},{7,6},{8,9},{9,8},{10,11... | collective-permute-start | bytes 4718600 | tf_op jit(solution)/shard_map/ppermute | solution.py:672
  197.2 18.3 %collective-permute-start.40 = (bf16[8,128,512]{2,1,0:T(8,128)(2,1)S(1)}, bf16[8,128,512]{2,1,0:T(8,128)(2,1)S(1)}, u32[]{:S(2)}, u32[]{:S(2)}) collective-permute-start(bf16[8,128,512]{2,1,0:T(8,128)(2,1)S(1)} %pad_maximum_fusion.1.refs_2_), channel_id=1, source_target_pairs={{0,2},{1,5},{2,0},{3,7},{4,6},{5,1},{6,4},{7,3},{8,10},{9,13},{10,... | collective-permute-start | bytes 3145736 | tf_op jit(solution)/shard_map/ppermute | solution.py:672
  198.6 10.6 %collective-permute-start.35 = (bf16[4,80,512]{2,1,0:T(8,128)(2,1)S(1)}, bf16[4,80,512]{2,1,0:T(8,128)(2,1)S(1)}, u32[]{:S(2)}, u32[]{:S(2)}) collective-permute-start(bf16[4,80,512]{2,1,0:T(8,128)(2,1)S(1)} %pad_maximum_fusion.5), channel_id=1, source_target_pairs={{0,4},{1,3},{2,6},{3,1},{4,0},{5,7},{6,2},{7,5},{8,12},{9,11},{10,... | collective-permute-start | bytes 983048 | tf_op jit(solution)/shard_map/ppermute | solution.py:672
  209.3 13.3 %collective-permute-start.37 = (bf16[8,80,512]{2,1,0:T(8,128)(2,1)S(1)}, bf16[8,80,512]{2,1,0:T(8,128)(2,1)S(1)}, u32[]{:S(2)}, u32[]{:S(2)}) collective-permute-start(bf16[8,80,512]{2,1,0:T(8,128)(2,1)S(1)} %pad_maximum_fusion.3.refs_2_), channel_id=1, source_target_pairs={{0,2},{1,5},{2,0},{3,7},{4,6},{5,1},{6,4},{7,3},{8,10},{9,13},{10,... | collective-permute-start | bytes 1966088 | tf_op jit(solution)/shard_map/ppermute | solution.py:672
  215.5 8.2 %collective-permute-start.43 = (bf16[8,128,512]{2,1,0:T(8,128)(2,1)S(1)}, bf16[8,128,512]{2,1,0:T(8,128)(2,1)S(1)}, u32[]{:S(2)}, u32[]{:S(2)}) collective-permute-start(bf16[8,128,512]{2,1,0:T(8,128)(2,1)S(1)} %pad_maximum_fusion.1.refs_2_), channel_id=1, source_target_pairs={{0,1},{1,0},{2,3},{3,2},{4,5},{5,4},{6,7},{7,6},{8,9},{9,8},{10,11... | collective-permute-start | bytes 3145736 | tf_op jit(solution)/shard_map/ppermute | solution.py:672
  215.6 8.1 %collective-permute-start.44 = (bf16[8,128,512]{2,1,0:T(8,128)(2,1)S(1)}, bf16[8,128,512]{2,1,0:T(8,128)(2,1)S(1)}, u32[]{:S(2)}, u32[]{:S(2)}) collective-permute-start(bf16[8,128,512]{2,1,0:T(8,128)(2,1)S(1)} %collective-permute-done.40.refs_3_), channel_id=1, source_target_pairs={{0,1},{1,0},{2,3},{3,2},{4,5},{5,4},{6,7},{7,6},{8,9},{9,8},{10,11... | collective-permute-start | bytes 3145736 | tf_op jit(solution)/shard_map/ppermute | solution.py:672
  222.6 5.2 %collective-permute-start.41 = (bf16[8,80,512]{2,1,0:T(8,128)(2,1)S(1)}, bf16[8,80,512]{2,1,0:T(8,128)(2,1)S(1)}, u32[]{:S(2)}, u32[]{:S(2)}) collective-permute-start(bf16[8,80,512]{2,1,0:T(8,128)(2,1)S(1)} %pad_maximum_fusion.3.refs_2_), channel_id=1, source_target_pairs={{0,1},{1,0},{2,3},{3,2},{4,5},{5,4},{6,7},{7,6},{8,9},{9,8},{10,11... | collective-permute-start | bytes 1966088 | tf_op jit(solution)/shard_map/ppermute | solution.py:672
  222.7 5.1 %collective-permute-start.42 = (bf16[8,80,512]{2,1,0:T(8,128)(2,1)S(1)}, bf16[8,80,512]{2,1,0:T(8,128)(2,1)S(1)}, u32[]{:S(2)}, u32[]{:S(2)}) collective-permute-start(bf16[8,80,512]{2,1,0:T(8,128)(2,1)S(1)} %collective-permute-done.37.refs_3_), channel_id=1, source_target_pairs={{0,1},{1,0},{2,3},{3,2},{4,5},{5,4},{6,7},{7,6},{8,9},{9,8},{10,11... | collective-permute-start | bytes 1966088 | tf_op jit(solution)/shard_map/ppermute | solution.py:672
  (4 other events, 37.3 us)

commit v5 on v4

--- a/solution.py
+++ b/solution.py
@@ -637,7 +637,7 @@
                 small_s[c] = block[0:8]
             return carry
 
-        lax.fori_loop(0, piece.shape[0], body, 0, unroll=True)
+        lax.fori_loop(0, piece.shape[0], body, 0)
     if with_small:
         for f in range(2):
             for i in range(8):

time: 236 us -> 236 us (level)
  no operation moved by 1% of the time
where the time goes in v5:
time: 236 us; the launch traced here: 232 us
  Pallas kernels  96.6 us (41%)
  waiting for transfers between devices  62.3 us (26%)
  starting transfers between devices  52.9 us (22%)
  other arithmetic  17.2 us (7%)
    pallas_call x12, Pallas kernels, __call__(): *outs, self.token = call(*([self.token] if skip else []), *operands)  96.6 us
    ppermute x38, waiting for transfers between devices, exchange(): return lax.ppermute(x, AXES, [(d, d ^ masks[d & 1]) for d in range(n)])  60.5 us
    ppermute x38, starting transfers between devices, exchange(): return lax.ppermute(x, AXES, [(d, d ^ masks[d & 1]) for d in range(n)])  43.6 us
    convert_element_type x13, other arithmetic, total(): return sum((p.astype(F32) for p in parts)).astype(B16)  16.7 us
    ppermute x7, starting transfers between devices, issue(): lax.ppermute(mine, AXES, [(d, d ^ m) for d in range(self.n)])  9.25 us
  transfers between devices with their start and end apart: 45, of which 17 were waited for; matrix products, arithmetic and copies ran while one was open for 3% of the time, Pallas kernels for 29%

profile of v5, /device:TPU:0, one launch (start us, length us, event | category | flops | bytes accessed | tf_op | source)
XLA Modules:
  0.0 231.8 jit_solution(1127497213687733408)
XLA Ops:
  0.7 10.2 %front.1 = (bf16[1024,512]{1,0:T(8,128)(2,1)}, bf16[1024,512]{1,0:T(8,128)(2,1)}, bf16[1024,512]{1,0:T(8,128)(2,1)}, bf16[256,512]{1,0:T(8,128)(2,1)}, bf16[256,...) custom-call(s32[4,4]{1,0:T(4,128)} %refs_0_.1, s32[4]{0:T(128)} %refs_1_.7, ...), custom_call_target="tpu_custom_call" | custom-call | flops 199999995904 | bytes 1000 | tf_op jit(solution)/shard_map/front/pallas_call | solution.py:745
  10.8 5.1 %collective-permute-start.2 = (bf16[1,16,512]{2,1,0:T(8,128)(2,1)}, bf16[1,16,512]{2,1,0:T(8,128)(2,1)}, u32[]{:S(2)}, u32[]{:S(2)}) collective-permute-start(bf16[1,16,512]{2,1,0:T(8,128)(2,1)} %bitcast.11), channel_id=1, source_target_pairs={{0,24},{1,25},{2,26},{3,27},{4,28},{5,29},{6,30},{7,31},{8,16},{9,... | collective-permute-start | bytes 49160 | tf_op jit(solution)/shard_map/ppermute | solution.py:857
  16.6 6.3 %passage_attention.2 = (bf16[4,2,1024,256]{3,2,1,0:T(8,128)(2,1)}, bf16[1024,512]{1,0:T(8,128)(2,1)}, f32[1024,512]{1,0:T(8,128)}, f32[8,128]{1,0:T(8,128)}) custom-call(f32[8,128]{1,0:T(8,128)} %get-tuple-element.219.refs_0_, bf16[1024,512]{1,0:T(8,128)(2,1)} %get-tuple-element.220.refs_1_.refs_5_, bf16[1024,512]{1,0:T(8,128)(2,1)} %get-tuple-element.221.refs_2_.refs_6_, ...), custom_call_target="tpu_custom_call" | custom-call | flops 199999995904 | bytes 1000 | tf_op jit(solution)/shard_map/passage_attention/pallas_call | solution.py:745
  23.0 1.4 join.2
  24.4 2.6 %collective-permute-start.5 = (bf16[4,16,512]{2,1,0:T(8,128)(2,1)}, bf16[4,16,512]{2,1,0:T(8,128)(2,1)}, u32[]{:S(2)}, u32[]{:S(2)}) collective-permute-start(bf16[4,16,512]{2,1,0:T(8,128)(2,1)} %get-tuple-element.236.refs_1_), channel_id=1, source_target_pairs={{0,6},{1,7},{2,4},{3,5},{4,2},{5,3},{6,0},{7,1},{8,14},{9,15},{10,... | collective-permute-start | bytes 196616 | tf_op jit(solution)/shard_map/ppermute | solution.py:857
  27.9 4.2 %question_attention.1 = (bf16[2,1024,256]{2,1,0:T(8,128)(2,1)}, bf16[256,512]{1,0:T(8,128)(2,1)}, f32[256,512]{1,0:T(8,128)}, f32[8,128]{1,0:T(8,128)}) custom-call(f32[8,128]{1,0:T(8,128)} %get-tuple-element.230.refs_0_, bf16[256,512]{1,0:T(8,128)(2,1)} %get-tuple-element.231.refs_1_.refs_6_, bf16[256,512]{1,0:T(8,128)(2,1)} %get-tuple-element.232.refs_2_.refs_7_, ...), custom_call_target="tpu_custom_call" | custom-call | flops 199999995904 | bytes 1000 | tf_op jit(solution)/shard_map/question_attention/pallas_call | solution.py:745
  32.1 1.6 join.3
  33.7 1.7 collective-permute-done.6
  36.2 13.1 %question_back.1 = (f32[8,128]{1,0:T(8,128)}, f32[8,512]{1,0:T(8,128)}, f32[256,512]{1,0:T(8,128)}, f32[16,512]{1,0:T(8,128)}, bf16[256,512]{1,0:T(8,128)(2,1)},...) custom-call(f32[8,128]{1,0:T(8,128)} %get-tuple-element.242.refs_0_, ...), custom_call_target="tpu_custom_call" | custom-call | flops 199999995904 | bytes 1000 | tf_op jit(solution)/shard_map/question_back/pallas_call | solution.py:745
  49.4 6.4 %passage_attention.3 = (bf16[4,2,1024,256]{3,2,1,0:T(8,128)(2,1)}, bf16[1024,512]{1,0:T(8,128)(2,1)}, f32[1024,512]{1,0:T(8,128)}, f32[8,128]{1,0:T(8,128)}) custom-call(f32[8,128]{1,0:T(8,128)} %get-tuple-element.253.refs_0_, bf16[1024,512]{1,0:T(8,128)(2,1)} %get-tuple-element.220.refs_1_.refs_5_, ...), custom_call_target="tpu_custom_call", output_to_operand_aliasing={{0}: (7, {}), {1}: (8, {}), {2}: (9, {})} | custom-call | flops 199999995904 | bytes 1000 | tf_op jit(solution)/shard_map/passage_attention/pallas_call | solution.py:745
  55.8 3.5 %add_convert_fusion = bf16[8,192,512]{2,1,0:T(8,128)(2,1)} fusion(bf16[16,192,512]{2,1,0:T(8,128)(2,1)} %collective-permute-done.7, bf16[16,192,512]{2,1,0:T(8,128)(2,1)} %get-tuple-element.249), kind=kLoop, calls=%fused_computation | loop fusion | flops 3145728 | bytes 4718592 | tf_op jit(solution)/shard_map/convert_element_type | solution.py:676
  59.4 1.6 collective-permute-start.8
  61.0 23.6 %passage_feed.1 = (bf16[1024,512]{1,0:T(8,128)(2,1)}, f32[1024,512]{1,0:T(8,128)}, f32[16,512]{1,0:T(8,128)}, bf16[16,128,512]{2,1,0:T(8,128)(2,1)}, bf16[16,128,512]{2,1,0:T(8,128)(2,1)}, /*index=5*/f32[8,128]{1,0:T(8,128)}) custom-call(f32[8,128]{1,0:T(8,128)} %get-tuple-element.260.refs_0_, s32[32,32]{1,0:T(8,128)} %constant.4.clone.refs_1_, ...), custom_call_target="tpu_custom_call" | custom-call | flops 199999995904 | bytes 1000 | tf_op jit(solution)/shard_map/passage_feed/pallas_call | solution.py:745
  84.6 2.8 %add_convert_fusion.2 = bf16[4,192,512]{2,1,0:T(8,128)(2,1)} fusion(bf16[8,192,512]{2,1,0:T(8,128)(2,1)} %collective-permute-done.8, bf16[16,192,512]{2,1,0:T(8,128)(2,1)} %collective-permute-done.7, bf16[16,192,512]{2,1,0:T(8,128)(2,1)} %get-tuple-element.249), kind=kLoop, calls=%fused_computation.3 | loop fusion | flops 2359296 | bytes 3145728 | tf_op jit(solution)/shard_map/convert_element_type | solution.py:676
  87.4 1.5 collective-permute-start.9
  88.9 16.9 %passage_attention_back.1 = (f32[1024,512]{1,0:T(8,128)}, bf16[16,80,512]{2,1,0:T(8,128)(2,1)}, bf16[16,80,512]{2,1,0:T(8,128)(2,1)}, f32[8,128]{1,0:T(8,128)}) custom-call(f32[8,128]{1,0:T(8,128)} %get-tuple-element.271.refs_0_, s32[32,32]{1,0:T(8,128)} %constant.4.clone.refs_1_, f32[16,512]{1,0:T(8,128)} %get-tuple-element.272.refs_2_, ...), custom_call_target="tpu_custom_call" | custom-call | flops 199999995904 | bytes 1000 | tf_op jit(solution)/shard_map/passage_attention_back/pallas_call | solution.py:745
  105.9 1.7 add_convert_fusion.5
  107.5 2.0 add_convert_fusion.1
  111.6 9.1 %collective-permute-done.13 = bf16[2,192,512]{2,1,0:T(8,128)(2,1)S(1)} collective-permute-done((bf16[2,192,512]{2,1,0:T(8,128)(2,1)S(1)}, bf16[2,192,512]{2,1,0:T(8,128)(2,1)S(1)}, u32[]{:S(2)}, u32[]{:S(2)}) %collective-permute-start.13) | collective-permute-done | bytes 393248 | tf_op jit(solution)/shard_map/ppermute | solution.py:672
  122.0 3.5 %collective-permute-start.15 = (bf16[1,192,512]{2,1,0:T(8,128)(2,1)S(1)}, bf16[1,192,512]{2,1,0:T(8,128)(2,1)S(1)}, u32[]{:S(2)}, u32[]{:S(2)}) collective-permute-start(bf16[1,192,512]{2,1,0:T(8,128)(2,1)S(1)} %add_convert_fusion.8), channel_id=1, source_target_pairs={{0,16},{1,3},{2,18},{3,1},{4,20},{5,7},{6,22},{7,5},{8,24},{9,11},... | collective-permute-start | bytes 589832 | tf_op jit(solution)/shard_map/ppermute | solution.py:672
  128.2 3.1 %collective-permute-done.15 = bf16[1,192,512]{2,1,0:T(8,128)(2,1)S(1)} collective-permute-done((bf16[1,192,512]{2,1,0:T(8,128)(2,1)S(1)}, bf16[1,192,512]{2,1,0:T(8,128)(2,1)S(1)}, u32[]{:S(2)}, u32[]{:S(2)}) %collective-permute-start.15) | collective-permute-done | bytes 196640 | tf_op jit(solution)/shard_map/ppermute | solution.py:672
  131.3 1.4 add_convert_fusion.7
  132.7 3.9 %collective-permute-start.18 = (bf16[1,192,512]{2,1,0:T(8,128)(2,1)S(1)}, bf16[1,192,512]{2,1,0:T(8,128)(2,1)S(1)}, u32[]{:S(2)}, u32[]{:S(2)}) collective-permute-start(bf16[1,192,512]{2,1,0:T(8,128)(2,1)S(1)} %add_convert_fusion.7), channel_id=1, source_target_pairs={{0,24},{1,25},{2,26},{3,27},{4,28},{5,29},{6,30},{7,31},{8,16},{9,... | collective-permute-start | bytes 589832 | tf_op jit(solution)/shard_map/ppermute | solution.py:672
  137.2 2.3 collective-permute-start.14
  140.8 1.7 collective-permute-done.18
  142.5 3.3 %collective-permute-done.17 = bf16[1,192,512]{2,1,0:T(8,128)(2,1)S(1)} collective-permute-done((bf16[1,192,512]{2,1,0:T(8,128)(2,1)S(1)}, bf16[1,192,512]{2,1,0:T(8,128)(2,1)S(1)}, u32[]{:S(2)}, u32[]{:S(2)}) %collective-permute-start.17) | collective-permute-done | bytes 196640 | tf_op jit(solution)/shard_map/ppermute | solution.py:672
  145.8 4.2 %collective-permute-done.16 = bf16[1,192,512]{2,1,0:T(8,128)(2,1)S(1)} collective-permute-done((bf16[1,192,512]{2,1,0:T(8,128)(2,1)S(1)}, bf16[1,192,512]{2,1,0:T(8,128)(2,1)S(1)}, u32[]{:S(2)}, u32[]{:S(2)}) %collective-permute-start.16) | collective-permute-done | bytes 196640 | tf_op jit(solution)/shard_map/ppermute | solution.py:672
  151.4 3.3 %collective-permute-start.23 = (bf16[1,128,512]{2,1,0:T(8,128)(2,1)S(1)}, bf16[1,128,512]{2,1,0:T(8,128)(2,1)S(1)}, u32[]{:S(2)}, u32[]{:S(2)}) collective-permute-start(bf16[1,128,512]{2,1,0:T(8,128)(2,1)S(1)} %get-tuple-element.320), channel_id=1, source_target_pairs={{0,8},{1,9},{2,10},{3,11},{4,12},{5,13},{6,14},{7,15},{8,0},{9,1},... | collective-permute-start | bytes 393224 | tf_op jit(solution)/shard_map/ppermute | solution.py:672
  155.9 6.1 %collective-permute-done.22 = bf16[1,128,512]{2,1,0:T(8,128)(2,1)S(1)} collective-permute-done((bf16[1,128,512]{2,1,0:T(8,128)(2,1)S(1)}, bf16[1,128,512]{2,1,0:T(8,128)(2,1)S(1)}, u32[]{:S(2)}, u32[]{:S(2)}) %collective-permute-start.22) | collective-permute-done | bytes 131104 | tf_op jit(solution)/shard_map/ppermute | solution.py:672
  165.0 3.1 %collective-permute-start.30 = (bf16[1,128,512]{2,1,0:T(8,128)(2,1)S(1)}, bf16[1,128,512]{2,1,0:T(8,128)(2,1)S(1)}, u32[]{:S(2)}, u32[]{:S(2)}) collective-permute-start(bf16[1,128,512]{2,1,0:T(8,128)(2,1)S(1)} %add_convert_fusion.9), channel_id=1, source_target_pairs={{0,24},{1,25},{2,26},{3,27},{4,28},{5,29},{6,30},{7,31},{8,16},{9,... | collective-permute-start | bytes 393224 | tf_op jit(solution)/shard_map/ppermute | solution.py:672
  169.4 5.1 %collective-permute-done.20 = bf16[4,80,512]{2,1,0:T(8,128)(2,1)S(1)} collective-permute-done((bf16[4,80,512]{2,1,0:T(8,128)(2,1)S(1)}, bf16[4,80,512]{2,1,0:T(8,128)(2,1)S(1)}, u32[]{:S(2)}, u32[]{:S(2)}) %collective-permute-start.20) | collective-permute-done | bytes 327712 | tf_op jit(solution)/shard_map/ppermute | solution.py:672
  174.7 3.6 %collective-permute-done.28 = bf16[1,128,512]{2,1,0:T(8,128)(2,1)S(1)} collective-permute-done((bf16[1,128,512]{2,1,0:T(8,128)(2,1)S(1)}, bf16[1,128,512]{2,1,0:T(8,128)(2,1)S(1)}, u32[]{:S(2)}, u32[]{:S(2)}) %collective-permute-start.28) | collective-permute-done | bytes 131104 | tf_op jit(solution)/shard_map/ppermute | solution.py:672
  178.6 1.4 collective-permute-start.25
  180.0 2.2 collective-permute-start.26
  183.0 3.7 %collective-permute-done.25 = bf16[1,80,512]{2,1,0:T(8,128)(2,1)S(1)} collective-permute-done((bf16[1,80,512]{2,1,0:T(8,128)(2,1)S(1)}, bf16[1,80,512]{2,1,0:T(8,128)(2,1)S(1)}, u32[]{:S(2)}, u32[]{:S(2)}) %collective-permute-start.25) | collective-permute-done | bytes 81952 | tf_op jit(solution)/shard_map/ppermute | solution.py:672
  187.1 1.4 collective-permute-done.27
  188.5 1.9 collective-permute-start.33
  191.0 2.0 collective-permute-start.31
  193.1 1.8 collective-permute-done.33
  194.9 1.7 collective-permute-done.32
  197.2 1.4 collective-permute-start.40
  198.6 1.5 collective-permute-start.35
  200.1 9.2 %collective-permute-done.35 = bf16[4,80,512]{2,1,0:T(8,128)(2,1)S(1)} collective-permute-done((bf16[4,80,512]{2,1,0:T(8,128)(2,1)S(1)}, bf16[4,80,512]{2,1,0:T(8,128)(2,1)S(1)}, u32[]{:S(2)}, u32[]{:S(2)}) %collective-permute-start.35) | collective-permute-done | bytes 327712 | tf_op jit(solution)/shard_map/ppermute | solution.py:672
  209.3 1.4 collective-permute-start.37
  210.6 4.9 %collective-permute-done.40.refs_3_ = bf16[8,128,512]{2,1,0:T(8,128)(2,1)S(1)} collective-permute-done((bf16[8,128,512]{2,1,0:T(8,128)(2,1)S(1)}, bf16[8,128,512]{2,1,0:T(8,128)(2,1)S(1)}, u32[]{:S(2)}, u32[]{:S(2)}) %collective-permute-start.40) | collective-permute-done | bytes 1048608 | tf_op jit(solution)/shard_map/ppermute | solution.py:672
  216.1 5.4 %place.3 = (f32[2,2048,512]{2,1,0:T(8,128)}, f32[2,512,2048]{2,1,0:T(8,128)}, f32[2,512,512]{2,1,0:T(8,128)}, f32[2,512,512]{2,1,0:T(8,128)}, f32[2,512,512]{2,1...) custom-call(f32[8,128]{1,0:T(8,128)S(1)} %copy-done.1, s32[32,32]{1,0:T(8,128)S(1)} %copy-done, ...), custom_call_target="tpu_custom_call" | custom-call | flops 1000 | bytes 1000 | tf_op jit(solution)/shard_map/place/pallas_call | solution.py:745
  223.7 4.1 %place.4 = (f32[2,2048,512]{2,1,0:T(8,128)}, f32[2,512,2048]{2,1,0:T(8,128)}, f32[8,128]{1,0:T(8,128)S(1)}) custom-call(f32[8,128]{1,0:T(8,128)S(1)} %get-tuple-element.384.refs_0_, s32[32,32]{1,0:T(8,128)S(1)} %copy-done, bf16[8,128,512]{2,1,0:T(8,128)(2,1)S(1)} %pad_maximum_fusion.1.refs_2_, ...), custom_call_target="tpu_custom_call", output_to_operand_aliasing={{0}: (6, {}), {1}: (7, {})} | custom-call | flops 1000 | bytes 1000 | tf_op jit(solution)/shard_map/place/pallas_call | solution.py:745
  227.8 3.5 %place.5 = (f32[2,512,512]{2,1,0:T(8,128)}, f32[2,512,512]{2,1,0:T(8,128)}, f32[2,512,512]{2,1,0:T(8,128)}, f32[2,512,512]{2,1,0:T(8,128)}, f32[2,512]{1,0:T(2,1...) custom-call(f32[8,128]{1,0:T(8,128)S(1)} %get-tuple-element.390.refs, ...), custom_call_target="tpu_custom_call", output_to_operand_aliasing={{0}: (6, {}), {1}: (7, {}), {2}: (8, {}), {3}: (9, {})} | custom-call | flops 1000 | bytes 1000 | tf_op jit(solution)/shard_map/place/pallas_call | solution.py:745
  (88 shorter events, 23.0 us)
Async XLA Ops:
  10.8 12.1 %collective-permute-start.2 = (bf16[1,16,512]{2,1,0:T(8,128)(2,1)}, bf16[1,16,512]{2,1,0:T(8,128)(2,1)}, u32[]{:S(2)}, u32[]{:S(2)}) collective-permute-start(bf16[1,16,512]{2,1,0:T(8,128)(2,1)} %bitcast.11), channel_id=1, source_target_pairs={{0,24},{1,25},{2,26},{3,27},{4,28},{5,29},{6,30},{7,31},{8,16},{9,... | collective-permute-start | bytes 49160 | tf_op jit(solution)/shard_map/ppermute | solution.py:857
  15.9 7.0 %collective-permute-start.1 = (bf16[1,16,512]{2,1,0:T(8,128)(2,1)}, bf16[1,16,512]{2,1,0:T(8,128)(2,1)}, u32[]{:S(2)}, u32[]{:S(2)}) collective-permute-start(bf16[1,16,512]{2,1,0:T(8,128)(2,1)} %bitcast.12), channel_id=1, source_target_pairs={{0,8},{1,9},{2,10},{3,11},{4,12},{5,13},{6,14},{7,15},{8,0},{9,1},... | collective-permute-start | bytes 49160 | tf_op jit(solution)/shard_map/ppermute | solution.py:857
  15.9 7.0 %collective-permute-start = (bf16[1,16,512]{2,1,0:T(8,128)(2,1)}, bf16[1,16,512]{2,1,0:T(8,128)(2,1)}, u32[]{:S(2)}, u32[]{:S(2)}) collective-permute-start(bf16[1,16,512]{2,1,0:T(8,128)(2,1)} %bitcast.13), channel_id=1, source_target_pairs={{0,16},{1,17},{2,18},{3,19},{4,20},{5,21},{6,22},{7,23},{8,24},{9,... | collective-permute-start | bytes 49160 | tf_op jit(solution)/shard_map/ppermute | solution.py:857
  24.4 7.7 %collective-permute-start.5 = (bf16[4,16,512]{2,1,0:T(8,128)(2,1)}, bf16[4,16,512]{2,1,0:T(8,128)(2,1)}, u32[]{:S(2)}, u32[]{:S(2)}) collective-permute-start(bf16[4,16,512]{2,1,0:T(8,128)(2,1)} %get-tuple-element.236.refs_1_), channel_id=1, source_target_pairs={{0,6},{1,7},{2,4},{3,5},{4,2},{5,3},{6,0},{7,1},{8,14},{9,15},{10,... | collective-permute-start | bytes 196616 | tf_op jit(solution)/shard_map/ppermute | solution.py:857
  27.0 5.1 %collective-permute-start.4 = (bf16[4,16,512]{2,1,0:T(8,128)(2,1)}, bf16[4,16,512]{2,1,0:T(8,128)(2,1)}, u32[]{:S(2)}, u32[]{:S(2)}) collective-permute-start(bf16[4,16,512]{2,1,0:T(8,128)(2,1)} %get-tuple-element.236.refs_1_), channel_id=1, source_target_pairs={{0,2},{1,3},{2,0},{3,1},{4,6},{5,7},{6,4},{7,5},{8,10},{9,11},{10,... | collective-permute-start | bytes 196616 | tf_op jit(solution)/shard_map/ppermute | solution.py:857
  27.5 4.6 %collective-permute-start.3 = (bf16[4,16,512]{2,1,0:T(8,128)(2,1)}, bf16[4,16,512]{2,1,0:T(8,128)(2,1)}, u32[]{:S(2)}, u32[]{:S(2)}) collective-permute-start(bf16[4,16,512]{2,1,0:T(8,128)(2,1)} %get-tuple-element.236.refs_1_), channel_id=1, source_target_pairs={{0,4},{1,5},{2,6},{3,7},{4,0},{5,1},{6,2},{7,3},{8,12},{9,13},{10,... | collective-permute-start | bytes 196616 | tf_op jit(solution)/shard_map/ppermute | solution.py:857
  33.7 1.7 collective-permute-start.6
  49.3 6.6 %collective-permute-start.7 = (bf16[16,192,512]{2,1,0:T(8,128)(2,1)}, bf16[16,192,512]{2,1,0:T(8,128)(2,1)}, u32[]{:S(2)}, u32[]{:S(2)}) collective-permute-start(bf16[16,192,512]{2,1,0:T(8,128)(2,1)} %get-tuple-element.252), channel_id=1, source_target_pairs={{0,1},{1,0},{2,3},{3,2},{4,5},{5,4},{6,7},{7,6},{8,9},{9,8},{10,11... | collective-permute-start | bytes 9437192 | tf_op jit(solution)/shard_map/ppermute | solution.py:672
  59.4 25.2 %collective-permute-start.8 = (bf16[8,192,512]{2,1,0:T(8,128)(2,1)}, bf16[8,192,512]{2,1,0:T(8,128)(2,1)}, u32[]{:S(2)}, u32[]{:S(2)}) collective-permute-start(bf16[8,192,512]{2,1,0:T(8,128)(2,1)} %add_convert_fusion), channel_id=1, source_target_pairs={{0,2},{1,5},{2,0},{3,7},{4,6},{5,1},{6,4},{7,3},{8,10},{9,13},{10,... | collective-permute-start | bytes 4718600 | tf_op jit(solution)/shard_map/ppermute | solution.py:672
  87.4 18.4 %collective-permute-start.9 = (bf16[4,192,512]{2,1,0:T(8,128)(2,1)}, bf16[4,192,512]{2,1,0:T(8,128)(2,1)}, u32[]{:S(2)}, u32[]{:S(2)}) collective-permute-start(bf16[4,192,512]{2,1,0:T(8,128)(2,1)} %add_convert_fusion.2), channel_id=1, source_target_pairs={{0,4},{1,9},{2,6},{3,11},{4,0},{5,13},{6,2},{7,15},{8,12},{9,1},{1... | collective-permute-start | bytes 2359304 | tf_op jit(solution)/shard_map/ppermute | solution.py:672
  88.9 16.9 %collective-permute-start.10 = (bf16[16,128,512]{2,1,0:T(8,128)(2,1)}, bf16[16,128,512]{2,1,0:T(8,128)(2,1)}, u32[]{:S(2)}, u32[]{:S(2)}) collective-permute-start(bf16[16,128,512]{2,1,0:T(8,128)(2,1)} %get-tuple-element.281), channel_id=1, source_target_pairs={{0,1},{1,0},{2,3},{3,2},{4,5},{5,4},{6,7},{7,6},{8,9},{9,8},{10,11... | collective-permute-start | bytes 6291464 | tf_op jit(solution)/shard_map/ppermute | solution.py:672
  109.5 18.5 %copy-start.3 = (bf16[16,80,512]{2,1,0:T(8,128)(2,1)S(1)}, bf16[16,80,512]{2,1,0:T(8,128)(2,1)}, u32[]{:S(2)}) copy-start(bf16[16,80,512]{2,1,0:T(8,128)(2,1)} %get-tuple-element.278) | copy-start | bytes 3932164
  109.5 16.0 %collective-permute-start.12 = (bf16[8,128,512]{2,1,0:T(8,128)(2,1)S(1)}, bf16[8,128,512]{2,1,0:T(8,128)(2,1)S(1)}, u32[]{:S(2)}, u32[]{:S(2)}) collective-permute-start(bf16[8,128,512]{2,1,0:T(8,128)(2,1)S(1)} %add_convert_fusion.1), channel_id=1, source_target_pairs={{0,2},{1,5},{2,0},{3,7},{4,6},{5,1},{6,4},{7,3},{8,10},{9,13},{10,... | collective-permute-start | bytes 3145736 | tf_op jit(solution)/shard_map/ppermute | solution.py:672
  110.6 17.4 %collective-permute-start.11 = (bf16[16,80,512]{2,1,0:T(8,128)(2,1)S(1)}, bf16[16,80,512]{2,1,0:T(8,128)(2,1)S(1)}, u32[]{:S(2)}, u32[]{:S(2)}) collective-permute-start(bf16[16,80,512]{2,1,0:T(8,128)(2,1)S(1)} %copy-done.5), channel_id=1, source_target_pairs={{0,1},{1,0},{2,3},{3,2},{4,5},{5,4},{6,7},{7,6},{8,9},{9,8},{10,11... | collective-permute-start | bytes 3932168 | tf_op jit(solution)/shard_map/ppermute | solution.py:672
  110.6 10.0 %collective-permute-start.13 = (bf16[2,192,512]{2,1,0:T(8,128)(2,1)S(1)}, bf16[2,192,512]{2,1,0:T(8,128)(2,1)S(1)}, u32[]{:S(2)}, u32[]{:S(2)}) collective-permute-start(bf16[2,192,512]{2,1,0:T(8,128)(2,1)S(1)} %add_convert_fusion.5), channel_id=1, source_target_pairs={{0,8},{1,17},{2,10},{3,19},{4,12},{5,21},{6,14},{7,23},{8,0},{9,25... | collective-permute-start | bytes 1179656 | tf_op jit(solution)/shard_map/ppermute | solution.py:672
  122.0 9.3 %collective-permute-start.15 = (bf16[1,192,512]{2,1,0:T(8,128)(2,1)S(1)}, bf16[1,192,512]{2,1,0:T(8,128)(2,1)S(1)}, u32[]{:S(2)}, u32[]{:S(2)}) collective-permute-start(bf16[1,192,512]{2,1,0:T(8,128)(2,1)S(1)} %add_convert_fusion.8), channel_id=1, source_target_pairs={{0,16},{1,3},{2,18},{3,1},{4,20},{5,7},{6,22},{7,5},{8,24},{9,11},... | collective-permute-start | bytes 589832 | tf_op jit(solution)/shard_map/ppermute | solution.py:672
  126.8 12.7 %collective-permute-start.19 = (bf16[4,128,512]{2,1,0:T(8,128)(2,1)S(1)}, bf16[4,128,512]{2,1,0:T(8,128)(2,1)S(1)}, u32[]{:S(2)}, u32[]{:S(2)}) collective-permute-start(bf16[4,128,512]{2,1,0:T(8,128)(2,1)S(1)} %add_convert_fusion.4), channel_id=1, source_target_pairs={{0,4},{1,3},{2,6},{3,1},{4,0},{5,7},{6,2},{7,5},{8,12},{9,11},{10,... | collective-permute-start | bytes 1572872 | tf_op jit(solution)/shard_map/ppermute | solution.py:672
  132.7 9.8 %collective-permute-start.18 = (bf16[1,192,512]{2,1,0:T(8,128)(2,1)S(1)}, bf16[1,192,512]{2,1,0:T(8,128)(2,1)S(1)}, u32[]{:S(2)}, u32[]{:S(2)}) collective-permute-start(bf16[1,192,512]{2,1,0:T(8,128)(2,1)S(1)} %add_convert_fusion.7), channel_id=1, source_target_pairs={{0,24},{1,25},{2,26},{3,27},{4,28},{5,29},{6,30},{7,31},{8,16},{9,... | collective-permute-start | bytes 589832 | tf_op jit(solution)/shard_map/ppermute | solution.py:672
  136.6 9.2 %collective-permute-start.17 = (bf16[1,192,512]{2,1,0:T(8,128)(2,1)S(1)}, bf16[1,192,512]{2,1,0:T(8,128)(2,1)S(1)}, u32[]{:S(2)}, u32[]{:S(2)}) collective-permute-start(bf16[1,192,512]{2,1,0:T(8,128)(2,1)S(1)} %add_convert_fusion.7), channel_id=1, source_target_pairs={{0,8},{1,9},{2,10},{3,11},{4,12},{5,13},{6,14},{7,15},{8,0},{9,1},... | collective-permute-start | bytes 589832 | tf_op jit(solution)/shard_map/ppermute | solution.py:672
  136.6 13.5 %collective-permute-start.16 = (bf16[1,192,512]{2,1,0:T(8,128)(2,1)S(1)}, bf16[1,192,512]{2,1,0:T(8,128)(2,1)S(1)}, u32[]{:S(2)}, u32[]{:S(2)}) collective-permute-start(bf16[1,192,512]{2,1,0:T(8,128)(2,1)S(1)} %add_convert_fusion.7), channel_id=1, source_target_pairs={{0,16},{1,17},{2,18},{3,19},{4,20},{5,21},{6,22},{7,23},{8,24},{9,... | collective-permute-start | bytes 589832 | tf_op jit(solution)/shard_map/ppermute | solution.py:672
  137.2 18.5 %collective-permute-start.14 = (bf16[8,80,512]{2,1,0:T(8,128)(2,1)S(1)}, bf16[8,80,512]{2,1,0:T(8,128)(2,1)S(1)}, u32[]{:S(2)}, u32[]{:S(2)}) collective-permute-start(bf16[8,80,512]{2,1,0:T(8,128)(2,1)S(1)} %add_convert_fusion.3), channel_id=1, source_target_pairs={{0,2},{1,5},{2,0},{3,7},{4,6},{5,1},{6,4},{7,3},{8,10},{9,13},{10,... | collective-permute-start | bytes 1966088 | tf_op jit(solution)/shard_map/ppermute | solution.py:672
  150.1 12.9 %collective-permute-start.21 = (bf16[4,192,512]{2,1,0:T(8,128)(2,1)S(1)}, bf16[4,192,512]{2,1,0:T(8,128)(2,1)S(1)}, u32[]{:S(2)}, u32[]{:S(2)}) collective-permute-start(bf16[4,192,512]{2,1,0:T(8,128)(2,1)S(1)} %pad_maximum_fusion.2), channel_id=1, source_target_pairs={{0,4},{1,3},{2,6},{3,1},{4,0},{5,7},{6,2},{7,5},{8,12},{9,11},{10,... | collective-permute-start | bytes 2359304 | tf_op jit(solution)/shard_map/ppermute | solution.py:672
  151.4 10.6 %collective-permute-start.22 = (bf16[1,128,512]{2,1,0:T(8,128)(2,1)S(1)}, bf16[1,128,512]{2,1,0:T(8,128)(2,1)S(1)}, u32[]{:S(2)}, u32[]{:S(2)}) collective-permute-start(bf16[1,128,512]{2,1,0:T(8,128)(2,1)S(1)} %get-tuple-element.319), channel_id=1, source_target_pairs={{0,16},{1,17},{2,18},{3,19},{4,20},{5,21},{6,22},{7,23},{8,24},{9,... | collective-permute-start | bytes 393224 | tf_op jit(solution)/shard_map/ppermute | solution.py:672
  151.4 10.6 %collective-permute-start.23 = (bf16[1,128,512]{2,1,0:T(8,128)(2,1)S(1)}, bf16[1,128,512]{2,1,0:T(8,128)(2,1)S(1)}, u32[]{:S(2)}, u32[]{:S(2)}) collective-permute-start(bf16[1,128,512]{2,1,0:T(8,128)(2,1)S(1)} %get-tuple-element.320), channel_id=1, source_target_pairs={{0,8},{1,9},{2,10},{3,11},{4,12},{5,13},{6,14},{7,15},{8,0},{9,1},... | collective-permute-start | bytes 393224 | tf_op jit(solution)/shard_map/ppermute | solution.py:672
  154.7 7.3 %collective-permute-start.24 = (bf16[1,128,512]{2,1,0:T(8,128)(2,1)S(1)}, bf16[1,128,512]{2,1,0:T(8,128)(2,1)S(1)}, u32[]{:S(2)}, u32[]{:S(2)}) collective-permute-start(bf16[1,128,512]{2,1,0:T(8,128)(2,1)S(1)} %get-tuple-element.321), channel_id=1, source_target_pairs={{0,24},{1,25},{2,26},{3,27},{4,28},{5,29},{6,30},{7,31},{8,16},{9,... | collective-permute-start | bytes 393224 | tf_op jit(solution)/shard_map/ppermute | solution.py:672
  163.2 33.5 %collective-permute-start.36 = (bf16[8,192,512]{2,1,0:T(8,128)(2,1)S(1)}, bf16[8,192,512]{2,1,0:T(8,128)(2,1)S(1)}, u32[]{:S(2)}, u32[]{:S(2)}) collective-permute-start(bf16[8,192,512]{2,1,0:T(8,128)(2,1)S(1)} %pad_maximum_fusion.refs_2_), channel_id=1, source_target_pairs={{0,2},{1,5},{2,0},{3,7},{4,6},{5,1},{6,4},{7,3},{8,10},{9,13},{10,... | collective-permute-start | bytes 4718600 | tf_op jit(solution)/shard_map/ppermute | solution.py:672
  163.9 10.6 %collective-permute-start.20 = (bf16[4,80,512]{2,1,0:T(8,128)(2,1)S(1)}, bf16[4,80,512]{2,1,0:T(8,128)(2,1)S(1)}, u32[]{:S(2)}, u32[]{:S(2)}) collective-permute-start(bf16[4,80,512]{2,1,0:T(8,128)(2,1)S(1)} %add_convert_fusion.6), channel_id=1, source_target_pairs={{0,4},{1,3},{2,6},{3,1},{4,0},{5,7},{6,2},{7,5},{8,12},{9,11},{10,... | collective-permute-start | bytes 983048 | tf_op jit(solution)/shard_map/ppermute | solution.py:672
  165.0 9.6 %collective-permute-start.30 = (bf16[1,128,512]{2,1,0:T(8,128)(2,1)S(1)}, bf16[1,128,512]{2,1,0:T(8,128)(2,1)S(1)}, u32[]{:S(2)}, u32[]{:S(2)}) collective-permute-start(bf16[1,128,512]{2,1,0:T(8,128)(2,1)S(1)} %add_convert_fusion.9), channel_id=1, source_target_pairs={{0,24},{1,25},{2,26},{3,27},{4,28},{5,29},{6,30},{7,31},{8,16},{9,... | collective-permute-start | bytes 393224 | tf_op jit(solution)/shard_map/ppermute | solution.py:672
  168.1 6.5 %collective-permute-start.29 = (bf16[1,128,512]{2,1,0:T(8,128)(2,1)S(1)}, bf16[1,128,512]{2,1,0:T(8,128)(2,1)S(1)}, u32[]{:S(2)}, u32[]{:S(2)}) collective-permute-start(bf16[1,128,512]{2,1,0:T(8,128)(2,1)S(1)} %add_convert_fusion.9), channel_id=1, source_target_pairs={{0,8},{1,9},{2,10},{3,11},{4,12},{5,13},{6,14},{7,15},{8,0},{9,1},... | collective-permute-start | bytes 393224 | tf_op jit(solution)/shard_map/ppermute | solution.py:672
  168.1 10.1 %collective-permute-start.28 = (bf16[1,128,512]{2,1,0:T(8,128)(2,1)S(1)}, bf16[1,128,512]{2,1,0:T(8,128)(2,1)S(1)}, u32[]{:S(2)}, u32[]{:S(2)}) collective-permute-start(bf16[1,128,512]{2,1,0:T(8,128)(2,1)S(1)} %add_convert_fusion.9), channel_id=1, source_target_pairs={{0,16},{1,17},{2,18},{3,19},{4,20},{5,21},{6,22},{7,23},{8,24},{9,... | collective-permute-start | bytes 393224 | tf_op jit(solution)/shard_map/ppermute | solution.py:672
  178.3 14.6 %collective-permute-start.34 = (bf16[4,128,512]{2,1,0:T(8,128)(2,1)S(1)}, bf16[4,128,512]{2,1,0:T(8,128)(2,1)S(1)}, u32[]{:S(2)}, u32[]{:S(2)}) collective-permute-start(bf16[4,128,512]{2,1,0:T(8,128)(2,1)S(1)} %pad_maximum_fusion.4), channel_id=1, source_target_pairs={{0,4},{1,3},{2,6},{3,1},{4,0},{5,7},{6,2},{7,5},{8,12},{9,11},{10,... | collective-permute-start | bytes 1572872 | tf_op jit(solution)/shard_map/ppermute | solution.py:672
  178.6 8.1 %collective-permute-start.25 = (bf16[1,80,512]{2,1,0:T(8,128)(2,1)S(1)}, bf16[1,80,512]{2,1,0:T(8,128)(2,1)S(1)}, u32[]{:S(2)}, u32[]{:S(2)}) collective-permute-start(bf16[1,80,512]{2,1,0:T(8,128)(2,1)S(1)} %get-tuple-element.333), channel_id=1, source_target_pairs={{0,16},{1,17},{2,18},{3,19},{4,20},{5,21},{6,22},{7,23},{8,24},{9,... | collective-permute-start | bytes 245768 | tf_op jit(solution)/shard_map/ppermute | solution.py:672
  180.0 7.1 %collective-permute-start.26 = (bf16[1,80,512]{2,1,0:T(8,128)(2,1)S(1)}, bf16[1,80,512]{2,1,0:T(8,128)(2,1)S(1)}, u32[]{:S(2)}, u32[]{:S(2)}) collective-permute-start(bf16[1,80,512]{2,1,0:T(8,128)(2,1)S(1)} %get-tuple-element.334), channel_id=1, source_target_pairs={{0,8},{1,9},{2,10},{3,11},{4,12},{5,13},{6,14},{7,15},{8,0},{9,1},... | collective-permute-start | bytes 245768 | tf_op jit(solution)/shard_map/ppermute | solution.py:672
  182.2 6.2 %collective-permute-start.27 = (bf16[1,80,512]{2,1,0:T(8,128)(2,1)S(1)}, bf16[1,80,512]{2,1,0:T(8,128)(2,1)S(1)}, u32[]{:S(2)}, u32[]{:S(2)}) collective-permute-start(bf16[1,80,512]{2,1,0:T(8,128)(2,1)S(1)} %get-tuple-element.335), channel_id=1, source_target_pairs={{0,24},{1,25},{2,26},{3,27},{4,28},{5,29},{6,30},{7,31},{8,16},{9,... | collective-permute-start | bytes 245768 | tf_op jit(solution)/shard_map/ppermute | solution.py:672
  188.5 27.6 %copy-start = (s32[32,32]{1,0:T(8,128)S(1)}, s32[32,32]{1,0:T(8,128)}, u32[]{:S(2)}) copy-start(s32[32,32]{1,0:T(8,128)} %constant.4.clone.refs_1_) | copy-start | bytes 12292
  188.5 27.5 %copy-start.1 = (f32[8,128]{1,0:T(8,128)S(1)}, f32[8,128]{1,0:T(8,128)}, u32[]{:S(2)}) copy-start(f32[8,128]{1,0:T(8,128)} %get-tuple-element.373.refs_0_) | copy-start | bytes 12292
  188.5 6.4 %collective-permute-start.33 = (bf16[1,80,512]{2,1,0:T(8,128)(2,1)S(1)}, bf16[1,80,512]{2,1,0:T(8,128)(2,1)S(1)}, u32[]{:S(2)}, u32[]{:S(2)}) collective-permute-start(bf16[1,80,512]{2,1,0:T(8,128)(2,1)S(1)} %add_convert_fusion.13), channel_id=1, source_target_pairs={{0,24},{1,25},{2,26},{3,27},{4,28},{5,29},{6,30},{7,31},{8,16},{9,... | collective-permute-start | bytes 245768 | tf_op jit(solution)/shard_map/ppermute | solution.py:672
  190.4 6.2 %collective-permute-start.32 = (bf16[1,80,512]{2,1,0:T(8,128)(2,1)S(1)}, bf16[1,80,512]{2,1,0:T(8,128)(2,1)S(1)}, u32[]{:S(2)}, u32[]{:S(2)}) collective-permute-start(bf16[1,80,512]{2,1,0:T(8,128)(2,1)S(1)} %add_convert_fusion.13), channel_id=1, source_target_pairs={{0,8},{1,9},{2,10},{3,11},{4,12},{5,13},{6,14},{7,15},{8,0},{9,1},... | collective-permute-start | bytes 245768 | tf_op jit(solution)/shard_map/ppermute | solution.py:672
  191.0 5.6 %collective-permute-start.31 = (bf16[1,80,512]{2,1,0:T(8,128)(2,1)S(1)}, bf16[1,80,512]{2,1,0:T(8,128)(2,1)S(1)}, u32[]{:S(2)}, u32[]{:S(2)}) collective-permute-start(bf16[1,80,512]{2,1,0:T(8,128)(2,1)S(1)} %add_convert_fusion.13), channel_id=1, source_target_pairs={{0,16},{1,17},{2,18},{3,19},{4,20},{5,21},{6,22},{7,23},{8,24},{9,... | collective-permute-start | bytes 245768 | tf_op jit(solution)/shard_map/ppermute | solution.py:672
  196.6 19.4 %collective-permute-start.38 = (bf16[8,192,512]{2,1,0:T(8,128)(2,1)S(1)}, bf16[8,192,512]{2,1,0:T(8,128)(2,1)S(1)}, u32[]{:S(2)}, u32[]{:S(2)}) collective-permute-start(bf16[8,192,512]{2,1,0:T(8,128)(2,1)S(1)} %pad_maximum_fusion.refs_2_), channel_id=1, source_target_pairs={{0,1},{1,0},{2,3},{3,2},{4,5},{5,4},{6,7},{7,6},{8,9},{9,8},{10,11... | collective-permute-start | bytes 4718600 | tf_op jit(solution)/shard_map/ppermute | solution.py:672
  196.7 19.3 %collective-permute-start.39 = (bf16[8,192,512]{2,1,0:T(8,128)(2,1)S(1)}, bf16[8,192,512]{2,1,0:T(8,128)(2,1)S(1)}, u32[]{:S(2)}, u32[]{:S(2)}) collective-permute-start(bf16[8,192,512]{2,1,0:T(8,128)(2,1)S(1)} %collective-permute-done.36.refs_3_), channel_id=1, source_target_pairs={{0,1},{1,0},{2,3},{3,2},{4,5},{5,4},{6,7},{7,6},{8,9},{9,8},{10,11... | collective-permute-start | bytes 4718600 | tf_op jit(solution)/shard_map/ppermute | solution.py:672
  197.2 18.3 %collective-permute-start.40 = (bf16[8,128,512]{2,1,0:T(8,128)(2,1)S(1)}, bf16[8,128,512]{2,1,0:T(8,128)(2,1)S(1)}, u32[]{:S(2)}, u32[]{:S(2)}) collective-permute-start(bf16[8,128,512]{2,1,0:T(8,128)(2,1)S(1)} %pad_maximum_fusion.1.refs_2_), channel_id=1, source_target_pairs={{0,2},{1,5},{2,0},{3,7},{4,6},{5,1},{6,4},{7,3},{8,10},{9,13},{10,... | collective-permute-start | bytes 3145736 | tf_op jit(solution)/shard_map/ppermute | solution.py:672
  198.6 10.6 %collective-permute-start.35 = (bf16[4,80,512]{2,1,0:T(8,128)(2,1)S(1)}, bf16[4,80,512]{2,1,0:T(8,128)(2,1)S(1)}, u32[]{:S(2)}, u32[]{:S(2)}) collective-permute-start(bf16[4,80,512]{2,1,0:T(8,128)(2,1)S(1)} %pad_maximum_fusion.5), channel_id=1, source_target_pairs={{0,4},{1,3},{2,6},{3,1},{4,0},{5,7},{6,2},{7,5},{8,12},{9,11},{10,... | collective-permute-start | bytes 983048 | tf_op jit(solution)/shard_map/ppermute | solution.py:672
  209.3 13.3 %collective-permute-start.37 = (bf16[8,80,512]{2,1,0:T(8,128)(2,1)S(1)}, bf16[8,80,512]{2,1,0:T(8,128)(2,1)S(1)}, u32[]{:S(2)}, u32[]{:S(2)}) collective-permute-start(bf16[8,80,512]{2,1,0:T(8,128)(2,1)S(1)} %pad_maximum_fusion.3.refs_2_), channel_id=1, source_target_pairs={{0,2},{1,5},{2,0},{3,7},{4,6},{5,1},{6,4},{7,3},{8,10},{9,13},{10,... | collective-permute-start | bytes 1966088 | tf_op jit(solution)/shard_map/ppermute | solution.py:672
  215.5 8.2 %collective-permute-start.43 = (bf16[8,128,512]{2,1,0:T(8,128)(2,1)S(1)}, bf16[8,128,512]{2,1,0:T(8,128)(2,1)S(1)}, u32[]{:S(2)}, u32[]{:S(2)}) collective-permute-start(bf16[8,128,512]{2,1,0:T(8,128)(2,1)S(1)} %pad_maximum_fusion.1.refs_2_), channel_id=1, source_target_pairs={{0,1},{1,0},{2,3},{3,2},{4,5},{5,4},{6,7},{7,6},{8,9},{9,8},{10,11... | collective-permute-start | bytes 3145736 | tf_op jit(solution)/shard_map/ppermute | solution.py:672
  215.6 8.1 %collective-permute-start.44 = (bf16[8,128,512]{2,1,0:T(8,128)(2,1)S(1)}, bf16[8,128,512]{2,1,0:T(8,128)(2,1)S(1)}, u32[]{:S(2)}, u32[]{:S(2)}) collective-permute-start(bf16[8,128,512]{2,1,0:T(8,128)(2,1)S(1)} %collective-permute-done.40.refs_3_), channel_id=1, source_target_pairs={{0,1},{1,0},{2,3},{3,2},{4,5},{5,4},{6,7},{7,6},{8,9},{9,8},{10,11... | collective-permute-start | bytes 3145736 | tf_op jit(solution)/shard_map/ppermute | solution.py:672
  222.6 5.2 %collective-permute-start.41 = (bf16[8,80,512]{2,1,0:T(8,128)(2,1)S(1)}, bf16[8,80,512]{2,1,0:T(8,128)(2,1)S(1)}, u32[]{:S(2)}, u32[]{:S(2)}) collective-permute-start(bf16[8,80,512]{2,1,0:T(8,128)(2,1)S(1)} %pad_maximum_fusion.3.refs_2_), channel_id=1, source_target_pairs={{0,1},{1,0},{2,3},{3,2},{4,5},{5,4},{6,7},{7,6},{8,9},{9,8},{10,11... | collective-permute-start | bytes 1966088 | tf_op jit(solution)/shard_map/ppermute | solution.py:672
  222.7 5.1 %collective-permute-start.42 = (bf16[8,80,512]{2,1,0:T(8,128)(2,1)S(1)}, bf16[8,80,512]{2,1,0:T(8,128)(2,1)S(1)}, u32[]{:S(2)}, u32[]{:S(2)}) collective-permute-start(bf16[8,80,512]{2,1,0:T(8,128)(2,1)S(1)} %collective-permute-done.37.refs_3_), channel_id=1, source_target_pairs={{0,1},{1,0},{2,3},{3,2},{4,5},{5,4},{6,7},{7,6},{8,9},{9,8},{10,11... | collective-permute-start | bytes 1966088 | tf_op jit(solution)/shard_map/ppermute | solution.py:672
  (4 other events, 37.3 us)
